TPU v7x, 512 devices: a whole 4x8x8 slice. The times are simulated.
512 devices in a mesh: gx: 16 (over z, core), gy: 8 (over y), gz: 4 (over x).
Axes of the slice: x: 4, y: 8, z: 8, core: 2. Of those that a mesh axis runs over, the one named last changes fastest.
Arguments:
- populations: float32 [19, 32, 256, 512], P(None, 'gx', 'gy', 'gz')
- orientation: float32 [6, 32, 256, 512], P(None, 'gx', 'gy', 'gz')
- slot_table: int32 [32, 256, 4], P('gx', 'gy', 'gz'), may hold values from -1 to 15, as said below
- w_in: bfloat16 [6, 512], replicated, may hold values from -12 to 12
- b_in: float32 [512], replicated, may hold values from -3 to 3
- w_mid: bfloat16 [512, 512], replicated, may hold values from -0.25 to 0.25
- b_mid: float32 [512], replicated, may hold values from -3 to 3
- w_out: bfloat16 [512, 15], replicated, may hold values from -0.25 to 0.25
- b_out: float32 [15], replicated, may hold values from -2 to 2
Outputs:
- flow_moments: bfloat16 [4, 32, 256, 512], P(None, 'gx', 'gy', 'gz')
- closure: bfloat16 [15, 32, 256, 512], P(None, 'gx', 'gy', 'gz')
Inputs may be any that keep to these rules, and one draw needn't show every extreme that they name: `slot_table`: on one device the non-negative values are distinct: d + j marks the j-th block that the device sends to index d of gx for evaluation. A device with n occupied blocks sends n / 16 of them to every index of gx, using j from 0 upward; n is at most 16, which some device of every group along gx holds, and every device receives exactly 16 blocks in all.
All inputs are finite; a program needn't handle non-finite values.
Results may differ from a plain program's by a relative error of at most 0.0059.
Values may be sent and summed in bfloat16 or wider, within the bound.
No kernel may reach another device: no remote copies, remote signals or barrier semaphores. Data moves between devices by JAX's collectives and lax.ppermute only.
A program may use at most 128 MiB of HBM per device.

v0:
```python
import jax
import jax.numpy as jnp
from jax import lax
from jax.sharding import PartitionSpec as P

OWN_MAX = 16
ITERS = 2


VELOCITIES = [
    (0, 0, 0),
    (1, 0, 0),
    (-1, 0, 0),
    (0, 1, 0),
    (0, -1, 0),
    (0, 0, 1),
    (0, 0, -1),
    (1, 1, 0),
    (-1, -1, 0),
    (1, -1, 0),
    (-1, 1, 0),
    (1, 0, 1),
    (-1, 0, -1),
    (1, 0, -1),
    (-1, 0, 1),
    (0, 1, 1),
    (0, -1, -1),
    (0, 1, -1),
    (0, -1, 1),
]
LATTICE_WEIGHTS = [1.0 / 3.0] + [1.0 / 18.0] * 6 + [1.0 / 36.0] * 12
RELAX_TIME = 0.8
SHAPE_FACTOR = 0.95
ORIENT_STEP = 4.0
TENSOR_PAIRS = [(0, 0), (1, 1), (2, 2), (0, 1), (0, 2), (1, 2)]
OFFSETS_AHEAD = [(1, 0, 0), (0, 1, 0), (0, 0, 1)]
OFFSETS_BEHIND = [(-1, 0, 0), (0, -1, 0), (0, 0, -1)]
ROW_GROUP = 8


def extended(cells, sides, width):
    for axis, dim in sides:
        count = lax.axis_size(axis)
        head = lax.slice_in_dim(cells, 0, width, axis=dim)
        tail = lax.slice_in_dim(cells, cells.shape[dim] - width, cells.shape[dim], axis=dim)
        cells = jnp.concatenate(
            [
                lax.ppermute(tail, axis, [(i, (i + 1) % count) for i in range(count)]),
                cells,
                lax.ppermute(head, axis, [((i + 1) % count, i) for i in range(count)]),
            ],
            axis=dim,
        )
    return cells


def opposite_of(number):
    return number + 1 if number % 2 == 1 else number - 1


def fluid_moments(populations):
    density = populations[0]
    for number in range(1, 19):
        density = density + populations[number]
    velocity = []
    for axis_number in range(3):
        momentum = None
        for number in range(19):
            component = VELOCITIES[number][axis_number]
            if component != 0:
                summand = populations[number] if component > 0 else -populations[number]
                momentum = summand if momentum is None else momentum + summand
        velocity.append(momentum / density)
    return (density, velocity)


def collide(populations, density, velocity):
    speed_square = velocity[0] * velocity[0] + velocity[1] * velocity[1] + velocity[2] * velocity[2]
    relaxed = []
    for number in range(19):
        projection = jnp.zeros_like(density)
        for axis_number in range(3):
            component = VELOCITIES[number][axis_number]
            if component != 0:
                projection = projection + component * velocity[axis_number]
        equilibrium = (
            LATTICE_WEIGHTS[number]
            * density
            * (1.0 + 3.0 * projection + 4.5 * projection * projection - 1.5 * speed_square)
        )
        relaxed.append(populations[number] - (populations[number] - equilibrium) / RELAX_TIME)
    return jnp.stack(relaxed)


def full_tensor(entries):
    return [
        [entries[0], entries[3], entries[4]],
        [entries[3], entries[1], entries[5]],
        [entries[4], entries[5], entries[2]],
    ]


def jeffery_rate(entries, gradient):
    tensor = full_tensor(entries)
    strain = [
        [
            0.5 * (gradient[row_index][col_index] + gradient[col_index][row_index])
            for col_index in range(3)
        ]
        for row_index in range(3)
    ]
    rotation = [
        [
            0.5 * (gradient[row_index][col_index] - gradient[col_index][row_index])
            for col_index in range(3)
        ]
        for row_index in range(3)
    ]
    contraction = None
    for row_index in range(3):
        for col_index in range(3):
            product = tensor[row_index][col_index] * strain[row_index][col_index]
            contraction = product if contraction is None else contraction + product
    rate_list = []
    for row_index, col_index in TENSOR_PAIRS:
        turned = None
        stretched = None
        for inner_index in range(3):
            spin_term = (
                tensor[row_index][inner_index] * rotation[inner_index][col_index]
                - rotation[row_index][inner_index] * tensor[inner_index][col_index]
            )
            strain_term = (
                strain[row_index][inner_index] * tensor[inner_index][col_index]
                + tensor[row_index][inner_index] * strain[inner_index][col_index]
            )
            turned = spin_term if turned is None else turned + spin_term
            stretched = strain_term if stretched is None else stretched + strain_term
        rate_list.append(
            turned + SHAPE_FACTOR * (stretched - 2.0 * contraction * tensor[row_index][col_index])
        )
    return rate_list


def window(padded, offsets, width_x, width_y, depth_cells):
    return padded[
        :,
        1 + offsets[0] : 1 + offsets[0] + width_x,
        1 + offsets[1] : 1 + offsets[1] + width_y,
        1 + offsets[2] : 1 + offsets[2] + depth_cells,
    ]


def closure_net(features, w_in, b_in, w_mid, b_mid, w_out, b_out):
    block_count = features.shape[0]
    depth_cells = features.shape[2]
    padded_count = -(-block_count // ROW_GROUP) * ROW_GROUP
    filled = jnp.concatenate(
        [
            features,
            jnp.zeros((padded_count - block_count, features.shape[1], depth_cells), jnp.bfloat16),
        ],
        axis=0,
    )
    grouped = filled.reshape(padded_count // ROW_GROUP, ROW_GROUP, features.shape[1], depth_cells)

    def one_step(one_group):
        first_layer = (
            jnp.einsum("bfc,fh->bch", one_group, w_in, preferred_element_type=jnp.float32) + b_in
        )
        hidden_one = jax.nn.silu(first_layer).astype(jnp.bfloat16)
        second_layer = (
            jnp.einsum("bch,hk->bck", hidden_one, w_mid, preferred_element_type=jnp.float32) + b_mid
        )
        hidden_two = jax.nn.silu(second_layer).astype(jnp.bfloat16)
        third_layer = (
            jnp.einsum("bch,hk->bkc", hidden_two, w_out, preferred_element_type=jnp.float32)
            + b_out[:, None]
        )
        return third_layer.astype(jnp.bfloat16)

    evaluated = lax.map(one_step, grouped)
    return evaluated.reshape(padded_count, w_out.shape[1], depth_cells)


def local(populations, orientation, slot_table, w_in, b_in, w_mid, b_mid, w_out, b_out):
    width_x = populations.shape[1]
    width_y = populations.shape[2]
    depth_cells = populations.shape[3]
    layer_count = lax.axis_size("gz")
    low_side = lax.axis_index("gz") == 0
    high_side = lax.axis_index("gz") == layer_count - 1
    cell_plane = jnp.arange(depth_cells)
    wall_low = (cell_plane == 0) & low_side
    wall_high = (cell_plane == depth_cells - 1) & high_side
    padded_plane = jnp.arange(depth_cells + 2)
    rim_low = (padded_plane == 0) & low_side
    rim_high = (padded_plane == depth_cells + 1) & high_side
    for step_number in range(ITERS):
        density, velocity = fluid_moments(populations)
        relaxed = collide(populations, density, velocity)
        outgoing = jnp.concatenate([relaxed, jnp.stack(velocity), orientation], axis=0)
        padded = extended(outgoing, (("gx", 1), ("gy", 2), ("gz", 3)), 1)
        relaxed_pad = padded[:19]
        velocity_pad = padded[19:22]
        tensor_pad = padded[22:]
        velocity_pad = jnp.where(rim_low | rim_high, 0.0, velocity_pad)
        lifted_low = jnp.concatenate([tensor_pad[..., 1:2], tensor_pad[..., 1:]], axis=-1)
        lifted_high = jnp.concatenate([tensor_pad[..., :-1], tensor_pad[..., -2:-1]], axis=-1)
        tensor_pad = jnp.where(rim_low, lifted_low, jnp.where(rim_high, lifted_high, tensor_pad))
        read = []
        for number in range(19):
            shift_x, shift_y, shift_z = VELOCITIES[number]
            pulled = relaxed_pad[
                number,
                1 - shift_x : 1 - shift_x + width_x,
                1 - shift_y : 1 - shift_y + width_y,
                1 - shift_z : 1 - shift_z + depth_cells,
            ]
            if shift_z == 1:
                pulled = jnp.where(wall_low, relaxed[opposite_of(number)], pulled)
            if shift_z == -1:
                pulled = jnp.where(wall_high, relaxed[opposite_of(number)], pulled)
            read.append(pulled)
        gradient = [[None, None, None] for row_index in range(3)]
        tensor_diffs = []
        for axis_number in range(3):
            ahead = window(velocity_pad, OFFSETS_AHEAD[axis_number], width_x, width_y, depth_cells)
            behind = window(
                velocity_pad, OFFSETS_BEHIND[axis_number], width_x, width_y, depth_cells
            )
            for row_index in range(3):
                gradient[row_index][axis_number] = 0.5 * (ahead[row_index] - behind[row_index])
            tensor_ahead = window(
                tensor_pad, OFFSETS_AHEAD[axis_number], width_x, width_y, depth_cells
            )
            tensor_behind = window(
                tensor_pad, OFFSETS_BEHIND[axis_number], width_x, width_y, depth_cells
            )
            tensor_diffs.append(0.5 * (tensor_ahead - tensor_behind))
        advection = (
            velocity[0] * tensor_diffs[0]
            + velocity[1] * tensor_diffs[1]
            + velocity[2] * tensor_diffs[2]
        )
        rate_list = jeffery_rate([orientation[number] for number in range(6)], gradient)
        orientation = orientation + ORIENT_STEP * (jnp.stack(rate_list) - advection)
        populations = jnp.stack(read)
    density, velocity = fluid_moments(populations)
    flow_moments = jnp.stack([density] + velocity).astype(jnp.bfloat16)
    features = orientation.astype(jnp.bfloat16)
    component_count = features.shape[0]
    block_total = width_x * width_y
    slot_list = slot_table.reshape(block_total)
    selector = (slot_list[None, :] == jnp.arange(OWN_MAX)[:, None]).astype(jnp.bfloat16)
    feature_blocks = jnp.transpose(features, (1, 2, 0, 3)).reshape(
        block_total, component_count * depth_cells
    )
    chosen = jnp.dot(selector, feature_blocks, preferred_element_type=jnp.float32).astype(
        jnp.bfloat16
    )
    chosen = chosen.reshape(OWN_MAX, component_count, depth_cells)
    term_count = w_out.shape[1]
    results = closure_net(chosen, w_in, b_in, w_mid, b_mid, w_out, b_out)
    closure_blocks = jnp.dot(
        selector.T,
        results.reshape(OWN_MAX, term_count * depth_cells),
        preferred_element_type=jnp.float32,
    ).astype(jnp.bfloat16)
    closure = jnp.transpose(
        closure_blocks.reshape(width_x, width_y, term_count, depth_cells), (2, 0, 1, 3)
    )
    return (flow_moments, closure)


def solution(mesh):
    in_specs = (
        P(None, "gx", "gy", "gz"),
        P(None, "gx", "gy", "gz"),
        P("gx", "gy", "gz"),
        P(),
        P(),
        P(),
        P(),
        P(),
        P(),
    )
    out_specs = (P(None, "gx", "gy", "gz"), P(None, "gx", "gy", "gz"))
    return jax.shard_map(local, mesh=mesh, in_specs=in_specs, out_specs=out_specs, check_vma=False)
```

profile of v0, /device:TPU:22, one launch (start us, length us, event | category | flops | bytes accessed | tf_op | source)
XLA Modules:
  0.0 138.5 jit_solution(376752890405606717)
XLA Ops:
  0.6 1.8 %multiply_bitcast_fusion.5 = (f32[2,32,128]{2,1,0:T(8,128)}, f32[1,2,32,128]{3,2,1,0:T(8,128)S(1)}, f32[1,2,32,128]{3,2,1,0:T(8,128)S(1)}) fusion(f32[19,2,32,128]{3,2,1,0:T(8,128)} %param.11), kind=kLoop, calls=%fused_computation.471 | loop fusion | flops 278528 | bytes 720896 | tf_op jit(solution)/shard_map/mul | solution.py:242
  2.4 1.5 %multiply_bitcast_fusion.3 = (f32[2,32,128]{2,1,0:T(8,128)}, f32[1,2,32,128]{3,2,1,0:T(8,128)S(1)}) fusion(f32[1,2,32,128]{3,2,1,0:T(8,128)S(1)} %get-tuple-element.207, f32[19,2,32,128]{3,2,1,0:T(8,128)} %param.11), kind=kLoop, calls=%fused_computation.469 | loop fusion | flops 131072 | bytes 425984 | tf_op jit(solution)/shard_map/mul | solution.py:244
  4.0 1.6 %multiply_bitcast_fusion.4 = (f32[2,32,128]{2,1,0:T(8,128)}, f32[1,2,32,128]{3,2,1,0:T(8,128)S(1)}) fusion(f32[1,2,32,128]{3,2,1,0:T(8,128)S(1)} %get-tuple-element.207, f32[19,2,32,128]{3,2,1,0:T(8,128)} %param.11), kind=kLoop, calls=%fused_computation.470 | loop fusion | flops 131072 | bytes 425984 | tf_op jit(solution)/shard_map/mul | solution.py:243
  5.5 1.4 constant_dynamic-update-slice_fusion.22
  6.9 0.8 constant_dynamic-update-slice_fusion.21
  7.7 0.8 constant_dynamic-update-slice_fusion.20
  8.5 0.8 constant_dynamic-update-slice_fusion.19
  15.9 8.5 %collective-permute-start.1 = (f32[28,1,32,128]{3,2,1,0:T(8,128)S(1)}, f32[28,1,32,128]{3,2,1,0:T(8,128)S(1)}, u32[]{:S(2)}, u32[]{:S(2)}) collective-permute-start(f32[28,1,32,128]{3,2,1,0:T(8,128)S(1)} %get-tuple-element.282), channel_id=1, source_target_pairs={{32,0},{64,32},{96,64},{128,96},{160,128},{192,160},{224,192},{256... | collective-permute-start | bytes 1376264 | tf_op jit(solution)/shard_map/ppermute | solution.py:50
  24.4 6.1 %collective-permute-done = f32[28,1,32,128]{3,2,1,0:T(8,128)S(1)} collective-permute-done((f32[28,1,32,128]{3,2,1,0:T(8,128)S(1)}, f32[28,1,32,128]{3,2,1,0:T(8,128)S(1)}, u32[]{:S(2)}, u32[]{:S(2)}) %collective-permute-start) | collective-permute-done | bytes 458784 | tf_op jit(solution)/shard_map/ppermute | solution.py:48
  30.7 3.5 %collective-permute-start.2 = (f32[28,4,1,128]{3,0,2,1:T(8,128)S(1)}, f32[28,4,1,128]{3,0,2,1:T(8,128)S(1)}, u32[]{:S(2)}, u32[]{:S(2)}) collective-permute-start(f32[28,4,1,128]{3,0,2,1:T(8,128)S(1)} %copy.1336), channel_id=1, source_target_pairs={{0,4},{4,8},{8,12},{12,16},{16,20},{20,24},{24,28},{28,0},{1,5},{5... | collective-permute-start | bytes 172040 | tf_op jit(solution)/shard_map/ppermute | solution.py:48
  34.2 2.4 %collective-permute-start.3 = (f32[28,4,1,128]{3,0,2,1:T(8,128)S(1)}, f32[28,4,1,128]{3,0,2,1:T(8,128)S(1)}, u32[]{:S(2)}, u32[]{:S(2)}) collective-permute-start(f32[28,4,1,128]{3,0,2,1:T(8,128)S(1)} %copy.1337), channel_id=1, source_target_pairs={{4,0},{8,4},{12,8},{16,12},{20,16},{24,20},{28,24},{0,28},{5,1},{9... | collective-permute-start | bytes 172040 | tf_op jit(solution)/shard_map/ppermute | solution.py:50
  36.9 4.2 %collective-permute-done.3 = f32[28,4,1,128]{3,0,2,1:T(8,128)S(1)} collective-permute-done((f32[28,4,1,128]{3,0,2,1:T(8,128)S(1)}, f32[28,4,1,128]{3,0,2,1:T(8,128)S(1)}, u32[]{:S(2)}, u32[]{:S(2)}) %collective-permute-start.3) | collective-permute-done | bytes 57376 | tf_op jit(solution)/shard_map/ppermute | solution.py:50
  41.8 2.9 %fusion.281 = (f32[28,4,34,1]{3,2,1,0:T(8,128)}, f32[28,4,34,1]{3,2,1,0:T(8,128)}) fusion(f32[28,4,34,128]{3,2,1,0:T(8,128)S(1)} %pad_maximum_fusion), kind=kLoop, calls=%fused_computation.537 | loop fusion | bytes 60928 | tf_op jit(solution)/shard_map/slice | solution.py:44
  44.7 3.4 %copy.1314 = f32[28,4,34,1]{2,0,3,1:T(8,128)} copy(f32[28,4,34,1]{3,2,1,0:T(8,128)} %get-tuple-element.275) | data formatting | bytes 30464 | tf_op jit(solution)/shard_map/slice | solution.py:45
  48.2 2.4 %collective-permute-start.4 = (f32[28,4,34,1]{2,0,3,1:T(8,128)}, f32[28,4,34,1]{2,0,3,1:T(8,128)}, u32[]{:S(2)}, u32[]{:S(2)}) collective-permute-start(f32[28,4,34,1]{2,0,3,1:T(8,128)} %copy.1314), channel_id=1, source_target_pairs={{0,1},{1,2},{2,3},{3,0},{4,5},{5,6},{6,7},{7,4},{8,9},{9,10},{10,1... | collective-permute-start | bytes 45704 | tf_op jit(solution)/shard_map/ppermute | solution.py:48
  50.5 1.6 %copy.1316 = f32[28,4,34,1]{2,0,3,1:T(8,128)} copy(f32[28,4,34,1]{3,2,1,0:T(8,128)S(1)} %copy-done.14) | data formatting | bytes 30464 | tf_op jit(solution)/shard_map/slice | solution.py:44
  52.2 3.4 %collective-permute-start.5 = (f32[28,4,34,1]{2,0,3,1:T(8,128)}, f32[28,4,34,1]{2,0,3,1:T(8,128)}, u32[]{:S(2)}, u32[]{:S(2)}) collective-permute-start(f32[28,4,34,1]{2,0,3,1:T(8,128)} %copy.1316), channel_id=1, source_target_pairs={{1,0},{2,1},{3,2},{0,3},{5,4},{6,5},{7,6},{4,7},{9,8},{10,9},{11,1... | collective-permute-start | bytes 45704 | tf_op jit(solution)/shard_map/ppermute | solution.py:50
  55.7 1.7 %copy.1315 = f32[28,4,34,1]{3,2,1,0:T(8,128)S(1)} copy(f32[28,4,34,1]{2,0,3,1:T(8,128)} %collective-permute-done.4) | data formatting | bytes 30464 | tf_op jit(solution)/shard_map/ppermute | solution.py:48
  57.4 2.4 %collective-permute-done.5 = f32[28,4,34,1]{2,0,3,1:T(8,128)} collective-permute-done((f32[28,4,34,1]{2,0,3,1:T(8,128)}, f32[28,4,34,1]{2,0,3,1:T(8,128)}, u32[]{:S(2)}, u32[]{:S(2)}) %collective-permute-start.5) | collective-permute-done | bytes 15264 | tf_op jit(solution)/shard_map/ppermute | solution.py:50
  59.8 3.1 %copy.1317 = f32[28,4,34,1]{3,2,1,0:T(8,128)} copy(f32[28,4,34,1]{2,0,3,1:T(8,128)} %collective-permute-done.5) | data formatting | bytes 30464 | tf_op jit(solution)/shard_map/ppermute | solution.py:50
  62.9 2.0 %multiply_bitcast_fusion.2 = (f32[2,32,128]{2,1,0:T(8,128)}, f32[1,2,32,128]{3,2,1,0:T(8,128)S(1)}, f32[1,2,32,128]{3,2,1,0:T(8,128)S(1)}, f32[1,2,32,128]{3,2,1...) fusion(f32[1,2,32,128]{3,2,1,0:T(8,128)S(1)} %copy-done.21, ...), kind=kLoop, calls=%fused_computation.443 | loop fusion | flops 933888 | bytes 3028992 | tf_op jit(solution)/shard_map/mul | solution.py:242
  73.4 0.8 fusion.19
  74.2 1.0 constant_dynamic-update-slice_fusion.29
  75.3 2.9 %collective-permute-start.7 = (f32[28,1,32,128]{3,2,1,0:T(8,128)S(1)}, f32[28,1,32,128]{3,2,1,0:T(8,128)S(1)}, u32[]{:S(2)}, u32[]{:S(2)}) collective-permute-start(f32[28,1,32,128]{3,2,1,0:T(8,128)S(1)} %get-tuple-element.280), channel_id=1, source_target_pairs={{32,0},{64,32},{96,64},{128,96},{160,128},{192,160},{224,192},{256... | collective-permute-start | bytes 1376264 | tf_op jit(solution)/shard_map/ppermute | solution.py:50
  78.3 6.2 %collective-permute-done.6 = f32[28,1,32,128]{3,2,1,0:T(8,128)S(1)} collective-permute-done((f32[28,1,32,128]{3,2,1,0:T(8,128)S(1)}, f32[28,1,32,128]{3,2,1,0:T(8,128)S(1)}, u32[]{:S(2)}, u32[]{:S(2)}) %collective-permute-start.6) | collective-permute-done | bytes 458784 | tf_op jit(solution)/shard_map/ppermute | solution.py:48
  84.5 5.1 %collective-permute-start.8 = (f32[28,4,1,128]{3,0,2,1:T(8,128)S(1)}, f32[28,4,1,128]{3,0,2,1:T(8,128)S(1)}, u32[]{:S(2)}, u32[]{:S(2)}) collective-permute-start(f32[28,4,1,128]{3,0,2,1:T(8,128)S(1)} %copy.1338), channel_id=1, source_target_pairs={{0,4},{4,8},{8,12},{12,16},{16,20},{20,24},{24,28},{28,0},{1,5},{5... | collective-permute-start | bytes 172040 | tf_op jit(solution)/shard_map/ppermute | solution.py:48
  89.7 1.9 %collective-permute-start.9 = (f32[28,4,1,128]{3,0,2,1:T(8,128)S(1)}, f32[28,4,1,128]{3,0,2,1:T(8,128)S(1)}, u32[]{:S(2)}, u32[]{:S(2)}) collective-permute-start(f32[28,4,1,128]{3,0,2,1:T(8,128)S(1)} %copy.1339), channel_id=1, source_target_pairs={{4,0},{8,4},{12,8},{16,12},{20,16},{24,20},{28,24},{0,28},{5,1},{9... | collective-permute-start | bytes 172040 | tf_op jit(solution)/shard_map/ppermute | solution.py:50
  91.7 4.2 %collective-permute-done.9 = f32[28,4,1,128]{3,0,2,1:T(8,128)S(1)} collective-permute-done((f32[28,4,1,128]{3,0,2,1:T(8,128)S(1)}, f32[28,4,1,128]{3,0,2,1:T(8,128)S(1)}, u32[]{:S(2)}, u32[]{:S(2)}) %collective-permute-start.9) | collective-permute-done | bytes 57376 | tf_op jit(solution)/shard_map/ppermute | solution.py:50
  96.4 2.2 %fusion.280 = (f32[28,4,34,1]{3,2,1,0:T(8,128)S(1)}, f32[28,4,34,1]{3,2,1,0:T(8,128)}) fusion(f32[28,4,34,128]{3,2,1,0:T(8,128)S(1)} %pad_maximum_fusion.1), kind=kLoop, calls=%fused_computation.536 | loop fusion | bytes 60928 | tf_op jit(solution)/shard_map/slice | solution.py:44
  98.6 2.6 %copy.1326 = f32[28,4,34,1]{2,0,3,1:T(8,128)S(1)} copy(f32[28,4,34,1]{3,2,1,0:T(8,128)} %get-tuple-element.273) | data formatting | bytes 30464 | tf_op jit(solution)/shard_map/slice | solution.py:45
  101.2 2.2 %collective-permute-start.10 = (f32[28,4,34,1]{2,0,3,1:T(8,128)S(1)}, f32[28,4,34,1]{2,0,3,1:T(8,128)S(1)}, u32[]{:S(2)}, u32[]{:S(2)}) collective-permute-start(f32[28,4,34,1]{2,0,3,1:T(8,128)S(1)} %copy.1326), channel_id=1, source_target_pairs={{0,1},{1,2},{2,3},{3,0},{4,5},{5,6},{6,7},{7,4},{8,9},{9,10},{10,1... | collective-permute-start | bytes 45704 | tf_op jit(solution)/shard_map/ppermute | solution.py:48
  103.4 1.0 copy.1328
  104.4 3.8 %collective-permute-start.11 = (f32[28,4,34,1]{2,0,3,1:T(8,128)S(1)}, f32[28,4,34,1]{2,0,3,1:T(8,128)}, u32[]{:S(2)}, u32[]{:S(2)}) collective-permute-start(f32[28,4,34,1]{2,0,3,1:T(8,128)S(1)} %copy.1328), channel_id=1, source_target_pairs={{1,0},{2,1},{3,2},{0,3},{5,4},{6,5},{7,6},{4,7},{9,8},{10,9},{11,1... | collective-permute-start | bytes 45704 | tf_op jit(solution)/shard_map/ppermute | solution.py:50
  109.6 0.9 copy.1327
  110.5 1.3 collective-permute-done.11
  111.9 3.1 %copy.1329 = f32[28,4,34,1]{3,2,1,0:T(8,128)} copy(f32[28,4,34,1]{2,0,3,1:T(8,128)} %collective-permute-done.11) | data formatting | bytes 30464 | tf_op jit(solution)/shard_map/ppermute | solution.py:50
  115.0 1.3 maximum_select_fusion
  116.9 1.0 copy-done.1
  118.1 0.8 fusion.15
  119.6 11.4 %while.10 = (s32[]{:T(128)}, bf16[2,8,15,128]{3,2,1,0:T(8,128)(2,1)}, bf16[2,8,6,128]{3,1,2,0:T(8,128)(2,1)S(1)}, bf16[6,512]{1,0:T(8,128)(2,1)}, f32[512]{0:T(5...) while((s32[]{:T(128)}, ...), condition=%wide.region_1.2_spmd, body=%wide.region_0.1_spmd.sunk | while | flops 565213184 | bytes 2786805 | solution.py:182
  119.6 2.5 %multiply_convert_fusion.3 = bf16[8,128,512]{2,1,0:T(8,128)(2,1)} fusion(f32[512]{0:T(512)S(1)} %get-tuple-element.372, bf16[1,8,6,128]{3,1,2,0:T(8,128)(2,1)S(1)} %constant_dynamic-slice_fusion.2, bf16[6,512]{1,0:T(8,128)(2,1)} %get-tuple-element.371), kind=kOutput, calls=%fused_computation.1.clone.1 | convolution fusion | flops 9437184 | bytes 1069056 | tf_op jit(solution)/shard_map/while/body/eval_jaxpr/bfc,fh->bch/dot_general | solution.py:169
  122.1 3.2 %fusion.294 = bf16[2,8,15,128]{3,2,1,0:T(8,128)(2,1)} fusion(bf16[2,8,15,128]{3,2,1,0:T(8,128)(2,1)} %get-tuple-element.359, s32[]{:T(128)S(6)} %copy.1411, bf16[8,128,512]{2,1,0:T(8,128)(2,1)} %multiply_convert_fusion.3, f32[512]{0:T(512)S(1)} %copy-done.34, bf16[512,512]{1,0:T(8,128)(2,1)} %get-tuple-element.373, f32[15]{0:T(128)S(1)} %copy-done.35, ...), kind=kOutput, calls=%fused_computation.6.clone.1 | convolution fusion | flops 555776000 | bytes 1623104 | tf_op jit(solution)/shard_map/while/body/eval_jaxpr/bch,hk->bkc/dot_general | solution.py:177
  125.3 2.5 %multiply_convert_fusion.3 = bf16[8,128,512]{2,1,0:T(8,128)(2,1)} fusion(f32[512]{0:T(512)S(1)} %get-tuple-element.372, bf16[1,8,6,128]{3,1,2,0:T(8,128)(2,1)S(1)} %constant_dynamic-slice_fusion.2, bf16[6,512]{1,0:T(8,128)(2,1)} %get-tuple-element.371), kind=kOutput, calls=%fused_computation.1.clone.1 | convolution fusion | flops 9437184 | bytes 1069056 | tf_op jit(solution)/shard_map/while/body/eval_jaxpr/bfc,fh->bch/dot_general | solution.py:169
  127.8 3.2 %fusion.294 = bf16[2,8,15,128]{3,2,1,0:T(8,128)(2,1)} fusion(bf16[2,8,15,128]{3,2,1,0:T(8,128)(2,1)} %get-tuple-element.359, s32[]{:T(128)S(6)} %copy.1411, bf16[8,128,512]{2,1,0:T(8,128)(2,1)} %multiply_convert_fusion.3, f32[512]{0:T(512)S(1)} %copy-done.34, bf16[512,512]{1,0:T(8,128)(2,1)} %get-tuple-element.373, f32[15]{0:T(128)S(1)} %copy-done.35, ...), kind=kOutput, calls=%fused_computation.6.clone.1 | convolution fusion | flops 555776000 | bytes 1623104 | tf_op jit(solution)/shard_map/while/body/eval_jaxpr/bch,hk->bkc/dot_general | solution.py:177
  131.0 1.8 %convolution_convert_fusion = bf16[64,1920]{1,0:T(8,128)(2,1)} fusion(bf16[2,8,15,128]{3,2,1,0:T(8,128)(2,1)} %get-tuple-element.49, s32[64]{0:T(128)S(1)} %eq.55), kind=kOutput, calls=%fused_computation.15 | convolution fusion | flops 4056064 | bytes 307456 | tf_op jit(solution)/shard_map/dot_general | solution.py:265
  132.8 1.9 %reshape.27 = bf16[2,32,15,128]{3,2,1,0:T(8,128)(2,1)} reshape(bf16[64,1920]{1,0:T(8,128)(2,1)} %convolution_convert_fusion) | data formatting | bytes 491520 | tf_op jit(solution)/shard_map/reshape | solution.py:271
  134.6 1.7 %copy.1334 = bf16[15,2,32,128]{3,2,1,0:T(8,128)(2,1)} copy(bf16[15,2,32,128]{3,0,2,1:T(8,128)(2,1)} %bitcast.60) | data formatting | bytes 491520
  136.3 1.4 %fusion.254 = (bf16[1,2,32,128]{3,2,1,0:T(8,128)(2,1)S(1)}, f32[1,2,32,128]{3,2,1,0:T(8,128)S(1)}, f32[1,2,32,128]{3,2,1,0:T(8,128)S(1)}, f32[1,2,32,128]{3,2,1,...) fusion(f32[1,2,32,128]{3,2,1,0:T(8,128)S(1)} %copy-done.23, ...), kind=kLoop, calls=%fused_computation.535 | loop fusion | flops 860160 | bytes 3045376 | tf_op jit(solution)/shard_map/convert
  (168 shorter events, 20.2 us)
Async XLA Ops:
  0.6 8.6 %copy-start.15 = (f32[19,2,32,128]{3,2,1,0:T(8,128)S(1)}, f32[19,2,32,128]{3,2,1,0:T(8,128)}, u32[]{:S(2)}) copy-start(f32[19,2,32,128]{3,2,1,0:T(8,128)} %param.11) | copy-start | bytes 1867780
  4.0 11.9 %copy-start.4 = (f32[6,2,32,128]{3,2,1,0:T(8,128)S(1)}, f32[6,2,32,128]{3,2,1,0:T(8,128)}, u32[]{:S(2)}) copy-start(f32[6,2,32,128]{3,2,1,0:T(8,128)} %param.12) | copy-start | bytes 589828
  15.9 14.7 %collective-permute-start = (f32[28,1,32,128]{3,2,1,0:T(8,128)S(1)}, f32[28,1,32,128]{3,2,1,0:T(8,128)S(1)}, u32[]{:S(2)}, u32[]{:S(2)}) collective-permute-start(f32[28,1,32,128]{3,2,1,0:T(8,128)S(1)} %get-tuple-element.283), channel_id=1, source_target_pairs={{0,32},{32,64},{64,96},{96,128},{128,160},{160,192},{192,224},{224... | collective-permute-start | bytes 1376264 | tf_op jit(solution)/shard_map/ppermute | solution.py:48
  15.9 14.6 %collective-permute-start.1 = (f32[28,1,32,128]{3,2,1,0:T(8,128)S(1)}, f32[28,1,32,128]{3,2,1,0:T(8,128)S(1)}, u32[]{:S(2)}, u32[]{:S(2)}) collective-permute-start(f32[28,1,32,128]{3,2,1,0:T(8,128)S(1)} %get-tuple-element.282), channel_id=1, source_target_pairs={{32,0},{64,32},{96,64},{128,96},{160,128},{192,160},{224,192},{256... | collective-permute-start | bytes 1376264 | tf_op jit(solution)/shard_map/ppermute | solution.py:50
  30.6 11.0 %copy-start.6 = (f32[28,1,32,128]{3,2,1,0:T(8,128)}, f32[28,1,32,128]{3,2,1,0:T(8,128)S(1)}, u32[]{:S(2)}) copy-start(f32[28,1,32,128]{3,2,1,0:T(8,128)S(1)} %collective-permute-done) | copy-start | bytes 1376260
  30.6 11.0 %copy-start.8 = (f32[28,1,32,128]{3,2,1,0:T(8,128)}, f32[28,1,32,128]{3,2,1,0:T(8,128)S(1)}, u32[]{:S(2)}) copy-start(f32[28,1,32,128]{3,2,1,0:T(8,128)S(1)} %collective-permute-done.1) | copy-start | bytes 1376260
  30.7 6.2 %collective-permute-start.2 = (f32[28,4,1,128]{3,0,2,1:T(8,128)S(1)}, f32[28,4,1,128]{3,0,2,1:T(8,128)S(1)}, u32[]{:S(2)}, u32[]{:S(2)}) collective-permute-start(f32[28,4,1,128]{3,0,2,1:T(8,128)S(1)} %copy.1336), channel_id=1, source_target_pairs={{0,4},{4,8},{8,12},{12,16},{16,20},{20,24},{24,28},{28,0},{1,5},{5... | collective-permute-start | bytes 172040 | tf_op jit(solution)/shard_map/ppermute | solution.py:48
  34.2 6.9 %collective-permute-start.3 = (f32[28,4,1,128]{3,0,2,1:T(8,128)S(1)}, f32[28,4,1,128]{3,0,2,1:T(8,128)S(1)}, u32[]{:S(2)}, u32[]{:S(2)}) collective-permute-start(f32[28,4,1,128]{3,0,2,1:T(8,128)S(1)} %copy.1337), channel_id=1, source_target_pairs={{4,0},{8,4},{12,8},{16,12},{20,16},{24,20},{28,24},{0,28},{5,1},{9... | collective-permute-start | bytes 172040 | tf_op jit(solution)/shard_map/ppermute | solution.py:50
  44.7 5.8 %copy-start.14 = (f32[28,4,34,1]{3,2,1,0:T(8,128)S(1)}, f32[28,4,34,1]{3,2,1,0:T(8,128)}, u32[]{:S(2)}) copy-start(f32[28,4,34,1]{3,2,1,0:T(8,128)} %get-tuple-element.274) | copy-start | bytes 45700
  48.2 7.5 %collective-permute-start.4 = (f32[28,4,34,1]{2,0,3,1:T(8,128)}, f32[28,4,34,1]{2,0,3,1:T(8,128)}, u32[]{:S(2)}, u32[]{:S(2)}) collective-permute-start(f32[28,4,34,1]{2,0,3,1:T(8,128)} %copy.1314), channel_id=1, source_target_pairs={{0,1},{1,2},{2,3},{3,0},{4,5},{5,6},{6,7},{7,4},{8,9},{9,10},{10,1... | collective-permute-start | bytes 45704 | tf_op jit(solution)/shard_map/ppermute | solution.py:48
  52.2 7.7 %collective-permute-start.5 = (f32[28,4,34,1]{2,0,3,1:T(8,128)}, f32[28,4,34,1]{2,0,3,1:T(8,128)}, u32[]{:S(2)}, u32[]{:S(2)}) collective-permute-start(f32[28,4,34,1]{2,0,3,1:T(8,128)} %copy.1316), channel_id=1, source_target_pairs={{1,0},{2,1},{3,2},{0,3},{5,4},{6,5},{7,6},{4,7},{9,8},{10,9},{11,1... | collective-permute-start | bytes 45704 | tf_op jit(solution)/shard_map/ppermute | solution.py:50
  55.6 7.3 %copy-start.21 = (f32[1,2,32,128]{3,2,1,0:T(8,128)S(1)}, f32[1,2,32,128]{3,2,1,0:T(8,128)}, u32[]{:S(2)}) copy-start(f32[1,2,32,128]{3,2,1,0:T(8,128)} %get-tuple-element.270) | copy-start | bytes 98308
  62.9 2.8 %copy-start.22 = (f32[1,2,32,128]{3,2,1,0:T(8,128)S(1)}, f32[1,2,32,128]{3,2,1,0:T(8,128)}, u32[]{:S(2)}) copy-start(f32[1,2,32,128]{3,2,1,0:T(8,128)} %get-tuple-element.270) | copy-start | bytes 98308
  65.0 7.4 %copy-start = (f32[28,4,34,1]{3,2,1,0:T(8,128)S(1)}, f32[28,4,34,1]{3,2,1,0:T(8,128)}, u32[]{:S(2)}) copy-start(f32[28,4,34,1]{3,2,1,0:T(8,128)} %copy.1317) | copy-start | bytes 45700
  65.0 7.4 %copy-start.7 = (f32[28,1,32,128]{3,2,1,0:T(8,128)S(1)}, f32[28,1,32,128]{3,2,1,0:T(8,128)}, u32[]{:S(2)}) copy-start(f32[28,1,32,128]{3,2,1,0:T(8,128)} %copy-done.6) | copy-start | bytes 1376260
  65.0 7.4 %copy-start.9 = (f32[28,1,32,128]{3,2,1,0:T(8,128)S(1)}, f32[28,1,32,128]{3,2,1,0:T(8,128)}, u32[]{:S(2)}) copy-start(f32[28,1,32,128]{3,2,1,0:T(8,128)} %copy-done.8) | copy-start | bytes 1376260
  65.0 7.4 %copy-start.17 = (f32[28,4,1,128]{3,2,1,0:T(1,128)S(1)}, f32[28,4,1,128]{3,2,1,0:T(1,128)}, u32[]{:S(2)}) copy-start(f32[28,4,1,128]{3,2,1,0:T(1,128)} %copy-done.16) | copy-start | bytes 172036
  73.3 0.8 copy-start.25
  73.4 0.8 copy-start.27
  73.4 0.8 copy-start.28
  75.2 20.7 %copy-start.2 = (f32[28,2,32,128]{3,2,1,0:T(8,128)}, f32[28,2,32,128]{3,2,1,0:T(8,128)S(1)}, u32[]{:S(2)}) copy-start(f32[28,2,32,128]{3,2,1,0:T(8,128)S(1)} %get-tuple-element.203) | copy-start | bytes 2752516
  75.3 9.1 %collective-permute-start.6 = (f32[28,1,32,128]{3,2,1,0:T(8,128)S(1)}, f32[28,1,32,128]{3,2,1,0:T(8,128)S(1)}, u32[]{:S(2)}, u32[]{:S(2)}) collective-permute-start(f32[28,1,32,128]{3,2,1,0:T(8,128)S(1)} %get-tuple-element.281), channel_id=1, source_target_pairs={{0,32},{32,64},{64,96},{96,128},{128,160},{160,192},{192,224},{224... | collective-permute-start | bytes 1376264 | tf_op jit(solution)/shard_map/ppermute | solution.py:48
  75.3 9.1 %collective-permute-start.7 = (f32[28,1,32,128]{3,2,1,0:T(8,128)S(1)}, f32[28,1,32,128]{3,2,1,0:T(8,128)S(1)}, u32[]{:S(2)}, u32[]{:S(2)}) collective-permute-start(f32[28,1,32,128]{3,2,1,0:T(8,128)S(1)} %get-tuple-element.280), channel_id=1, source_target_pairs={{32,0},{64,32},{96,64},{128,96},{160,128},{192,160},{224,192},{256... | collective-permute-start | bytes 1376264 | tf_op jit(solution)/shard_map/ppermute | solution.py:50
  84.4 11.9 %copy-start.10 = (f32[28,1,32,128]{3,2,1,0:T(8,128)}, f32[28,1,32,128]{3,2,1,0:T(8,128)S(1)}, u32[]{:S(2)}) copy-start(f32[28,1,32,128]{3,2,1,0:T(8,128)S(1)} %collective-permute-done.6) | copy-start | bytes 1376260
  84.4 11.9 %copy-start.12 = (f32[28,1,32,128]{3,2,1,0:T(8,128)}, f32[28,1,32,128]{3,2,1,0:T(8,128)S(1)}, u32[]{:S(2)}) copy-start(f32[28,1,32,128]{3,2,1,0:T(8,128)S(1)} %collective-permute-done.7) | copy-start | bytes 1376260
  84.5 7.1 %collective-permute-start.8 = (f32[28,4,1,128]{3,0,2,1:T(8,128)S(1)}, f32[28,4,1,128]{3,0,2,1:T(8,128)S(1)}, u32[]{:S(2)}, u32[]{:S(2)}) collective-permute-start(f32[28,4,1,128]{3,0,2,1:T(8,128)S(1)} %copy.1338), channel_id=1, source_target_pairs={{0,4},{4,8},{8,12},{12,16},{16,20},{20,24},{24,28},{28,0},{1,5},{5... | collective-permute-start | bytes 172040 | tf_op jit(solution)/shard_map/ppermute | solution.py:48
  89.7 6.2 %collective-permute-start.9 = (f32[28,4,1,128]{3,0,2,1:T(8,128)S(1)}, f32[28,4,1,128]{3,0,2,1:T(8,128)S(1)}, u32[]{:S(2)}, u32[]{:S(2)}) collective-permute-start(f32[28,4,1,128]{3,0,2,1:T(8,128)S(1)} %copy.1339), channel_id=1, source_target_pairs={{4,0},{8,4},{12,8},{16,12},{20,16},{24,20},{28,24},{0,28},{5,1},{9... | collective-permute-start | bytes 172040 | tf_op jit(solution)/shard_map/ppermute | solution.py:50
  95.9 2.6 %copy-start.18 = (f32[28,4,1,128]{3,2,1,0:T(1,128)}, f32[28,4,1,128]{3,2,1,0:T(1,128)S(1)}, u32[]{:S(2)}) copy-start(f32[28,4,1,128]{3,2,1,0:T(1,128)S(1)} %copy.1323) | copy-start | bytes 172036
  98.6 10.3 %copy-start.31 = (s32[2,32,1]{1,2,0:T(1,128)S(1)}, s32[2,32,1]{1,2,0:T(1,128)}, u32[]{:S(2)}) copy-start(s32[2,32,1]{1,2,0:T(1,128)} %param.13) | copy-start | bytes 772
  101.2 8.4 %collective-permute-start.10 = (f32[28,4,34,1]{2,0,3,1:T(8,128)S(1)}, f32[28,4,34,1]{2,0,3,1:T(8,128)S(1)}, u32[]{:S(2)}, u32[]{:S(2)}) collective-permute-start(f32[28,4,34,1]{2,0,3,1:T(8,128)S(1)} %copy.1326), channel_id=1, source_target_pairs={{0,1},{1,2},{2,3},{3,0},{4,5},{5,6},{6,7},{7,4},{8,9},{9,10},{10,1... | collective-permute-start | bytes 45704 | tf_op jit(solution)/shard_map/ppermute | solution.py:48
  104.4 7.5 %collective-permute-start.11 = (f32[28,4,34,1]{2,0,3,1:T(8,128)S(1)}, f32[28,4,34,1]{2,0,3,1:T(8,128)}, u32[]{:S(2)}, u32[]{:S(2)}) collective-permute-start(f32[28,4,34,1]{2,0,3,1:T(8,128)S(1)} %copy.1328), channel_id=1, source_target_pairs={{1,0},{2,1},{3,2},{0,3},{5,4},{6,5},{7,6},{4,7},{9,8},{10,9},{11,1... | collective-permute-start | bytes 45704 | tf_op jit(solution)/shard_map/ppermute | solution.py:50
  109.6 5.3 %copy-start.3 = (f32[28,2,32,128]{3,2,1,0:T(8,128)S(1)}, f32[28,2,32,128]{3,2,1,0:T(8,128)}, u32[]{:S(2)}) copy-start(f32[28,2,32,128]{3,2,1,0:T(8,128)} %copy-done.2) | copy-start | bytes 2752516
  114.9 1.4 copy-start.5
  116.3 1.6 %copy-start.1 = (f32[28,4,34,1]{3,2,1,0:T(8,128)S(1)}, f32[28,4,34,1]{3,2,1,0:T(8,128)}, u32[]{:S(2)}) copy-start(f32[28,4,34,1]{3,2,1,0:T(8,128)} %copy.1329) | copy-start | bytes 45700
  116.3 1.7 %copy-start.11 = (f32[28,1,32,128]{3,2,1,0:T(8,128)S(1)}, f32[28,1,32,128]{3,2,1,0:T(8,128)}, u32[]{:S(2)}) copy-start(f32[28,1,32,128]{3,2,1,0:T(8,128)} %copy-done.10) | copy-start | bytes 1376260
  116.3 1.8 %copy-start.13 = (f32[28,1,32,128]{3,2,1,0:T(8,128)S(1)}, f32[28,1,32,128]{3,2,1,0:T(8,128)}, u32[]{:S(2)}) copy-start(f32[28,1,32,128]{3,2,1,0:T(8,128)} %copy-done.12) | copy-start | bytes 1376260
  116.3 1.8 %copy-start.19 = (f32[28,4,1,128]{3,2,1,0:T(1,128)S(1)}, f32[28,4,1,128]{3,2,1,0:T(1,128)}, u32[]{:S(2)}) copy-start(f32[28,4,1,128]{3,2,1,0:T(1,128)} %copy-done.18) | copy-start | bytes 172036
  118.1 0.8 copy-start.30
  118.1 1.4 %copy-start.33 = (f32[512]{0:T(512)S(1)}, f32[512]{0:T(512)}, u32[]{:S(2)}) copy-start(f32[512]{0:T(512)} %param.15) | copy-start | bytes 6148
  119.5 16.8 %copy-start.20 = (f32[28,4,1,128]{3,2,1,0:T(1,128)S(1)}, f32[28,4,1,128]{3,2,1,0:T(1,128)}, u32[]{:S(2)}) copy-start(f32[28,4,1,128]{3,2,1,0:T(1,128)} %copy-done.18) | copy-start | bytes 172036
  119.5 16.8 %copy-start.23 = (f32[1,2,32,128]{3,2,1,0:T(8,128)S(1)}, f32[1,2,32,128]{3,2,1,0:T(8,128)}, u32[]{:S(2)}) copy-start(f32[1,2,32,128]{3,2,1,0:T(8,128)} %get-tuple-element.270) | copy-start | bytes 98308
  119.6 16.8 %copy-start.26 = (f32[1,2,32,128]{3,2,1,0:T(8,128)S(1)}, f32[1,2,32,128]{3,2,1,0:T(8,128)}, u32[]{:S(2)}) copy-start(f32[1,2,32,128]{3,2,1,0:T(8,128)} %get-tuple-element.242) | copy-start | bytes 98308
  119.6 2.5 %copy-start.32 = (bf16[512,15]{0,1:T(8,128)(2,1)S(1)}, bf16[512,15]{0,1:T(8,128)(2,1)}, u32[]{:S(2)}) copy-start(bf16[512,15]{0,1:T(8,128)(2,1)} %get-tuple-element.375) | copy-start | bytes 46084 | tf_op jit(solution)/shard_map/while
  119.6 2.5 %copy-start.34 = (f32[512]{0:T(512)S(1)}, f32[512]{0:T(512)}, u32[]{:S(2)}) copy-start(f32[512]{0:T(512)} %get-tuple-element.374) | copy-start | bytes 6148 | tf_op jit(solution)/shard_map/while
  119.6 2.5 %copy-start.35 = (f32[15]{0:T(128)S(1)}, f32[15]{0:T(128)}, u32[]{:S(2)}) copy-start(f32[15]{0:T(128)} %get-tuple-element.376) | copy-start | bytes 184 | tf_op jit(solution)/shard_map/while
  125.3 2.5 %copy-start.32 = (bf16[512,15]{0,1:T(8,128)(2,1)S(1)}, bf16[512,15]{0,1:T(8,128)(2,1)}, u32[]{:S(2)}) copy-start(bf16[512,15]{0,1:T(8,128)(2,1)} %get-tuple-element.375) | copy-start | bytes 46084 | tf_op jit(solution)/shard_map/while
  125.3 2.5 %copy-start.34 = (f32[512]{0:T(512)S(1)}, f32[512]{0:T(512)}, u32[]{:S(2)}) copy-start(f32[512]{0:T(512)} %get-tuple-element.374) | copy-start | bytes 6148 | tf_op jit(solution)/shard_map/while
  125.3 2.5 %copy-start.35 = (f32[15]{0:T(128)S(1)}, f32[15]{0:T(128)}, u32[]{:S(2)}) copy-start(f32[15]{0:T(128)} %get-tuple-element.376) | copy-start | bytes 184 | tf_op jit(solution)/shard_map/while
  (3 other events, 2.3 us)
where the time goes:
time: 140 us; the launch traced here: 138 us
  starting transfers between devices  36.2 us (26%)
  other arithmetic  34 us (24%)
  local copies, waits for them, and re-layouts  28.9 us (21%)
  waiting for transfers between devices  24.7 us (18%)
  matrix products  13.2 us (9%)
    ppermute x6, starting transfers between devices, extended(): lax.ppermute(head, axis, [((i + 1) % count, i) for i in range(count)])  23 us
    unnamed x49, other arithmetic  18.6 us
    ppermute x6, starting transfers between devices, extended(): lax.ppermute(tail, axis, [(i, (i + 1) % count) for i in range(count)])  13.2 us
    ppermute x6, waiting for transfers between devices, extended(): lax.ppermute(tail, axis, [(i, (i + 1) % count) for i in range(count)])  12.6 us
    ppermute x6, waiting for transfers between devices, extended(): lax.ppermute(head, axis, [((i + 1) % count, i) for i in range(count)])  12.1 us
    slice x6, local copies, waits for them, and re-layouts, extended(): head = lax.slice_in_dim(cells, 0, width, axis=dim)  7.84 us
    dot_general x2, matrix products, one_step(): jnp.einsum('bch,hk->bkc', hidden_two, w_out, preferred_element_type=jnp.f...  6.33 us
    ppermute x4, local copies, waits for them, and re-layouts, extended(): lax.ppermute(head, axis, [((i + 1) % count, i) for i in range(count)])  6.3 us
  transfers between devices with their start and end apart: 12, of which 7 were waited for; matrix products, arithmetic and copies ran while one was open for 5% of the time, Pallas kernels for 0%

commit v1 on v0

v1 whole, which is shorter than its diff:
```python
import functools

import jax
import jax.numpy as jnp
from jax import lax
from jax.experimental import pallas as pl
from jax.experimental.pallas import tpu as pltpu
from jax.sharding import PartitionSpec as P


VELOCITIES = [
    (0, 0, 0),
    (1, 0, 0),
    (-1, 0, 0),
    (0, 1, 0),
    (0, -1, 0),
    (0, 0, 1),
    (0, 0, -1),
    (1, 1, 0),
    (-1, -1, 0),
    (1, -1, 0),
    (-1, 1, 0),
    (1, 0, 1),
    (-1, 0, -1),
    (1, 0, -1),
    (-1, 0, 1),
    (0, 1, 1),
    (0, -1, -1),
    (0, 1, -1),
    (0, -1, 1),
]
WEIGHTS = [1.0 / 3.0] + [1.0 / 18.0] * 6 + [1.0 / 36.0] * 12
OMEGA = 1.0 / 0.8
SHAPE_FACTOR = 0.95
ORIENT_STEP = 4.0
PAIRS = [(0, 0), (1, 1), (2, 2), (0, 1), (0, 2), (1, 2)]
ENTRY = [[0, 3, 4], [3, 1, 5], [4, 5, 2]]
TOWARD = {
    0: [i for i in range(19) if VELOCITIES[i][0] == -1],
    1: [i for i in range(19) if VELOCITIES[i][0] == 1],
}
KNOWN = {0: [i for i in range(19) if VELOCITIES[i][0] != 1], 1: [i for i in range(19) if VELOCITIES[i][0] != -1]}
MSG_WIDE = 23
MSG_ROWS = 1072
HALO_AT = 928
SIDE_AT = 1024
CORNER_AT = 1056
STATE = 38


def opposite(i):
    return 0 if i == 0 else (i + 1 if i % 2 == 1 else i - 1)


def lanes_of():
    return lax.broadcasted_iota(jnp.int32, (8, 128), 1)


def rows_of():
    return lax.broadcasted_iota(jnp.int32, (8, 128), 0)


def roll(v, shift, axis):
    shift = shift % v.shape[axis]
    return v if shift == 0 else pltpu.roll(v, shift, axis)


def add_all(terms):
    while len(terms) > 1:
        terms = [
            terms[k] + terms[k + 1] if k + 1 < len(terms) else terms[k] for k in range(0, len(terms), 2)
        ]
    return terms[0]


def moments(f, numbers):
    rho = add_all([f[i] for i in numbers])
    mom = []
    for ax in range(3):
        pos = [f[i] for i in numbers if VELOCITIES[i][ax] > 0]
        neg = [f[i] for i in numbers if VELOCITIES[i][ax] < 0]
        total = add_all(pos) if pos else None
        if neg:
            total = add_all(neg) * -1.0 if total is None else total - add_all(neg)
        mom.append(total)
    return rho, mom


def relax(f, rho, u, numbers):
    usq = 1.0 - 1.5 * (u[0] * u[0] + u[1] * u[1] + u[2] * u[2])
    scaled = {w: (w * OMEGA) * rho for w in sorted(set(WEIGHTS[i] for i in numbers))}
    out = {}
    for i in numbers:
        proj = None
        for ax in range(3):
            c = VELOCITIES[i][ax]
            if c != 0:
                if proj is None:
                    proj = u[ax] if c > 0 else -u[ax]
                else:
                    proj = proj + u[ax] if c > 0 else proj - u[ax]
        poly = usq if proj is None else usq + proj * (3.0 + 4.5 * proj)
        out[i] = f[i] * (1.0 - OMEGA) + scaled[WEIGHTS[i]] * poly
    return out


def plus(a, b):
    if a is None:
        return b
    if b is None:
        return a
    return a + b


def minus(a, b):
    if b is None:
        return a
    if a is None:
        return -b
    return a - b


def times(a, b):
    return None if a is None or b is None else a * b


def jeffery(a, g):
    half = [[None if g[j][k] is None else 0.5 * g[j][k] for k in range(3)] for j in range(3)]
    d = [[plus(half[j][k], half[k][j]) if j <= k else None for k in range(3)] for j in range(3)]
    w = [[minus(half[j][k], half[k][j]) if j < k else None for k in range(3)] for j in range(3)]
    full = lambda j, k: a[ENTRY[j][k]]
    strain = lambda j, k: d[min(j, k)][max(j, k)]

    def spin(j, k):
        if j == k:
            return None
        if j < k:
            return w[j][k]
        return None if w[k][j] is None else -w[k][j]

    contraction = None
    for j in range(3):
        contraction = plus(contraction, times(full(j, j), strain(j, j)))
    for j, k in ((0, 1), (0, 2), (1, 2)):
        cross = times(full(j, k), strain(j, k))
        contraction = plus(contraction, None if cross is None else 2.0 * cross)
    twice = 2.0 * contraction
    mix = [[plus(spin(j, k), times(strain(j, k), SHAPE_FACTOR)) for k in range(3)] for j in range(3)]
    z = [[None] * 3 for _ in range(3)]
    for j in range(3):
        for k in range(3):
            for m in range(3):
                z[j][k] = plus(z[j][k], times(full(j, m), mix[m][k]))
    scaled = SHAPE_FACTOR * twice
    return [plus(z[j][k], z[k][j]) - scaled * full(j, k) for j, k in PAIRS]


def put(ref, at, r, v):
    if r < 4:
        ref[at + (pl.ds(16 + 8 * r, 8), slice(None))] = v
    else:
        ref[at + (pl.ds(8, 8), slice(None))] = v
        ref[at + (pl.ds(48, 8), slice(None))] = v


def get(ref, at, r, dy=0):
    if r < 4:
        return ref[at + (pl.ds(16 + 8 * r + dy, 8), slice(None))]
    if dy == 0:
        return ref[at + (pl.ds(48, 8), slice(None))]
    return jnp.where(
        rows_of() < 4,
        ref[at + (pl.ds(48 + dy, 8), slice(None))],
        ref[at + (pl.ds(8 + dy, 8), slice(None))],
    )


def pull_z(own, side, dz, want_side=True):
    if dz == 0:
        return own, side
    lane = lanes_of()
    own_r, side_r = roll(own, dz, 1), roll(side, dz, 1)
    edge = lane == (0 if dz > 0 else 127)
    return jnp.where(edge, side_r, own_r), jnp.where(edge, own_r, side_r) if want_side else None


def walls():
    layer = lax.axis_index("gz")
    last = lax.axis_size("gz") - 1
    lane = lanes_of()
    low = lane == jnp.where(layer == 0, 0, -1)
    high = lane == jnp.where(layer == last, 127, -1)
    return low, high


def wall_of(i, low, high):
    dz = VELOCITIES[i][2]
    return None if dz == 0 else (low if dz > 0 else high)


def stream(ref, at_of, i, r, low, high, reflected, want_side=True):
    _, cy, cz = VELOCITIES[i]
    own = get(ref, at_of(0), r, -cy)
    side = get(ref, at_of(1), r, -cy) if (want_side or cz != 0) else None
    if cz == 0:
        return own, side
    own, side = pull_z(own, side, cz, want_side)
    return jnp.where(wall_of(i, low, high), reflected(), own), side


def central(ref, at_of, r, axis, low, high, outside, want_side=True):
    if axis == 1:
        out = []
        for t in (0, 1) if want_side else (0,):
            out.append(0.5 * (get(ref, at_of(t), r, 1) - get(ref, at_of(t), r, -1)))
        return out
    own, side = get(ref, at_of(0), r), get(ref, at_of(1), r)
    behind, behind_side = pull_z(own, side, 1, want_side)
    ahead, ahead_side = pull_z(own, side, -1, want_side)
    past = own if outside else jnp.zeros_like(own)
    diff = 0.5 * (jnp.where(high, past, ahead) - jnp.where(low, past, behind))
    return [diff, 0.5 * (ahead_side - behind_side)] if want_side else [diff]


def pack_z_kernel(pop, ori, zpack, low_rows, high_rows):
    lane = lax.broadcasted_iota(jnp.int32, (32, 128), 1)
    tiles = [jnp.zeros((32, 128), jnp.float32), jnp.zeros((32, 128), jnp.float32)]
    for f in range(25):
        for x in range(2):
            s = 2 * f + x
            src = pop if f < 19 else ori
            k = f if f < 19 else f - 19
            v = src[k, x]
            at = 4 * (s % 32)
            tiles[s // 32] = jnp.where((lane >= at) & (lane < at + 4), roll(v, at + 2, 1), tiles[s // 32])
            low_rows[pl.ds(2 * s, 2), :] = src[k, x, 0:2, :]
            high_rows[pl.ds(2 * s, 2), :] = src[k, x, 30:32, :]
    zpack[0] = tiles[0]
    zpack[1] = tiles[1]
    low_rows[100:104, :] = jnp.zeros((4, 128), jnp.float32)
    high_rows[100:104, :] = jnp.zeros((4, 128), jnp.float32)


def pack_y_kernel(from_minus, from_plus, low_in, high_in, sides, low_rows, high_rows):
    lane = lax.broadcasted_iota(jnp.int32, (32, 128), 1)
    low_rows[...] = low_in[...]
    high_rows[...] = high_in[...]
    for t in range(2):
        both = jnp.where(lane % 4 < 2, from_minus[t], from_plus[t])
        sides[t] = both
        low_rows[pl.ds(100 + 2 * t, 2), :] = sides[t, 0:2, :]
        high_rows[pl.ds(100 + 2 * t, 2), :] = sides[t, 30:32, :]


def step_one_kernel(pop, ori, sides, from_yminus, from_yplus, state, msg_low, msg_high, halo, fields, out):
    low, high = walls()
    lane, row = lanes_of(), rows_of()
    for s in range(52):
        halo[s, 0:2, :] = from_yplus[pl.ds(2 * s, 2), :]
        halo[s, 6:8, :] = from_yminus[pl.ds(2 * s, 2), :]

    def raw(f, x, t, r):
        s = 2 * f + x
        if t == 0:
            if r == 4:
                return halo[s]
            return pop[f, x, pl.ds(8 * r, 8), :] if f < 19 else ori[f - 19, x, pl.ds(8 * r, 8), :]
        packed = halo[50 + s // 32] if r == 4 else sides[s // 32, pl.ds(8 * r, 8), :]
        return roll(packed, -(4 * (s % 32) + 2), 1)

    numbers = list(range(19))
    for x in range(2):
        for t in range(2):
            for r in range(5):
                f = [raw(i, x, t, r) for i in numbers]
                rho, mom = moments(f, numbers)
                inv = 1.0 / rho
                u = [m * inv for m in mom]
                relaxed = relax(f, rho, u, numbers)
                for i in numbers:
                    put(fields, (i, x, t), r, relaxed[i])
                for j in range(3):
                    put(fields, (19 + j, x, t), r, u[j])
                for k in range(6):
                    put(fields, (22 + k, x, t), r, raw(19 + k, x, t, r))

    for x in range(2):
        for r in range(5):
            place = lambda f, xs=x: (lambda t: (f, xs, t))
            known = [{}, {}]
            for i in KNOWN[x]:
                xs = x - VELOCITIES[i][0]
                pair = stream(
                    fields, place(i, xs), i, r, low, high, lambda i=i: get(fields, (opposite(i), x, 0), r)
                )
                known[0][i], known[1][i] = pair
            grad = [[[None] * 3 for _ in range(3)] for _ in range(2)]
            sign = 0.5 if x == 0 else -0.5
            for j in range(3):
                by_y = central(fields, place(19 + j), r, 1, low, high, False)
                by_z = central(fields, place(19 + j), r, 2, low, high, False)
                for t in range(2):
                    grad[t][j][0] = sign * get(fields, (19 + j, 1 - x, t), r)
                    grad[t][j][1] = by_y[t]
                    grad[t][j][2] = by_z[t]
            u = [[get(fields, (19 + j, x, t), r) for j in range(3)] for t in range(2)]
            a = [[get(fields, (22 + k, x, t), r) for k in range(6)] for t in range(2)]
            advect = [[], []]
            for k in range(6):
                by_y = central(fields, place(22 + k), r, 1, low, high, True)
                by_z = central(fields, place(22 + k), r, 2, low, high, True)
                for t in range(2):
                    by_x = sign * get(fields, (22 + k, 1 - x, t), r)
                    advect[t].append(u[t][0] * by_x + u[t][1] * by_y[t] + u[t][2] * by_z[t])
            side_pack = jnp.zeros((8, 128), jnp.float32)
            for t in range(2):
                rate = jeffery(a[t], grad[t])
                part = [a[t][k] + ORIENT_STEP * (rate[k] - advect[t][k]) for k in range(6)]
                rho, mom = moments(known[t], KNOWN[x])
                outward = [get(fields, (i, x, t), r) for i in TOWARD[x]]
                keep = [known[t][i] for i in KNOWN[x]] + [rho] + mom + part + u[t] + a[t] + outward
                for k in range(STATE):
                    state[x, k, t, pl.ds(8 * r, 8), :] = keep[k]
                wide = outward + u[t] + a[t] + [rho] + mom + [known[t][i] for i in TOWARD[x]]
                if t == 1:
                    for k in range(MSG_WIDE):
                        at = 4 * k
                        side_pack = jnp.where((lane >= at) & (lane < at + 4), roll(wide[k], at + 2, 1), side_pack)
                elif r < 4:
                    for k, v in enumerate(wide + part):
                        out[x, pl.ds(32 * k + 8 * r, 8), :] = v
                else:
                    inner = (row >= 2) & (row < 6)
                    for k in range(0, MSG_WIDE, 2):
                        v = wide[k]
                        if k + 1 < MSG_WIDE:
                            v = jnp.where(inner, roll(wide[k + 1], 4, 0), v)
                        out[x, pl.ds(HALO_AT + 4 * k, 8), :] = v
            out[x, pl.ds(SIDE_AT + 8 * r if r < 4 else CORNER_AT, 8), :] = side_pack
    for x in range(2):
        out[x, pl.ds(CORNER_AT + 8, 8), :] = jnp.zeros((8, 128), jnp.float32)
    msg_low[...] = out[0].astype(jnp.bfloat16)
    msg_high[...] = out[1].astype(jnp.bfloat16)


def step_two_kernel(
    slots, state, from_low, from_high, w_one, w_mid, b_mid, w_out, b_out, flow, closure,
    got, fields, near, level, feats, spread, place,
):
    low, high = walls()
    got[0] = from_low[...].astype(jnp.float32)
    got[1] = from_high[...].astype(jnp.float32)
    for s in range(17):
        place[s] = 64
    for b in range(64):
        s = slots[b]
        place[jnp.where(s >= 0, s, 16)] = b

    def arrived(x, k, t, r):
        if t == 0 and r < 4:
            return got[x, pl.ds(32 * k + 8 * r, 8), :]
        if t == 0:
            v = got[x, pl.ds(HALO_AT + 8 * (k // 2), 8), :]
            return roll(v, 4, 0) if k % 2 else v
        v = got[x, pl.ds(SIDE_AT + 8 * r if r < 4 else CORNER_AT, 8), :]
        return roll(v, -(4 * k + 2), 1)

    kept = lambda x, k, t, r: state[x, k, t, pl.ds(8 * r, 8), :]
    for x in range(2):
        for t in range(2):
            for r in range(5):
                for k in range(5):
                    put(near, (x, k, t), r, arrived(x, k, t, r))
                    put(near, (x, 5 + k, t), r, kept(x, 33 + k, t, r))
    numbers = list(range(19))
    for x in range(2):
        come = TOWARD[1 - x]
        go = TOWARD[x]
        sign = -0.5 if x == 0 else 0.5
        for r in range(5):
            come_f, go_f = [{}, {}], [{}, {}]
            for k, i in enumerate(come):
                back = go.index(opposite(i))
                pair = stream(
                    near, lambda t, k=k: (x, k, t), i, r, low, high,
                    lambda back=back: get(near, (x, 5 + back, 0), r),
                )
                come_f[0][i], come_f[1][i] = pair
            for k, i in enumerate(go):
                back = come.index(opposite(i))
                pair = stream(
                    near, lambda t, k=k: (x, 5 + k, t), i, r, low, high,
                    lambda back=back: get(near, (x, back, 0), r),
                )
                go_f[0][i], go_f[1][i] = pair
            for t in range(2):
                f = {i: kept(x, k, t, r) for k, i in enumerate(KNOWN[x])}
                f.update(come_f[t])
                rho_new, mom_new = moments(come_f[t], come)
                rho = kept(x, 14, t, r) + rho_new
                mom = [kept(x, 15 + j, t, r) + mom_new[j] for j in range(3)]
                inv = 1.0 / rho
                u = [m * inv for m in mom]
                relaxed = relax(f, rho, u, numbers)
                for i in numbers:
                    put(fields, (i, x, t), r, relaxed[i])
                for j in range(3):
                    put(fields, (19 + j, x, t), r, u[j])
                u0 = [kept(x, 24 + j, t, r) for j in range(3)]
                a0 = [kept(x, 27 + k, t, r) for k in range(6)]
                u0n = [arrived(x, 5 + j, t, r) for j in range(3)]
                a0n = [arrived(x, 8 + k, t, r) for k in range(6)]
                rate = jeffery(a0, [[sign * u0n[j], None, None] for j in range(3)])
                drift = (sign * u0[0])
                for k in range(6):
                    a1 = kept(x, 18 + k, t, r) + ORIENT_STEP * (rate[k] - drift * a0n[k])
                    put(fields, (22 + k, x, t), r, a1)
                rho_new, mom_new = moments(go_f[t], go)
                rho = arrived(x, 14, t, r) + rho_new
                inv = 1.0 / rho
                u = [(arrived(x, 15 + j, t, r) + mom_new[j]) * inv for j in range(3)]
                f = {i: arrived(x, 18 + k, t, r) for k, i in enumerate(come)}
                relaxed = relax(f, rho, u, come)
                for k, i in enumerate(come):
                    put(fields, (28 + k, x, t), r, relaxed[i])
                if t == 0 and r < 4:
                    rate = jeffery(a0n, [[-sign * u0[j], None, None] for j in range(3)])
                    drift = -sign * u0n[0]
                    for j in range(3):
                        level[x, j, pl.ds(8 * r, 8), :] = u[j]
                    for k in range(6):
                        a1 = arrived(x, 23 + k, t, r) + ORIENT_STEP * (rate[k] - drift * a0[k])
                        level[x, 3 + k, pl.ds(8 * r, 8), :] = a1

    feats[...] = jnp.ones(feats.shape, jnp.float32)
    for x in range(2):
        for r in range(4):
            f = {}
            for i in numbers:
                xs = x - VELOCITIES[i][0]
                if 0 <= xs <= 1:
                    at_of = lambda t, i=i, xs=xs: (i, xs, t)
                else:
                    k = TOWARD[1 - x].index(i)
                    at_of = lambda t, k=k: (28 + k, x, t)
                f[i], _ = stream(
                    fields, at_of, i, r, low, high, lambda i=i: get(fields, (opposite(i), x, 0), r), False
                )
            rho, mom = moments(f, numbers)
            inv = 1.0 / rho
            final = [rho] + [m * inv for m in mom]
            for k in range(4):
                spread[pl.ds(k * 64 + x * 32 + 8 * r, 8), :] = final[k]
            sign = -0.5 if x == 0 else 0.5
            by_x = lambda k, n: sign * (level[x, n, pl.ds(8 * r, 8), :] - get(fields, (k, 1 - x, 0), r))
            grad = [[None] * 3 for _ in range(3)]
            for j in range(3):
                place_u = lambda t, j=j: (19 + j, x, t)
                grad[j][0] = by_x(19 + j, j)
                grad[j][1] = central(fields, place_u, r, 1, low, high, False, False)[0]
                grad[j][2] = central(fields, place_u, r, 2, low, high, False, False)[0]
            u = [get(fields, (19 + j, x, 0), r) for j in range(3)]
            a = [get(fields, (22 + k, x, 0), r) for k in range(6)]
            rate = jeffery(a, grad)
            for k in range(6):
                place_a = lambda t, k=k: (22 + k, x, t)
                advect = (
                    u[0] * by_x(22 + k, 3 + k)
                    + u[1] * central(fields, place_a, r, 1, low, high, True, False)[0]
                    + u[2] * central(fields, place_a, r, 2, low, high, True, False)[0]
                )
                new = a[k] + ORIENT_STEP * (rate[k] - advect)
                feats[pl.ds((x * 32 + 8 * r) * 8 + k, 8, 8), :] = new
    for k in range(4):
        for x in range(2):
            flow[k, x] = spread[pl.ds(k * 64 + x * 32, 32), :].astype(jnp.bfloat16)

    spread[...] = jnp.zeros(spread.shape, jnp.float32)
    ones = jnp.ones((8, 128), jnp.bfloat16)
    bias_mid = jnp.dot(b_mid[...], ones, preferred_element_type=jnp.float32)
    bias_out = jnp.dot(b_out[...], ones, preferred_element_type=jnp.float32)
    group = 2
    bias_mid = jnp.concatenate([bias_mid] * group, axis=1)
    for g in range(16 // group):
        at = [place[g * group + k] for k in range(group)]
        cells = [feats[pl.ds(pl.multiple_of(b * 8, 8), 8), :] for b in at]
        cells = jnp.concatenate(cells, axis=1).astype(jnp.bfloat16)
        v = jnp.dot(w_one[...], cells, preferred_element_type=jnp.float32)
        h = (v + v * jnp.tanh(v)).astype(jnp.bfloat16)
        v = jnp.dot(w_mid[...], h, preferred_element_type=jnp.float32) + bias_mid
        h = (v + v * jnp.tanh(v)).astype(jnp.bfloat16)
        v = jnp.dot(w_out[...], h, preferred_element_type=jnp.float32)
        for k in range(group):
            spread[pl.ds(pl.multiple_of(at[k] * 16, 16), 16), :] = v[:, 128 * k : 128 * k + 128] + bias_out
    for c in range(15):
        for x in range(2):
            closure[c, x] = spread[pl.ds(x * 512 + c, 32, 16), :].astype(jnp.bfloat16)


def split_bias(bias):
    high = lax.reduce_precision(bias, 8, 7)
    rest = lax.reduce_precision(bias - high, 8, 7)
    return jnp.stack([high, rest], axis=1).astype(jnp.bfloat16)


def local(populations, orientation, slot_table, w_in, b_in, w_mid, b_mid, w_out, b_out):
    f32, bf16 = jnp.float32, jnp.bfloat16
    shape = lambda *s, d=f32: jax.ShapeDtypeStruct(s, d)
    vmem = pl.BlockSpec(memory_space=pltpu.VMEM)
    smem = pl.BlockSpec(memory_space=pltpu.SMEM)
    params = pltpu.CompilerParams(vmem_limit_bytes=48 * 1024 * 1024)

    def ring(axis, step, wrap):
        n = lax.axis_size(axis)
        return [(i, (i + step) % n) for i in range(n) if wrap or 0 <= i + step < n]

    half_in = 0.5 * b_in
    half_mid = 0.5 * b_mid
    w_one = jnp.concatenate([(0.5 * w_in).T, split_bias(half_in)], axis=1)
    w_two = (0.5 * w_mid).T
    b_two = jnp.pad(split_bias(half_mid), ((0, 0), (0, 6)))
    w_three = jnp.pad(w_out.T, ((0, 1), (0, 0)))
    b_three = jnp.pad(split_bias(b_out), ((0, 1), (0, 6)))
    slots = slot_table.reshape(64)

    zpack, low_raw, high_raw = pl.pallas_call(
        pack_z_kernel,
        out_shape=(shape(2, 32, 128), shape(104, 128), shape(104, 128)),
        in_specs=[vmem] * 2,
        out_specs=(vmem,) * 3,
        compiler_params=params,
    )(populations, orientation)
    from_minus = lax.ppermute(zpack, "gz", ring("gz", 1, False))
    from_plus = lax.ppermute(zpack, "gz", ring("gz", -1, False))
    sides, low_rows, high_rows = pl.pallas_call(
        pack_y_kernel,
        out_shape=(shape(2, 32, 128), shape(104, 128), shape(104, 128)),
        in_specs=[vmem] * 4,
        out_specs=(vmem,) * 3,
        compiler_params=params,
    )(from_minus, from_plus, low_raw, high_raw)
    from_yminus = lax.ppermute(high_rows, "gy", ring("gy", 1, True))
    from_yplus = lax.ppermute(low_rows, "gy", ring("gy", -1, True))
    state, msg_low, msg_high = pl.pallas_call(
        step_one_kernel,
        out_shape=(
            shape(2, STATE, 2, 40, 128),
            shape(MSG_ROWS, 128, d=bf16),
            shape(MSG_ROWS, 128, d=bf16),
        ),
        in_specs=[vmem] * 5,
        out_specs=(vmem,) * 3,
        scratch_shapes=[
            pltpu.VMEM((52, 8, 128), f32),
            pltpu.VMEM((28, 2, 2, 64, 128), f32),
            pltpu.VMEM((2, MSG_ROWS, 128), f32),
        ],
        compiler_params=params,
    )(populations, orientation, sides, from_yminus, from_yplus)
    from_low = lax.ppermute(msg_high, "gx", ring("gx", 1, True))
    from_high = lax.ppermute(msg_low, "gx", ring("gx", -1, True))
    return pl.pallas_call(
        step_two_kernel,
        out_shape=(shape(4, 2, 32, 128, d=bf16), shape(15, 2, 32, 128, d=bf16)),
        in_specs=[smem] + [vmem] * 8,
        out_specs=(vmem,) * 2,
        scratch_shapes=[
            pltpu.VMEM((2, MSG_ROWS, 128), f32),
            pltpu.VMEM((33, 2, 2, 64, 128), f32),
            pltpu.VMEM((2, 10, 2, 64, 128), f32),
            pltpu.VMEM((2, 9, 32, 128), f32),
            pltpu.VMEM((65 * 8, 128), f32),
            pltpu.VMEM((65 * 16, 128), f32),
            pltpu.SMEM((17,), jnp.int32),
        ],
        compiler_params=params,
    )(slots, state, from_low, from_high, w_one, w_two, b_two, w_three, b_three)


def solution(mesh):
    grid = P(None, "gx", "gy", "gz")
    in_specs = (grid, grid, P("gx", "gy", "gz"), P(), P(), P(), P(), P(), P())
    return jax.shard_map(local, mesh=mesh, in_specs=in_specs, out_specs=(grid, grid), check_vma=False)
```

time: 140 us -> 48.7 us (0.35)
  the two profiles are of different devices: /device:TPU:22 before, /device:TPU:24 now
where the time goes in v1:
time: 48.7 us; the launch traced here: 48.1 us
  starting transfers between devices  18.9 us (39%)
  Pallas kernels  11 us (23%)
  local copies, waits for them, and re-layouts  6.97 us (14%)
  waiting for transfers between devices  5.29 us (11%)
  other arithmetic  5.2 us (11%)
  between operations  0.78 us (2%)
    pallas_call x1, Pallas kernels, local(): pl.pallas_call(step_two_kernel, out_shape=(shape(4, 2, 32, 128, d=bf16),...  8.09 us
    ppermute x1, starting transfers between devices, local(): from_high = lax.ppermute(msg_low, 'gx', ring('gx', -1, True))  6.49 us
    unnamed x8, local copies, waits for them, and re-layouts  5.65 us
    ppermute x1, waiting for transfers between devices, local(): from_yplus = lax.ppermute(low_rows, 'gy', ring('gy', -1, True))  5.28 us
    ppermute x1, starting transfers between devices, local(): from_yminus = lax.ppermute(high_rows, 'gy', ring('gy', 1, True))  4.7 us
    ppermute x1, starting transfers between devices, local(): from_minus = lax.ppermute(zpack, 'gz', ring('gz', 1, False))  4.55 us
    pallas_call x1, Pallas kernels, local(): pl.pallas_call(step_one_kernel, out_shape=(shape(2, STATE, 2, 40, 128), s...  2.56 us
    ppermute x1, starting transfers between devices, local(): from_yplus = lax.ppermute(low_rows, 'gy', ring('gy', -1, True))  1.92 us
  transfers between devices with their start and end apart: 6, of which 1 were waited for; matrix products, arithmetic and copies ran while one was open for 19% of the time, Pallas kernels for 0%

profile of v1, /device:TPU:24, one launch (start us, length us, event | category | flops | bytes accessed | tf_op | source)
XLA Modules:
  0.0 48.1 jit_solution(13943706005943201348)
XLA Ops:
  0.6 0.0 copy-start
  0.6 1.1 %copy-done = f32[19,2,32,128]{3,2,1,0:T(8,128)S(1)} copy-done((f32[19,2,32,128]{3,2,1,0:T(8,128)S(1)}, f32[19,2,32,128]{3,2,1,0:T(8,128)}, u32[]{:S(2)}) %copy-start) | copy-done | bytes 622616
  1.7 0.0 copy-start.2
  1.7 0.9 %copy-done.2 = f32[6,2,32,128]{3,2,1,0:T(8,128)S(1)} copy-done((f32[6,2,32,128]{3,2,1,0:T(8,128)S(1)}, f32[6,2,32,128]{3,2,1,0:T(8,128)}, u32[]{:S(2)}) %copy-start.2) | copy-done | bytes 196632
  2.6 0.3 shard_map.104
  2.9 1.3 %collective-permute-start.1 = (f32[2,32,128]{2,1,0:T(8,128)S(1)}, f32[2,32,128]{2,1,0:T(8,128)S(1)}, u32[]{:S(2)}, u32[]{:S(2)}) collective-permute-start(f32[2,32,128]{2,1,0:T(8,128)S(1)} %get-tuple-element.11), channel_id=1, source_target_pairs={{1,0},{2,1},{3,2},{5,4},{6,5},{7,6},{9,8},{10,9},{11,10},{13,12},{... | collective-permute-start | bytes 98312 | tf_op jit(solution)/shard_map/ppermute | solution.py:534
  4.2 4.5 %collective-permute-start = (f32[2,32,128]{2,1,0:T(8,128)S(1)}, f32[2,32,128]{2,1,0:T(8,128)S(1)}, u32[]{:S(2)}, u32[]{:S(2)}) collective-permute-start(f32[2,32,128]{2,1,0:T(8,128)S(1)} %get-tuple-element.11), channel_id=1, source_target_pairs={{0,1},{1,2},{2,3},{4,5},{5,6},{6,7},{8,9},{9,10},{10,11},{12,13},{... | collective-permute-start | bytes 98312 | tf_op jit(solution)/shard_map/ppermute | solution.py:533
  8.8 0.7 %fusion.4 = (bf16[15,1]{0,1:T(2,128)(2,1)S(1)}, bf16[15,1]{0,1:T(2,128)(2,1)S(1)}) fusion(f32[15]{0:T(128)} %param.17), kind=kLoop, calls=%fused_computation.14 | loop fusion | flops 75 | bytes 120 | tf_op jit(solution)/shard_map/stack | solution.py:503
  9.4 0.7 %reduce-precision_convert_fusion.1 = (bf16[512]{0:T(512)(128)(2,1)S(1)}, bf16[512]{0:T(512)(128)(2,1)S(1)}) fusion(f32[512]{0:T(512)} %param.13), kind=kLoop, calls=%fused_computation.6 | loop fusion | flops 3072 | bytes 4096 | tf_op jit(solution)/shard_map/convert.11
  10.1 0.7 %reduce-precision_convert_fusion = (bf16[512]{0:T(512)(128)(2,1)S(1)}, bf16[512]{0:T(512)(128)(2,1)S(1)}) fusion(f32[512]{0:T(512)} %param.15), kind=kLoop, calls=%fused_computation.4 | loop fusion | flops 3072 | bytes 4096 | tf_op jit(solution)/shard_map/convert.7
  10.8 0.7 %multiply_bitcast_fusion.1 = bf16[512,6]{0,1:T(8,128)(2,1)S(1)} fusion(bf16[6,512]{1,0:T(8,128)(2,1)} %param.12), kind=kLoop, calls=%fused_computation.2 | loop fusion | flops 3072 | bytes 12288 | tf_op jit(solution)/shard_map/transpose | solution.py:519
  11.6 0.0 collective-permute-done.1.from_plus
  11.6 0.0 collective-permute-done.from_minus
  11.6 4.7 %collective-permute-start.2 = (f32[104,128]{1,0:T(8,128)S(1)}, f32[104,128]{1,0:T(8,128)S(1)}, u32[]{:S(2)}, u32[]{:S(2)}) collective-permute-start(f32[104,128]{1,0:T(8,128)S(1)} %get-tuple-element.15), channel_id=1, source_target_pairs={{0,4},{4,8},{8,12},{12,16},{16,20},{20,24},{24,28},{28,0},{1,5},{5... | collective-permute-start | bytes 159752 | tf_op jit(solution)/shard_map/ppermute | solution.py:542
  16.3 1.9 %collective-permute-start.3 = (f32[104,128]{1,0:T(8,128)S(1)}, f32[104,128]{1,0:T(8,128)S(1)}, u32[]{:S(2)}, u32[]{:S(2)}) collective-permute-start(f32[104,128]{1,0:T(8,128)S(1)} %get-tuple-element.16), channel_id=1, source_target_pairs={{0,28},{4,0},{8,4},{12,8},{16,12},{20,16},{24,20},{28,24},{1,29},{... | collective-permute-start | bytes 159752 | tf_op jit(solution)/shard_map/ppermute | solution.py:543
  18.3 0.0 collective-permute-done.2.from_yminus
  18.3 5.3 %collective-permute-done.3.from_yplus = f32[104,128]{1,0:T(8,128)S(1)} collective-permute-done((f32[104,128]{1,0:T(8,128)S(1)}, f32[104,128]{1,0:T(8,128)S(1)}, u32[]{:S(2)}, u32[]{:S(2)}) %collective-permute-start.3) | collective-permute-done | bytes 53280 | tf_op jit(solution)/shard_map/ppermute | solution.py:543
  23.6 0.0 copy-start.1
  23.6 1.1 %copy-done.1 = f32[19,2,32,128]{3,2,1,0:T(8,128)S(1)} copy-done((f32[19,2,32,128]{3,2,1,0:T(8,128)S(1)}, f32[19,2,32,128]{3,2,1,0:T(8,128)}, u32[]{:S(2)}) %copy-start.1) | copy-done | bytes 622616
  24.6 2.6 %shard_map.106 = (f32[2,38,2,40,128]{4,3,2,1,0:T(8,128)S(1)}, bf16[1072,128]{1,0:T(8,128)(2,1)}, bf16[1072,128]{1,0:T(8,128)(2,1)}) custom-call(f32[19,2,32,128]{3,2,1,0:T(8,128)S(1)} %copy-done.1, f32[6,2,32,128]{3,2,1,0:T(8,128)S(1)} %copy-done.2, f32[2,32,128]{2,1,0:T(8,128)S(1)} %get-tuple-element.14.sides, ...), custom_call_target="tpu_custom_call" | custom-call | tf_op jit(solution)/shard_map/pallas_call | solution.py:544
  27.2 0.0 collective-permute-start.4
  27.2 6.5 %collective-permute-start.5 = (bf16[1072,128]{1,0:T(8,128)(2,1)}, bf16[1072,128]{1,0:T(8,128)(2,1)}, u32[]{:S(2)}, u32[]{:S(2)}) collective-permute-start(bf16[1072,128]{1,0:T(8,128)(2,1)} %get-tuple-element.19), channel_id=1, source_target_pairs={{0,480},{32,0},{64,32},{96,64},{128,96},{160,128},{192,160},{224,1... | collective-permute-start | bytes 823304 | tf_op jit(solution)/shard_map/ppermute | solution.py:561
  33.7 0.5 %broadcast.17 = s32[]{:T(128)} broadcast(s32[]{:T(128)} %constant.34), dimensions={} | broadcast | bytes 8 | tf_op args[2]
  34.2 1.3 %reduce.3 = s32[2,32]{1,0:T(2,128)S(1)} reduce(s32[2,32,1]{1,2,0:T(1,128)} %param.11, s32[]{:T(128)} %broadcast.17), dimensions={2}, to_apply=%param.11.reduce_sub_computation.3 | reduce | bytes 516 | tf_op args[2]
  35.6 0.1 reshape.7.slots
  35.6 0.1 copy.27
  35.7 0.7 %pad.13.w_out = bf16[16,512]{1,0:T(8,128)(2,1)S(1)} pad(bf16[15,512]{1,0:T(8,128)(2,1)} %bitcast.10, bf16[]{:T(256)} %constant.2.clone.1), padding=0_1x0_0 | pad | bytes 31746 | tf_op jit(solution)/shard_map/jit(_pad)/pad | solution.py:522
  36.5 0.2 copy.28.w_one
  36.6 0.2 copy.26
  36.9 2.1 %copy.25 = bf16[512,512]{0,1:T(8,128)(2,1)} copy(bf16[512,512]{1,0:T(8,128)(2,1)} %param.14) | data formatting | bytes 1048576 | tf_op args[5]
  38.9 1.1 %multiply_bitcast_fusion.w_mid = bf16[512,512]{1,0:T(8,128)(2,1)S(1)} fusion(bf16[512,512]{0,1:T(8,128)(2,1)} %copy.25), kind=kLoop, calls=%fused_computation | loop fusion | flops 262144 | bytes 1048576 | tf_op jit(solution)/shard_map/transpose | solution.py:520
  40.0 0.0 collective-permute-done.4.from_low
  40.0 0.0 collective-permute-done.5.from_high
  40.1 8.1 %shard_map.107 = (bf16[4,2,32,128]{3,2,1,0:T(8,128)(2,1)}, bf16[15,2,32,128]{3,2,1,0:T(8,128)(2,1)}) custom-call(s32[64]{0:T(128)S(1)} %reshape.7.slots, f32[2,38,2,40,128]{4,3,2,1,0:T(8,128)S(1)} %get-tuple-element.17.state, bf16[1072,128]{1,0:T(8,128)(2,1)} %collective-permute-done.4.from_low, bf16[1072,128]{1,0:T(8,128)(2,1)} %collective-permute-done.5.from_high, ...), custom_call_target="tpu_custom_call" | custom-call | tf_op jit(solution)/shard_map/pallas_call | solution.py:562
  (10 shorter events, 0.1 us)
Async XLA Ops:
  0.6 1.1 %copy-start = (f32[19,2,32,128]{3,2,1,0:T(8,128)S(1)}, f32[19,2,32,128]{3,2,1,0:T(8,128)}, u32[]{:S(2)}) copy-start(f32[19,2,32,128]{3,2,1,0:T(8,128)} %pop.3) | copy-start | bytes 1867780
  1.7 0.9 %copy-start.2 = (f32[6,2,32,128]{3,2,1,0:T(8,128)S(1)}, f32[6,2,32,128]{3,2,1,0:T(8,128)}, u32[]{:S(2)}) copy-start(f32[6,2,32,128]{3,2,1,0:T(8,128)} %ori.3) | copy-start | bytes 589828
  2.9 8.6 %collective-permute-start.1 = (f32[2,32,128]{2,1,0:T(8,128)S(1)}, f32[2,32,128]{2,1,0:T(8,128)S(1)}, u32[]{:S(2)}, u32[]{:S(2)}) collective-permute-start(f32[2,32,128]{2,1,0:T(8,128)S(1)} %get-tuple-element.11), channel_id=1, source_target_pairs={{1,0},{2,1},{3,2},{5,4},{6,5},{7,6},{9,8},{10,9},{11,10},{13,12},{... | collective-permute-start | bytes 98312 | tf_op jit(solution)/shard_map/ppermute | solution.py:534
  4.2 7.4 %collective-permute-start = (f32[2,32,128]{2,1,0:T(8,128)S(1)}, f32[2,32,128]{2,1,0:T(8,128)S(1)}, u32[]{:S(2)}, u32[]{:S(2)}) collective-permute-start(f32[2,32,128]{2,1,0:T(8,128)S(1)} %get-tuple-element.11), channel_id=1, source_target_pairs={{0,1},{1,2},{2,3},{4,5},{5,6},{6,7},{8,9},{9,10},{10,11},{12,13},{... | collective-permute-start | bytes 98312 | tf_op jit(solution)/shard_map/ppermute | solution.py:533
  11.6 6.7 %collective-permute-start.2 = (f32[104,128]{1,0:T(8,128)S(1)}, f32[104,128]{1,0:T(8,128)S(1)}, u32[]{:S(2)}, u32[]{:S(2)}) collective-permute-start(f32[104,128]{1,0:T(8,128)S(1)} %get-tuple-element.15), channel_id=1, source_target_pairs={{0,4},{4,8},{8,12},{12,16},{16,20},{20,24},{24,28},{28,0},{1,5},{5... | collective-permute-start | bytes 159752 | tf_op jit(solution)/shard_map/ppermute | solution.py:542
  16.3 7.2 %collective-permute-start.3 = (f32[104,128]{1,0:T(8,128)S(1)}, f32[104,128]{1,0:T(8,128)S(1)}, u32[]{:S(2)}, u32[]{:S(2)}) collective-permute-start(f32[104,128]{1,0:T(8,128)S(1)} %get-tuple-element.16), channel_id=1, source_target_pairs={{0,28},{4,0},{8,4},{12,8},{16,12},{20,16},{24,20},{28,24},{1,29},{... | collective-permute-start | bytes 159752 | tf_op jit(solution)/shard_map/ppermute | solution.py:543
  23.6 1.1 %copy-start.1 = (f32[19,2,32,128]{3,2,1,0:T(8,128)S(1)}, f32[19,2,32,128]{3,2,1,0:T(8,128)}, u32[]{:S(2)}) copy-start(f32[19,2,32,128]{3,2,1,0:T(8,128)} %pop.3) | copy-start | bytes 1867780
  27.2 12.8 %collective-permute-start.4 = (bf16[1072,128]{1,0:T(8,128)(2,1)}, bf16[1072,128]{1,0:T(8,128)(2,1)}, u32[]{:S(2)}, u32[]{:S(2)}) collective-permute-start(bf16[1072,128]{1,0:T(8,128)(2,1)} %get-tuple-element.18), channel_id=1, source_target_pairs={{0,32},{32,64},{64,96},{96,128},{128,160},{160,192},{192,224},{224... | collective-permute-start | bytes 823304 | tf_op jit(solution)/shard_map/ppermute | solution.py:560
  27.2 12.8 %collective-permute-start.5 = (bf16[1072,128]{1,0:T(8,128)(2,1)}, bf16[1072,128]{1,0:T(8,128)(2,1)}, u32[]{:S(2)}, u32[]{:S(2)}) collective-permute-start(bf16[1072,128]{1,0:T(8,128)(2,1)} %get-tuple-element.19), channel_id=1, source_target_pairs={{0,480},{32,0},{64,32},{96,64},{128,96},{160,128},{192,160},{224,1... | collective-permute-start | bytes 823304 | tf_op jit(solution)/shard_map/ppermute | solution.py:561

commit v2 on v1

--- a/solution.py
+++ b/solution.py
@@ -45,6 +45,10 @@
 HALO_AT = 928
 SIDE_AT = 1024
 CORNER_AT = 1056
+MIB = 1024 * 1024
+LIMIT_PACK = 5375 * MIB // 100
+LIMIT_OWN = 5270 * MIB // 100
+LIMIT_WEIGHTS = 4900 * MIB // 100
 STATE = 38
 
 
@@ -222,7 +226,16 @@
     return [diff, 0.5 * (ahead_side - behind_side)] if want_side else [diff]
 
 
-def pack_z_kernel(pop, ori, zpack, low_rows, high_rows):
+def fetch(pairs, sems):
+    copies = [pltpu.make_async_copy(src, dst, sems.at[k]) for k, (src, dst) in enumerate(pairs)]
+    for copy in copies:
+        copy.start()
+    return copies
+
+
+def pack_z_kernel(pop_hbm, ori_hbm, zpack, low_rows, high_rows, pop, ori, sems):
+    for copy in fetch([(pop_hbm, pop), (ori_hbm, ori)], sems):
+        copy.wait()
     lane = lax.broadcasted_iota(jnp.int32, (32, 128), 1)
     tiles = [jnp.zeros((32, 128), jnp.float32), jnp.zeros((32, 128), jnp.float32)]
     for f in range(25):
@@ -241,6 +254,27 @@
     high_rows[100:104, :] = jnp.zeros((4, 128), jnp.float32)
 
 
+def own_kernel(pop_hbm, ori_hbm, after, own, pop, ori, sems):
+    del after
+    for copy in fetch([(pop_hbm, pop), (ori_hbm, ori)], sems):
+        copy.wait()
+    numbers = list(range(19))
+    for x in range(2):
+        for r in range(4):
+            rows = pl.ds(8 * r, 8)
+            f = [pop[i, x, rows, :] for i in numbers]
+            rho, mom = moments(f, numbers)
+            inv = 1.0 / rho
+            u = [m * inv for m in mom]
+            relaxed = relax(f, rho, u, numbers)
+            for i in numbers:
+                own[i, x, rows, :] = relaxed[i]
+            for j in range(3):
+                own[19 + j, x, rows, :] = u[j]
+            for k in range(6):
+                own[22 + k, x, rows, :] = ori[k, x, rows, :]
+
+
 def pack_y_kernel(from_minus, from_plus, low_in, high_in, sides, low_rows, high_rows):
     lane = lax.broadcasted_iota(jnp.int32, (32, 128), 1)
     low_rows[...] = low_in[...]
@@ -252,7 +286,7 @@
         high_rows[pl.ds(100 + 2 * t, 2), :] = sides[t, 30:32, :]
 
 
-def step_one_kernel(pop, ori, sides, from_yminus, from_yplus, state, msg_low, msg_high, halo, fields, out):
+def step_one_kernel(own, sides, from_yminus, from_yplus, state, msg_low, msg_high, halo, fields, out):
     low, high = walls()
     lane, row = lanes_of(), rows_of()
     for s in range(52):
@@ -262,9 +296,7 @@
     def raw(f, x, t, r):
         s = 2 * f + x
         if t == 0:
-            if r == 4:
-                return halo[s]
-            return pop[f, x, pl.ds(8 * r, 8), :] if f < 19 else ori[f - 19, x, pl.ds(8 * r, 8), :]
+            return halo[s]
         packed = halo[50 + s // 32] if r == 4 else sides[s // 32, pl.ds(8 * r, 8), :]
         return roll(packed, -(4 * (s % 32) + 2), 1)
 
@@ -272,6 +304,10 @@
     for x in range(2):
         for t in range(2):
             for r in range(5):
+                if t == 0 and r < 4:
+                    for k in range(28):
+                        put(fields, (k, x, t), r, own[k, x, pl.ds(8 * r, 8), :])
+                    continue
                 f = [raw(i, x, t, r) for i in numbers]
                 rho, mom = moments(f, numbers)
                 inv = 1.0 / rho
@@ -343,6 +379,35 @@
     msg_high[...] = out[1].astype(jnp.bfloat16)
 
 
+def weights_kernel(
+    w_in_hbm, b_in_hbm, w_mid_hbm, b_mid_hbm, w_out_hbm, b_out_hbm, w_one, w_two, bias_mid, w_three, bias_out,
+    w_in, b_in, w_mid, b_mid, b_out, wide, sems,
+):
+    pairs = [
+        (w_mid_hbm, w_mid),
+        (w_in_hbm, w_in),
+        (b_in_hbm, b_in),
+        (b_mid_hbm, b_mid),
+        (b_out_hbm, b_out),
+        (w_out_hbm, w_three),
+    ]
+    for copy in fetch(pairs, sems):
+        copy.wait()
+    f32, bf16 = jnp.float32, jnp.bfloat16
+    row = lax.broadcasted_iota(jnp.int32, (8, 512), 0)
+    bias = jnp.broadcast_to(0.5 * b_in[...], (8, 512))
+    first = bias.astype(bf16).astype(f32)
+    rest = bias - first
+    padded = jnp.concatenate([0.5 * w_in[...].astype(f32), jnp.zeros((2, 512), f32)], axis=0)
+    stacked = jnp.where(row == 6, first, jnp.where(row == 7, rest, padded))
+    w_one[...] = stacked.T.astype(bf16)
+    w_two[...] = (0.5 * w_mid[...].astype(f32)).T.astype(bf16)
+    bias_mid[...] = jnp.broadcast_to(jnp.broadcast_to(0.5 * b_mid[...], (8, 512)).T[:, 0:1], (512, 128))
+    wide[...] = jnp.zeros(wide.shape, f32)
+    wide[:, 0:15] = jnp.broadcast_to(b_out[...], (8, 15))
+    bias_out[...] = jnp.broadcast_to(wide[...].T[0:16, 0:1], (16, 128))
+
+
 def step_two_kernel(
     slots, state, from_low, from_high, w_one, w_mid, b_mid, w_out, b_out, flow, closure,
     got, fields, near, level, feats, spread, place,
@@ -353,7 +418,7 @@
     for s in range(17):
         place[s] = 64
     for b in range(64):
-        s = slots[b]
+        s = slots[b // 32, 0, b % 32]
         place[jnp.where(s >= 0, s, 16)] = b
 
     def arrived(x, k, t, r):
@@ -476,11 +541,8 @@
             flow[k, x] = spread[pl.ds(k * 64 + x * 32, 32), :].astype(jnp.bfloat16)
 
     spread[...] = jnp.zeros(spread.shape, jnp.float32)
-    ones = jnp.ones((8, 128), jnp.bfloat16)
-    bias_mid = jnp.dot(b_mid[...], ones, preferred_element_type=jnp.float32)
-    bias_out = jnp.dot(b_out[...], ones, preferred_element_type=jnp.float32)
-    group = 2
-    bias_mid = jnp.concatenate([bias_mid] * group, axis=1)
+    group = 8
+    bias_mid = jnp.concatenate([b_mid[...]] * group, axis=1)
     for g in range(16 // group):
         at = [place[g * group + k] for k in range(group)]
         cells = [feats[pl.ds(pl.multiple_of(b * 8, 8), 8), :] for b in at]
@@ -491,16 +553,10 @@
         h = (v + v * jnp.tanh(v)).astype(jnp.bfloat16)
         v = jnp.dot(w_out[...], h, preferred_element_type=jnp.float32)
         for k in range(group):
-            spread[pl.ds(pl.multiple_of(at[k] * 16, 16), 16), :] = v[:, 128 * k : 128 * k + 128] + bias_out
+            spread[pl.ds(pl.multiple_of(at[k] * 16, 16), 15), :] = v[:, 128 * k : 128 * k + 128] + b_out[0:15, :]
     for c in range(15):
         for x in range(2):
             closure[c, x] = spread[pl.ds(x * 512 + c, 32, 16), :].astype(jnp.bfloat16)
-
-
-def split_bias(bias):
-    high = lax.reduce_precision(bias, 8, 7)
-    rest = lax.reduce_precision(bias - high, 8, 7)
-    return jnp.stack([high, rest], axis=1).astype(jnp.bfloat16)
 
 
 def local(populations, orientation, slot_table, w_in, b_in, w_mid, b_mid, w_out, b_out):
@@ -514,22 +570,47 @@
         n = lax.axis_size(axis)
         return [(i, (i + step) % n) for i in range(n) if wrap or 0 <= i + step < n]
 
-    half_in = 0.5 * b_in
-    half_mid = 0.5 * b_mid
-    w_one = jnp.concatenate([(0.5 * w_in).T, split_bias(half_in)], axis=1)
-    w_two = (0.5 * w_mid).T
-    b_two = jnp.pad(split_bias(half_mid), ((0, 0), (0, 6)))
-    w_three = jnp.pad(w_out.T, ((0, 1), (0, 0)))
-    b_three = jnp.pad(split_bias(b_out), ((0, 1), (0, 6)))
-    slots = slot_table.reshape(64)
-
+    hbm = pl.BlockSpec(memory_space=pltpu.HBM)
+    slots = jnp.transpose(slot_table, (0, 2, 1))
+    w_one, w_two, bias_mid, w_three, bias_out = pl.pallas_call(
+        weights_kernel,
+        out_shape=(
+            shape(512, 8, d=bf16),
+            shape(512, 512, d=bf16),
+            shape(512, 128),
+            shape(15, 512, d=bf16),
+            shape(16, 128),
+        ),
+        in_specs=[hbm] * 6,
+        out_specs=(vmem,) * 5,
+        scratch_shapes=[
+            pltpu.VMEM((6, 512), bf16),
+            pltpu.VMEM((1, 512), f32),
+            pltpu.VMEM((512, 512), bf16),
+            pltpu.VMEM((1, 512), f32),
+            pltpu.VMEM((1, 15), f32),
+            pltpu.VMEM((8, 128), f32),
+            pltpu.SemaphoreType.DMA((6,)),
+        ],
+        compiler_params=pltpu.CompilerParams(vmem_limit_bytes=LIMIT_WEIGHTS),
+    )(w_in, b_in.reshape(1, 512), w_mid, b_mid.reshape(1, 512), w_out.T, b_out.reshape(1, 15))
+    raw_scratch = [pltpu.VMEM((19, 2, 32, 128), f32), pltpu.VMEM((6, 2, 32, 128), f32), pltpu.SemaphoreType.DMA((2,))]
     zpack, low_raw, high_raw = pl.pallas_call(
         pack_z_kernel,
         out_shape=(shape(2, 32, 128), shape(104, 128), shape(104, 128)),
-        in_specs=[vmem] * 2,
+        in_specs=[hbm] * 2,
         out_specs=(vmem,) * 3,
-        compiler_params=params,
+        scratch_shapes=raw_scratch,
+        compiler_params=pltpu.CompilerParams(vmem_limit_bytes=LIMIT_PACK),
     )(populations, orientation)
+    own = pl.pallas_call(
+        own_kernel,
+        out_shape=shape(28, 2, 32, 128),
+        in_specs=[hbm] * 3,
+        out_specs=vmem,
+        scratch_shapes=raw_scratch,
+        compiler_params=pltpu.CompilerParams(vmem_limit_bytes=LIMIT_OWN),
+    )(populations, orientation, zpack)
     from_minus = lax.ppermute(zpack, "gz", ring("gz", 1, False))
     from_plus = lax.ppermute(zpack, "gz", ring("gz", -1, False))
     sides, low_rows, high_rows = pl.pallas_call(
@@ -548,7 +629,7 @@
             shape(MSG_ROWS, 128, d=bf16),
             shape(MSG_ROWS, 128, d=bf16),
         ),
-        in_specs=[vmem] * 5,
+        in_specs=[vmem] * 4,
         out_specs=(vmem,) * 3,
         scratch_shapes=[
             pltpu.VMEM((52, 8, 128), f32),
@@ -556,7 +637,7 @@
             pltpu.VMEM((2, MSG_ROWS, 128), f32),
         ],
         compiler_params=params,
-    )(populations, orientation, sides, from_yminus, from_yplus)
+    )(own, sides, from_yminus, from_yplus)
     from_low = lax.ppermute(msg_high, "gx", ring("gx", 1, True))
     from_high = lax.ppermute(msg_low, "gx", ring("gx", -1, True))
     return pl.pallas_call(
@@ -574,7 +655,7 @@
             pltpu.SMEM((17,), jnp.int32),
         ],
         compiler_params=params,
-    )(slots, state, from_low, from_high, w_one, w_two, b_two, w_three, b_three)
+    )(slots, state, from_low, from_high, w_one, w_two, bias_mid, w_three, bias_out)
 
 
 def solution(mesh):

time: 48.7 us -> 42.6 us (0.87)
  the two profiles are of different devices: /device:TPU:24 before, /device:TPU:219 now
where the time goes in v2:
time: 42.6 us; the launch traced here: 42.2 us
  starting transfers between devices  18.4 us (43%)
  Pallas kernels  10.4 us (24%)
  waiting for transfers between devices  9.5 us (22%)
  local copies, waits for them, and re-layouts  3.21 us (8%)
  between operations  0.81 us (2%)
    ppermute x1, starting transfers between devices, local(): from_low = lax.ppermute(msg_high, 'gx', ring('gx', 1, True))  6.73 us
    pallas_call x1, Pallas kernels, local(): pl.pallas_call(step_two_kernel, out_shape=(shape(4, 2, 32, 128, d=bf16),...  5.08 us
    ppermute x1, starting transfers between devices, local(): from_yminus = lax.ppermute(high_rows, 'gy', ring('gy', 1, True))  4.42 us
    ppermute x1, waiting for transfers between devices, local(): from_high = lax.ppermute(msg_low, 'gx', ring('gx', -1, True))  3.69 us
    unnamed x20, local copies, waits for them, and re-layouts  3.21 us
    ppermute x1, starting transfers between devices, local(): from_minus = lax.ppermute(zpack, 'gz', ring('gz', 1, False))  3.12 us
    ppermute x1, waiting for transfers between devices, local(): from_low = lax.ppermute(msg_high, 'gx', ring('gx', 1, True))  2.79 us
    ppermute x1, waiting for transfers between devices, local(): from_plus = lax.ppermute(zpack, 'gz', ring('gz', -1, False))  2.48 us
  transfers between devices with their start and end apart: 6, of which 4 were waited for; matrix products, arithmetic and copies ran while one was open for 0% of the time, Pallas kernels for 5%

profile of v2, /device:TPU:219, one launch (start us, length us, event | category | flops | bytes accessed | tf_op | source)
XLA Modules:
  0.0 42.2 jit_solution(6153814212528342674)
XLA Ops:
  0.6 0.0 copy-start.6
  0.6 0.0 copy-start.7
  0.7 0.0 copy-start.4
  0.7 0.0 copy-start.9
  0.7 0.0 copy-start.5
  0.7 0.0 copy-start.3
  0.7 0.0 copy-start.8
  0.7 1.5 %shard_map.104 = (f32[2,32,128]{2,1,0:T(8,128)S(1)}, f32[104,128]{1,0:T(8,128)S(1)}, f32[104,128]{1,0:T(8,128)S(1)}) custom-call(f32[19,2,32,128]{3,2,1,0:T(8,128)} %pop_hbm.3, f32[6,2,32,128]{3,2,1,0:T(8,128)} %ori_hbm.3), custom_call_target="tpu_custom_call" | custom-call | tf_op jit(solution)/shard_map/pallas_call | solution.py:598
  2.2 3.1 %collective-permute-start = (f32[2,32,128]{2,1,0:T(8,128)S(1)}, f32[2,32,128]{2,1,0:T(8,128)S(1)}, u32[]{:S(2)}, u32[]{:S(2)}) collective-permute-start(f32[2,32,128]{2,1,0:T(8,128)S(1)} %get-tuple-element.16.after), channel_id=1, source_target_pairs={{0,1},{1,2},{2,3},{4,5},{5,6},{6,7},{8,9},{9,10},{10,11},{12,13},{... | collective-permute-start | bytes 98312 | tf_op jit(solution)/shard_map/ppermute | solution.py:614
  5.3 2.2 %collective-permute-start.1 = (f32[2,32,128]{2,1,0:T(8,128)S(1)}, f32[2,32,128]{2,1,0:T(8,128)S(1)}, u32[]{:S(2)}, u32[]{:S(2)}) collective-permute-start(f32[2,32,128]{2,1,0:T(8,128)S(1)} %get-tuple-element.16.after), channel_id=1, source_target_pairs={{1,0},{2,1},{3,2},{5,4},{6,5},{7,6},{9,8},{10,9},{11,10},{13,12},{... | collective-permute-start | bytes 98312 | tf_op jit(solution)/shard_map/ppermute | solution.py:615
  7.5 0.0 collective-permute-done.from_minus
  7.5 2.5 %collective-permute-done.1.from_plus = f32[2,32,128]{2,1,0:T(8,128)S(1)} collective-permute-done((f32[2,32,128]{2,1,0:T(8,128)S(1)}, f32[2,32,128]{2,1,0:T(8,128)S(1)}, u32[]{:S(2)}, u32[]{:S(2)}) %collective-permute-start.1) | collective-permute-done | bytes 32800 | tf_op jit(solution)/shard_map/ppermute | solution.py:615
  10.0 4.4 %collective-permute-start.2 = (f32[104,128]{1,0:T(8,128)S(1)}, f32[104,128]{1,0:T(8,128)S(1)}, u32[]{:S(2)}, u32[]{:S(2)}) collective-permute-start(f32[104,128]{1,0:T(8,128)S(1)} %get-tuple-element.20), channel_id=1, source_target_pairs={{0,4},{4,8},{8,12},{12,16},{16,20},{20,24},{24,28},{28,0},{1,5},{5... | collective-permute-start | bytes 159752 | tf_op jit(solution)/shard_map/ppermute | solution.py:623
  14.5 1.9 %collective-permute-start.3 = (f32[104,128]{1,0:T(8,128)S(1)}, f32[104,128]{1,0:T(8,128)S(1)}, u32[]{:S(2)}, u32[]{:S(2)}) collective-permute-start(f32[104,128]{1,0:T(8,128)S(1)} %get-tuple-element.21), channel_id=1, source_target_pairs={{0,28},{4,0},{8,4},{12,8},{16,12},{20,16},{24,20},{28,24},{1,29},{... | collective-permute-start | bytes 159752 | tf_op jit(solution)/shard_map/ppermute | solution.py:624
  16.4 0.0 copy-start.1
  16.4 1.1 %copy-done.1 = f32[19,2,32,128]{3,2,1,0:T(8,128)S(1)} copy-done((f32[19,2,32,128]{3,2,1,0:T(8,128)S(1)}, f32[19,2,32,128]{3,2,1,0:T(8,128)}, u32[]{:S(2)}) %copy-start.1) | copy-done | bytes 622616
  17.5 0.0 copy-start.2
  17.5 0.9 %copy-done.2 = f32[6,2,32,128]{3,2,1,0:T(8,128)S(1)} copy-done((f32[6,2,32,128]{3,2,1,0:T(8,128)S(1)}, f32[6,2,32,128]{3,2,1,0:T(8,128)}, u32[]{:S(2)}) %copy-start.2) | copy-done | bytes 196632
  18.4 1.6 %shard_map.105.own = f32[28,2,32,128]{3,2,1,0:T(8,128)} custom-call(f32[19,2,32,128]{3,2,1,0:T(8,128)S(1)} %copy-done.1, f32[6,2,32,128]{3,2,1,0:T(8,128)S(1)} %copy-done.2, f32[2,32,128]{2,1,0:T(8,128)S(1)} %get-tuple-element.16.after), custom_call_target="tpu_custom_call" | custom-call | tf_op jit(solution)/shard_map/pallas_call | solution.py:606
  20.0 0.0 collective-permute-done.2.from_yminus
  20.0 0.5 %collective-permute-done.3.from_yplus = f32[104,128]{1,0:T(8,128)S(1)} collective-permute-done((f32[104,128]{1,0:T(8,128)S(1)}, f32[104,128]{1,0:T(8,128)S(1)}, u32[]{:S(2)}, u32[]{:S(2)}) %collective-permute-start.3) | collective-permute-done | bytes 53280 | tf_op jit(solution)/shard_map/ppermute | solution.py:624
  20.5 0.0 copy-start
  20.5 1.2 %copy-done = f32[28,2,32,128]{3,2,1,0:T(8,128)S(1)} copy-done((f32[28,2,32,128]{3,2,1,0:T(8,128)S(1)}, f32[28,2,32,128]{3,2,1,0:T(8,128)}, u32[]{:S(2)}) %copy-start) | copy-done | bytes 917528
  21.7 1.5 %shard_map.107 = (f32[2,38,2,40,128]{4,3,2,1,0:T(8,128)S(1)}, bf16[1072,128]{1,0:T(8,128)(2,1)S(1)}, bf16[1072,128]{1,0:T(8,128)(2,1)S(1)}) custom-call(f32[28,2,32,128]{3,2,1,0:T(8,128)S(1)} %copy-done, f32[2,32,128]{2,1,0:T(8,128)S(1)} %get-tuple-element.19.sides, f32[104,128]{1,0:T(8,128)S(1)} %collective-permute-done.2.from_yminus, ...), custom_call_target="tpu_custom_call" | custom-call | tf_op jit(solution)/shard_map/pallas_call | solution.py:625
  23.3 6.7 %collective-permute-start.4 = (bf16[1072,128]{1,0:T(8,128)(2,1)S(1)}, bf16[1072,128]{1,0:T(8,128)(2,1)S(1)}, u32[]{:S(2)}, u32[]{:S(2)}) collective-permute-start(bf16[1072,128]{1,0:T(8,128)(2,1)S(1)} %get-tuple-element.23), channel_id=1, source_target_pairs={{0,32},{32,64},{64,96},{96,128},{128,160},{160,192},{192,224},{224... | collective-permute-start | bytes 823304 | tf_op jit(solution)/shard_map/ppermute | solution.py:641
  30.0 0.0 collective-permute-start.5
  30.0 0.0 copy-done.6
  30.0 0.0 copy-done.7
  30.0 0.0 copy-done.4
  30.0 0.0 copy-done.9
  30.0 0.0 copy-done.5
  30.1 0.0 copy-done.3
  30.1 0.6 %shard_map.108 = (bf16[512,8]{1,0:T(8,128)(2,1)S(1)}, bf16[512,512]{1,0:T(8,128)(2,1)S(1)}, f32[512,128]{1,0:T(8,128)S(1)}, bf16[15,512]{1,0:T(8,128)(2,1)S(1)}, f32[16,128]{1,0:T(8,128)S(1)}) custom-call(bf16[6,512]{1,0:T(8,128)(2,1)S(1)} %copy-done.5, f32[1,512]{1,0:T(1,128)S(1)} %bitcast.8, bf16[512,512]{1,0:T(8,128)(2,1)S(1)} %copy-done.3, ...), custom_call_target="tpu_custom_call" | custom-call | tf_op jit(solution)/shard_map/pallas_call | solution.py:575
  30.7 2.8 %collective-permute-done.4.from_low = bf16[1072,128]{1,0:T(8,128)(2,1)S(1)} collective-permute-done((bf16[1072,128]{1,0:T(8,128)(2,1)S(1)}, bf16[1072,128]{1,0:T(8,128)(2,1)S(1)}, u32[]{:S(2)}, u32[]{:S(2)}) %collective-permute-start.4) | collective-permute-done | bytes 274464 | tf_op jit(solution)/shard_map/ppermute | solution.py:641
  33.5 3.7 %collective-permute-done.5.from_high = bf16[1072,128]{1,0:T(8,128)(2,1)S(1)} collective-permute-done((bf16[1072,128]{1,0:T(8,128)(2,1)S(1)}, bf16[1072,128]{1,0:T(8,128)(2,1)S(1)}, u32[]{:S(2)}, u32[]{:S(2)}) %collective-permute-start.5) | collective-permute-done | bytes 274464 | tf_op jit(solution)/shard_map/ppermute | solution.py:642
  37.1 0.0 copy-done.8
  37.2 5.1 %shard_map.109 = (bf16[4,2,32,128]{3,2,1,0:T(8,128)(2,1)}, bf16[15,2,32,128]{3,2,1,0:T(8,128)(2,1)}) custom-call(s32[2,1,32]{2,1,0:T(1,128)S(1)} %bitcast.10, f32[2,38,2,40,128]{4,3,2,1,0:T(8,128)S(1)} %get-tuple-element.22.state, bf16[1072,128]{1,0:T(8,128)(2,1)S(1)} %collective-permute-done.4.from_low, ...), custom_call_target="tpu_custom_call" | custom-call | tf_op jit(solution)/shard_map/pallas_call | solution.py:643
  (1 shorter events, 0.0 us)
Async XLA Ops:
  0.6 29.4 %copy-start.6 = (f32[512]{0:T(512)S(1)}, f32[512]{0:T(512)}, u32[]{:S(2)}) copy-start(f32[512]{0:T(512)} %param.13) | copy-start | bytes 6148
  0.6 29.4 %copy-start.7 = (f32[512]{0:T(512)S(1)}, f32[512]{0:T(512)}, u32[]{:S(2)}) copy-start(f32[512]{0:T(512)} %param.15) | copy-start | bytes 6148
  0.7 29.4 %copy-start.4 = (bf16[512,15]{0,1:T(8,128)(2,1)S(1)}, bf16[512,15]{0,1:T(8,128)(2,1)}, u32[]{:S(2)}) copy-start(bf16[512,15]{0,1:T(8,128)(2,1)} %param.16) | copy-start | bytes 46084
  0.7 29.4 %copy-start.9 = (f32[15]{0:T(128)S(1)}, f32[15]{0:T(128)}, u32[]{:S(2)}) copy-start(f32[15]{0:T(128)} %param.17) | copy-start | bytes 184
  0.7 29.4 %copy-start.5 = (bf16[6,512]{1,0:T(8,128)(2,1)S(1)}, bf16[6,512]{1,0:T(8,128)(2,1)}, u32[]{:S(2)}) copy-start(bf16[6,512]{1,0:T(8,128)(2,1)} %w_in_hbm.1) | copy-start | bytes 18436
  0.7 29.4 %copy-start.3 = (bf16[512,512]{1,0:T(8,128)(2,1)S(1)}, bf16[512,512]{1,0:T(8,128)(2,1)}, u32[]{:S(2)}) copy-start(bf16[512,512]{1,0:T(8,128)(2,1)} %w_mid_hbm.1) | copy-start | bytes 1572868
  0.7 36.5 %copy-start.8 = (s32[2,32,1]{1,2,0:T(1,128)S(1)}, s32[2,32,1]{1,2,0:T(1,128)}, u32[]{:S(2)}) copy-start(s32[2,32,1]{1,2,0:T(1,128)} %param.11) | copy-start | bytes 772
  2.2 5.3 %collective-permute-start = (f32[2,32,128]{2,1,0:T(8,128)S(1)}, f32[2,32,128]{2,1,0:T(8,128)S(1)}, u32[]{:S(2)}, u32[]{:S(2)}) collective-permute-start(f32[2,32,128]{2,1,0:T(8,128)S(1)} %get-tuple-element.16.after), channel_id=1, source_target_pairs={{0,1},{1,2},{2,3},{4,5},{5,6},{6,7},{8,9},{9,10},{10,11},{12,13},{... | collective-permute-start | bytes 98312 | tf_op jit(solution)/shard_map/ppermute | solution.py:614
  5.3 4.7 %collective-permute-start.1 = (f32[2,32,128]{2,1,0:T(8,128)S(1)}, f32[2,32,128]{2,1,0:T(8,128)S(1)}, u32[]{:S(2)}, u32[]{:S(2)}) collective-permute-start(f32[2,32,128]{2,1,0:T(8,128)S(1)} %get-tuple-element.16.after), channel_id=1, source_target_pairs={{1,0},{2,1},{3,2},{5,4},{6,5},{7,6},{9,8},{10,9},{11,10},{13,12},{... | collective-permute-start | bytes 98312 | tf_op jit(solution)/shard_map/ppermute | solution.py:615
  10.0 10.0 %collective-permute-start.2 = (f32[104,128]{1,0:T(8,128)S(1)}, f32[104,128]{1,0:T(8,128)S(1)}, u32[]{:S(2)}, u32[]{:S(2)}) collective-permute-start(f32[104,128]{1,0:T(8,128)S(1)} %get-tuple-element.20), channel_id=1, source_target_pairs={{0,4},{4,8},{8,12},{12,16},{16,20},{20,24},{24,28},{28,0},{1,5},{5... | collective-permute-start | bytes 159752 | tf_op jit(solution)/shard_map/ppermute | solution.py:623
  14.5 6.1 %collective-permute-start.3 = (f32[104,128]{1,0:T(8,128)S(1)}, f32[104,128]{1,0:T(8,128)S(1)}, u32[]{:S(2)}, u32[]{:S(2)}) collective-permute-start(f32[104,128]{1,0:T(8,128)S(1)} %get-tuple-element.21), channel_id=1, source_target_pairs={{0,28},{4,0},{8,4},{12,8},{16,12},{20,16},{24,20},{28,24},{1,29},{... | collective-permute-start | bytes 159752 | tf_op jit(solution)/shard_map/ppermute | solution.py:624
  16.4 1.1 %copy-start.1 = (f32[19,2,32,128]{3,2,1,0:T(8,128)S(1)}, f32[19,2,32,128]{3,2,1,0:T(8,128)}, u32[]{:S(2)}) copy-start(f32[19,2,32,128]{3,2,1,0:T(8,128)} %pop_hbm.3) | copy-start | bytes 1867780
  17.5 0.9 %copy-start.2 = (f32[6,2,32,128]{3,2,1,0:T(8,128)S(1)}, f32[6,2,32,128]{3,2,1,0:T(8,128)}, u32[]{:S(2)}) copy-start(f32[6,2,32,128]{3,2,1,0:T(8,128)} %ori_hbm.3) | copy-start | bytes 589828
  20.5 1.2 %copy-start = (f32[28,2,32,128]{3,2,1,0:T(8,128)S(1)}, f32[28,2,32,128]{3,2,1,0:T(8,128)}, u32[]{:S(2)}) copy-start(f32[28,2,32,128]{3,2,1,0:T(8,128)} %shard_map.105.own) | copy-start | bytes 2752516
  23.3 10.2 %collective-permute-start.4 = (bf16[1072,128]{1,0:T(8,128)(2,1)S(1)}, bf16[1072,128]{1,0:T(8,128)(2,1)S(1)}, u32[]{:S(2)}, u32[]{:S(2)}) collective-permute-start(bf16[1072,128]{1,0:T(8,128)(2,1)S(1)} %get-tuple-element.23), channel_id=1, source_target_pairs={{0,32},{32,64},{64,96},{96,128},{128,160},{160,192},{192,224},{224... | collective-permute-start | bytes 823304 | tf_op jit(solution)/shard_map/ppermute | solution.py:641
  30.0 7.1 %collective-permute-start.5 = (bf16[1072,128]{1,0:T(8,128)(2,1)S(1)}, bf16[1072,128]{1,0:T(8,128)(2,1)S(1)}, u32[]{:S(2)}, u32[]{:S(2)}) collective-permute-start(bf16[1072,128]{1,0:T(8,128)(2,1)S(1)} %get-tuple-element.24), channel_id=1, source_target_pairs={{0,480},{32,0},{64,32},{96,64},{128,96},{160,128},{192,160},{224,1... | collective-permute-start | bytes 823304 | tf_op jit(solution)/shard_map/ppermute | solution.py:642

commit v3 on v2

--- a/solution.py
+++ b/solution.py
@@ -47,7 +47,7 @@
 CORNER_AT = 1056
 MIB = 1024 * 1024
 LIMIT_PACK = 5375 * MIB // 100
-LIMIT_OWN = 5270 * MIB // 100
+COST_PACK = pl.CostEstimate(flops=10**10, bytes_accessed=10**7, transcendentals=0)
 LIMIT_WEIGHTS = 4900 * MIB // 100
 STATE = 38
 
@@ -254,10 +254,8 @@
     high_rows[100:104, :] = jnp.zeros((4, 128), jnp.float32)
 
 
-def own_kernel(pop_hbm, ori_hbm, after, own, pop, ori, sems):
-    del after
-    for copy in fetch([(pop_hbm, pop), (ori_hbm, ori)], sems):
-        copy.wait()
+def own_kernel(pop, ori, after, own, token):
+    token[...] = jnp.zeros(token.shape, jnp.float32)
     numbers = list(range(19))
     for x in range(2):
         for r in range(4):
@@ -275,7 +273,7 @@
                 own[22 + k, x, rows, :] = ori[k, x, rows, :]
 
 
-def pack_y_kernel(from_minus, from_plus, low_in, high_in, sides, low_rows, high_rows):
+def pack_y_kernel(from_minus, from_plus, low_in, high_in, token, sides, low_rows, high_rows):
     lane = lax.broadcasted_iota(jnp.int32, (32, 128), 1)
     low_rows[...] = low_in[...]
     high_rows[...] = high_in[...]
@@ -594,32 +592,35 @@
         ],
         compiler_params=pltpu.CompilerParams(vmem_limit_bytes=LIMIT_WEIGHTS),
     )(w_in, b_in.reshape(1, 512), w_mid, b_mid.reshape(1, 512), w_out.T, b_out.reshape(1, 15))
-    raw_scratch = [pltpu.VMEM((19, 2, 32, 128), f32), pltpu.VMEM((6, 2, 32, 128), f32), pltpu.SemaphoreType.DMA((2,))]
     zpack, low_raw, high_raw = pl.pallas_call(
         pack_z_kernel,
         out_shape=(shape(2, 32, 128), shape(104, 128), shape(104, 128)),
         in_specs=[hbm] * 2,
         out_specs=(vmem,) * 3,
-        scratch_shapes=raw_scratch,
+        scratch_shapes=[
+            pltpu.VMEM((19, 2, 32, 128), f32),
+            pltpu.VMEM((6, 2, 32, 128), f32),
+            pltpu.SemaphoreType.DMA((2,)),
+        ],
         compiler_params=pltpu.CompilerParams(vmem_limit_bytes=LIMIT_PACK),
+        cost_estimate=COST_PACK,
     )(populations, orientation)
-    own = pl.pallas_call(
+    own, token = pl.pallas_call(
         own_kernel,
-        out_shape=shape(28, 2, 32, 128),
-        in_specs=[hbm] * 3,
-        out_specs=vmem,
-        scratch_shapes=raw_scratch,
-        compiler_params=pltpu.CompilerParams(vmem_limit_bytes=LIMIT_OWN),
+        out_shape=(shape(28, 2, 32, 128), shape(8, 128)),
+        in_specs=[vmem] * 3,
+        out_specs=(vmem,) * 2,
+        compiler_params=params,
     )(populations, orientation, zpack)
     from_minus = lax.ppermute(zpack, "gz", ring("gz", 1, False))
     from_plus = lax.ppermute(zpack, "gz", ring("gz", -1, False))
     sides, low_rows, high_rows = pl.pallas_call(
         pack_y_kernel,
         out_shape=(shape(2, 32, 128), shape(104, 128), shape(104, 128)),
-        in_specs=[vmem] * 4,
+        in_specs=[vmem] * 5,
         out_specs=(vmem,) * 3,
         compiler_params=params,
-    )(from_minus, from_plus, low_raw, high_raw)
+    )(from_minus, from_plus, low_raw, high_raw, token)
     from_yminus = lax.ppermute(high_rows, "gy", ring("gy", 1, True))
     from_yplus = lax.ppermute(low_rows, "gy", ring("gy", -1, True))
     state, msg_low, msg_high = pl.pallas_call(

time: 42.6 us -> 41.3 us (0.969)
  waiting for transfers between devices: 9.5 us -> 12.8 us
  local copies, waits for them, and re-layouts: 3.21 us -> 0.04 us
  Pallas kernels: 10.4 us -> 9.09 us
    ppermute x1, waiting for transfers between devices: 0.54 us -> 4.15 us  [local(): from_yplus = lax.ppermute(low_rows, 'gy', ring('gy', -1, True))]
    unnamed x20 -> x18, local copies, waits for them, and re-layouts: 3.21 us -> 0.04 us
    pallas_call x1, Pallas kernels: 1.59 us -> 0.27 us  [local(): pl.pallas_call(own_kernel, out_shape=(shape(28, 2, 32, 128), shape(8, 128...]
  transfers between devices with their start and end apart: 6 -> 6, of which waited for: 4 -> 4; matrix products, arithmetic and copies ran while one was open for 0% -> 0% of each run, Pallas kernels for 5% -> 2%
where the time goes in v3:
time: 41.3 us; the launch traced here: 41.1 us
  starting transfers between devices  18.4 us (45%)
  waiting for transfers between devices  12.8 us (31%)
  Pallas kernels  9.09 us (22%)
  between operations  0.83 us (2%)
    ppermute x1, starting transfers between devices, local(): from_low = lax.ppermute(msg_high, 'gx', ring('gx', 1, True))  6.73 us
    pallas_call x1, Pallas kernels, local(): pl.pallas_call(step_two_kernel, out_shape=(shape(4, 2, 32, 128, d=bf16),...  5.08 us
    ppermute x1, starting transfers between devices, local(): from_yminus = lax.ppermute(high_rows, 'gy', ring('gy', 1, True))  4.42 us
    ppermute x1, waiting for transfers between devices, local(): from_yplus = lax.ppermute(low_rows, 'gy', ring('gy', -1, True))  4.15 us
    ppermute x1, waiting for transfers between devices, local(): from_high = lax.ppermute(msg_low, 'gx', ring('gx', -1, True))  3.69 us
    ppermute x1, starting transfers between devices, local(): from_minus = lax.ppermute(zpack, 'gz', ring('gz', 1, False))  3.12 us
    ppermute x1, waiting for transfers between devices, local(): from_low = lax.ppermute(msg_high, 'gx', ring('gx', 1, True))  2.79 us
    ppermute x1, waiting for transfers between devices, local(): from_plus = lax.ppermute(zpack, 'gz', ring('gz', -1, False))  2.19 us
  transfers between devices with their start and end apart: 6, of which 4 were waited for; matrix products, arithmetic and copies ran while one was open for 0% of the time, Pallas kernels for 2%

profile of v3, /device:TPU:219, one launch (start us, length us, event | category | flops | bytes accessed | tf_op | source)
XLA Modules:
  0.0 41.1 jit_solution(433865218057175716)
XLA Ops:
  0.6 0.0 copy-start.2
  0.6 0.0 copy-start
  0.7 0.0 copy-start.5
  0.7 0.0 copy-start.6
  0.7 0.0 copy-start.3
  0.7 0.0 copy-start.8
  0.7 0.0 copy-start.4
  0.7 0.0 copy-start.1
  0.7 0.0 copy-start.7
  0.7 1.5 %shard_map.104 = (f32[2,32,128]{2,1,0:T(8,128)S(1)}, f32[104,128]{1,0:T(8,128)S(1)}, f32[104,128]{1,0:T(8,128)S(1)}) custom-call(f32[19,2,32,128]{3,2,1,0:T(8,128)} %pop.1, f32[6,2,32,128]{3,2,1,0:T(8,128)} %ori.1), custom_call_target="tpu_custom_call" | custom-call | flops 10000000000 | bytes 10000000 | tf_op jit(solution)/shard_map/pallas_call | solution.py:595
  2.3 3.1 %collective-permute-start = (f32[2,32,128]{2,1,0:T(8,128)S(1)}, f32[2,32,128]{2,1,0:T(8,128)S(1)}, u32[]{:S(2)}, u32[]{:S(2)}) collective-permute-start(f32[2,32,128]{2,1,0:T(8,128)S(1)} %get-tuple-element.18.after), channel_id=1, source_target_pairs={{0,1},{1,2},{2,3},{4,5},{5,6},{6,7},{8,9},{9,10},{10,11},{12,13},{... | collective-permute-start | bytes 98312 | tf_op jit(solution)/shard_map/ppermute | solution.py:615
  5.4 2.2 %collective-permute-start.1 = (f32[2,32,128]{2,1,0:T(8,128)S(1)}, f32[2,32,128]{2,1,0:T(8,128)S(1)}, u32[]{:S(2)}, u32[]{:S(2)}) collective-permute-start(f32[2,32,128]{2,1,0:T(8,128)S(1)} %get-tuple-element.18.after), channel_id=1, source_target_pairs={{1,0},{2,1},{3,2},{5,4},{6,5},{7,6},{9,8},{10,9},{11,10},{13,12},{... | collective-permute-start | bytes 98312 | tf_op jit(solution)/shard_map/ppermute | solution.py:616
  7.6 0.0 copy-done.2
  7.6 0.0 copy-done
  7.6 0.3 shard_map.105
  7.9 0.0 collective-permute-done.from_minus
  7.9 2.2 %collective-permute-done.1.from_plus = f32[2,32,128]{2,1,0:T(8,128)S(1)} collective-permute-done((f32[2,32,128]{2,1,0:T(8,128)S(1)}, f32[2,32,128]{2,1,0:T(8,128)S(1)}, u32[]{:S(2)}, u32[]{:S(2)}) %collective-permute-start.1) | collective-permute-done | bytes 32800 | tf_op jit(solution)/shard_map/ppermute | solution.py:616
  10.1 4.4 %collective-permute-start.2 = (f32[104,128]{1,0:T(8,128)S(1)}, f32[104,128]{1,0:T(8,128)S(1)}, u32[]{:S(2)}, u32[]{:S(2)}) collective-permute-start(f32[104,128]{1,0:T(8,128)S(1)} %get-tuple-element.24), channel_id=1, source_target_pairs={{0,4},{4,8},{8,12},{12,16},{16,20},{20,24},{24,28},{28,0},{1,5},{5... | collective-permute-start | bytes 159752 | tf_op jit(solution)/shard_map/ppermute | solution.py:624
  14.5 1.9 %collective-permute-start.3 = (f32[104,128]{1,0:T(8,128)S(1)}, f32[104,128]{1,0:T(8,128)S(1)}, u32[]{:S(2)}, u32[]{:S(2)}) collective-permute-start(f32[104,128]{1,0:T(8,128)S(1)} %get-tuple-element.25), channel_id=1, source_target_pairs={{0,28},{4,0},{8,4},{12,8},{16,12},{20,16},{24,20},{28,24},{1,29},{... | collective-permute-start | bytes 159752 | tf_op jit(solution)/shard_map/ppermute | solution.py:625
  16.4 0.0 collective-permute-done.2.from_yminus
  16.4 4.2 %collective-permute-done.3.from_yplus = f32[104,128]{1,0:T(8,128)S(1)} collective-permute-done((f32[104,128]{1,0:T(8,128)S(1)}, f32[104,128]{1,0:T(8,128)S(1)}, u32[]{:S(2)}, u32[]{:S(2)}) %collective-permute-start.3) | collective-permute-done | bytes 53280 | tf_op jit(solution)/shard_map/ppermute | solution.py:625
  20.6 1.6 %shard_map.107 = (f32[2,38,2,40,128]{4,3,2,1,0:T(8,128)S(1)}, bf16[1072,128]{1,0:T(8,128)(2,1)S(1)}, bf16[1072,128]{1,0:T(8,128)(2,1)S(1)}) custom-call(f32[28,2,32,128]{3,2,1,0:T(8,128)S(1)} %get-tuple-element.19.own, f32[2,32,128]{2,1,0:T(8,128)S(1)} %get-tuple-element.23.sides, f32[104,128]{1,0:T(8,128)S(1)} %collective-permute-done.2.from_yminus, ...), custom_call_target="tpu_custom_call" | custom-call | tf_op jit(solution)/shard_map/pallas_call | solution.py:626
  22.2 6.7 %collective-permute-start.4 = (bf16[1072,128]{1,0:T(8,128)(2,1)S(1)}, bf16[1072,128]{1,0:T(8,128)(2,1)S(1)}, u32[]{:S(2)}, u32[]{:S(2)}) collective-permute-start(bf16[1072,128]{1,0:T(8,128)(2,1)S(1)} %get-tuple-element.27), channel_id=1, source_target_pairs={{0,32},{32,64},{64,96},{96,128},{128,160},{160,192},{192,224},{224... | collective-permute-start | bytes 823304 | tf_op jit(solution)/shard_map/ppermute | solution.py:642
  28.9 0.0 collective-permute-start.5
  28.9 0.0 copy-done.5
  28.9 0.0 copy-done.6
  28.9 0.0 copy-done.3
  28.9 0.0 copy-done.8
  28.9 0.0 copy-done.4
  28.9 0.0 copy-done.1
  29.0 0.6 %shard_map.108 = (bf16[512,8]{1,0:T(8,128)(2,1)S(1)}, bf16[512,512]{1,0:T(8,128)(2,1)S(1)}, f32[512,128]{1,0:T(8,128)S(1)}, bf16[15,512]{1,0:T(8,128)(2,1)S(1)}, f32[16,128]{1,0:T(8,128)S(1)}) custom-call(bf16[6,512]{1,0:T(8,128)(2,1)S(1)} %copy-done.4, f32[1,512]{1,0:T(1,128)S(1)} %bitcast.8, bf16[512,512]{1,0:T(8,128)(2,1)S(1)} %copy-done.1, ...), custom_call_target="tpu_custom_call" | custom-call | tf_op jit(solution)/shard_map/pallas_call | solution.py:573
  29.6 2.8 %collective-permute-done.4.from_low = bf16[1072,128]{1,0:T(8,128)(2,1)S(1)} collective-permute-done((bf16[1072,128]{1,0:T(8,128)(2,1)S(1)}, bf16[1072,128]{1,0:T(8,128)(2,1)S(1)}, u32[]{:S(2)}, u32[]{:S(2)}) %collective-permute-start.4) | collective-permute-done | bytes 274464 | tf_op jit(solution)/shard_map/ppermute | solution.py:642
  32.4 3.7 %collective-permute-done.5.from_high = bf16[1072,128]{1,0:T(8,128)(2,1)S(1)} collective-permute-done((bf16[1072,128]{1,0:T(8,128)(2,1)S(1)}, bf16[1072,128]{1,0:T(8,128)(2,1)S(1)}, u32[]{:S(2)}, u32[]{:S(2)}) %collective-permute-start.5) | collective-permute-done | bytes 274464 | tf_op jit(solution)/shard_map/ppermute | solution.py:643
  36.0 0.0 copy-done.7
  36.1 5.1 %shard_map.109 = (bf16[4,2,32,128]{3,2,1,0:T(8,128)(2,1)}, bf16[15,2,32,128]{3,2,1,0:T(8,128)(2,1)}) custom-call(s32[2,1,32]{2,1,0:T(1,128)S(1)} %bitcast.10, f32[2,38,2,40,128]{4,3,2,1,0:T(8,128)S(1)} %get-tuple-element.26.state, bf16[1072,128]{1,0:T(8,128)(2,1)S(1)} %collective-permute-done.4.from_low, ...), custom_call_target="tpu_custom_call" | custom-call | tf_op jit(solution)/shard_map/pallas_call | solution.py:644
  (1 shorter events, 0.0 us)
Async XLA Ops:
  0.6 6.9 %copy-start.2 = (f32[6,2,32,128]{3,2,1,0:T(8,128)S(1)}, f32[6,2,32,128]{3,2,1,0:T(8,128)}, u32[]{:S(2)}) copy-start(f32[6,2,32,128]{3,2,1,0:T(8,128)} %ori.1) | copy-start | bytes 589828
  0.6 6.9 %copy-start = (f32[19,2,32,128]{3,2,1,0:T(8,128)S(1)}, f32[19,2,32,128]{3,2,1,0:T(8,128)}, u32[]{:S(2)}) copy-start(f32[19,2,32,128]{3,2,1,0:T(8,128)} %pop.1) | copy-start | bytes 1867780
  0.7 28.3 %copy-start.5 = (f32[512]{0:T(512)S(1)}, f32[512]{0:T(512)}, u32[]{:S(2)}) copy-start(f32[512]{0:T(512)} %param.13) | copy-start | bytes 6148
  0.7 28.3 %copy-start.6 = (f32[512]{0:T(512)S(1)}, f32[512]{0:T(512)}, u32[]{:S(2)}) copy-start(f32[512]{0:T(512)} %param.15) | copy-start | bytes 6148
  0.7 28.2 %copy-start.3 = (bf16[512,15]{0,1:T(8,128)(2,1)S(1)}, bf16[512,15]{0,1:T(8,128)(2,1)}, u32[]{:S(2)}) copy-start(bf16[512,15]{0,1:T(8,128)(2,1)} %param.16) | copy-start | bytes 46084
  0.7 28.2 %copy-start.8 = (f32[15]{0:T(128)S(1)}, f32[15]{0:T(128)}, u32[]{:S(2)}) copy-start(f32[15]{0:T(128)} %param.17) | copy-start | bytes 184
  0.7 28.2 %copy-start.4 = (bf16[6,512]{1,0:T(8,128)(2,1)S(1)}, bf16[6,512]{1,0:T(8,128)(2,1)}, u32[]{:S(2)}) copy-start(bf16[6,512]{1,0:T(8,128)(2,1)} %w_in_hbm.1) | copy-start | bytes 18436
  0.7 28.2 %copy-start.1 = (bf16[512,512]{1,0:T(8,128)(2,1)S(1)}, bf16[512,512]{1,0:T(8,128)(2,1)}, u32[]{:S(2)}) copy-start(bf16[512,512]{1,0:T(8,128)(2,1)} %w_mid_hbm.1) | copy-start | bytes 1572868
  0.7 35.3 %copy-start.7 = (s32[2,32,1]{1,2,0:T(1,128)S(1)}, s32[2,32,1]{1,2,0:T(1,128)}, u32[]{:S(2)}) copy-start(s32[2,32,1]{1,2,0:T(1,128)} %param.11) | copy-start | bytes 772
  2.3 5.6 %collective-permute-start = (f32[2,32,128]{2,1,0:T(8,128)S(1)}, f32[2,32,128]{2,1,0:T(8,128)S(1)}, u32[]{:S(2)}, u32[]{:S(2)}) collective-permute-start(f32[2,32,128]{2,1,0:T(8,128)S(1)} %get-tuple-element.18.after), channel_id=1, source_target_pairs={{0,1},{1,2},{2,3},{4,5},{5,6},{6,7},{8,9},{9,10},{10,11},{12,13},{... | collective-permute-start | bytes 98312 | tf_op jit(solution)/shard_map/ppermute | solution.py:615
  5.4 4.7 %collective-permute-start.1 = (f32[2,32,128]{2,1,0:T(8,128)S(1)}, f32[2,32,128]{2,1,0:T(8,128)S(1)}, u32[]{:S(2)}, u32[]{:S(2)}) collective-permute-start(f32[2,32,128]{2,1,0:T(8,128)S(1)} %get-tuple-element.18.after), channel_id=1, source_target_pairs={{1,0},{2,1},{3,2},{5,4},{6,5},{7,6},{9,8},{10,9},{11,10},{13,12},{... | collective-permute-start | bytes 98312 | tf_op jit(solution)/shard_map/ppermute | solution.py:616
  10.1 6.4 %collective-permute-start.2 = (f32[104,128]{1,0:T(8,128)S(1)}, f32[104,128]{1,0:T(8,128)S(1)}, u32[]{:S(2)}, u32[]{:S(2)}) collective-permute-start(f32[104,128]{1,0:T(8,128)S(1)} %get-tuple-element.24), channel_id=1, source_target_pairs={{0,4},{4,8},{8,12},{12,16},{16,20},{20,24},{24,28},{28,0},{1,5},{5... | collective-permute-start | bytes 159752 | tf_op jit(solution)/shard_map/ppermute | solution.py:624
  14.5 6.1 %collective-permute-start.3 = (f32[104,128]{1,0:T(8,128)S(1)}, f32[104,128]{1,0:T(8,128)S(1)}, u32[]{:S(2)}, u32[]{:S(2)}) collective-permute-start(f32[104,128]{1,0:T(8,128)S(1)} %get-tuple-element.25), channel_id=1, source_target_pairs={{0,28},{4,0},{8,4},{12,8},{16,12},{20,16},{24,20},{28,24},{1,29},{... | collective-permute-start | bytes 159752 | tf_op jit(solution)/shard_map/ppermute | solution.py:625
  22.2 10.2 %collective-permute-start.4 = (bf16[1072,128]{1,0:T(8,128)(2,1)S(1)}, bf16[1072,128]{1,0:T(8,128)(2,1)S(1)}, u32[]{:S(2)}, u32[]{:S(2)}) collective-permute-start(bf16[1072,128]{1,0:T(8,128)(2,1)S(1)} %get-tuple-element.27), channel_id=1, source_target_pairs={{0,32},{32,64},{64,96},{96,128},{128,160},{160,192},{192,224},{224... | collective-permute-start | bytes 823304 | tf_op jit(solution)/shard_map/ppermute | solution.py:642
  28.9 7.1 %collective-permute-start.5 = (bf16[1072,128]{1,0:T(8,128)(2,1)S(1)}, bf16[1072,128]{1,0:T(8,128)(2,1)S(1)}, u32[]{:S(2)}, u32[]{:S(2)}) collective-permute-start(bf16[1072,128]{1,0:T(8,128)(2,1)S(1)} %get-tuple-element.28), channel_id=1, source_target_pairs={{0,480},{32,0},{64,32},{96,64},{128,96},{160,128},{192,160},{224,1... | collective-permute-start | bytes 823304 | tf_op jit(solution)/shard_map/ppermute | solution.py:643

commit v4 on v3

--- a/solution.py
+++ b/solution.py
@@ -284,7 +284,7 @@
         high_rows[pl.ds(100 + 2 * t, 2), :] = sides[t, 30:32, :]
 
 
-def step_one_kernel(own, sides, from_yminus, from_yplus, state, msg_low, msg_high, halo, fields, out):
+def step_one_kernel(own, sides, from_yminus, from_yplus, state, msg_off, msg_on, halo, fields, out):
     low, high = walls()
     lane, row = lanes_of(), rows_of()
     for s in range(52):
@@ -373,8 +373,9 @@
             out[x, pl.ds(SIDE_AT + 8 * r if r < 4 else CORNER_AT, 8), :] = side_pack
     for x in range(2):
         out[x, pl.ds(CORNER_AT + 8, 8), :] = jnp.zeros((8, 128), jnp.float32)
-    msg_low[...] = out[0].astype(jnp.bfloat16)
-    msg_high[...] = out[1].astype(jnp.bfloat16)
+    odd = lax.axis_index("gx") % 2
+    msg_off[...] = out[odd].astype(jnp.bfloat16)
+    msg_on[...] = out[1 - odd].astype(jnp.bfloat16)
 
 
 def weights_kernel(
@@ -407,12 +408,13 @@
 
 
 def step_two_kernel(
-    slots, state, from_low, from_high, w_one, w_mid, b_mid, w_out, b_out, flow, closure,
+    slots, state, from_off, from_on, w_one, w_mid, b_mid, w_out, b_out, flow, closure,
     got, fields, near, level, feats, spread, place,
 ):
     low, high = walls()
-    got[0] = from_low[...].astype(jnp.float32)
-    got[1] = from_high[...].astype(jnp.float32)
+    odd = lax.axis_index("gx") % 2
+    got[odd] = from_off[...].astype(jnp.float32)
+    got[1 - odd] = from_on[...].astype(jnp.float32)
     for s in range(17):
         place[s] = 64
     for b in range(64):
@@ -623,7 +625,7 @@
     )(from_minus, from_plus, low_raw, high_raw, token)
     from_yminus = lax.ppermute(high_rows, "gy", ring("gy", 1, True))
     from_yplus = lax.ppermute(low_rows, "gy", ring("gy", -1, True))
-    state, msg_low, msg_high = pl.pallas_call(
+    state, msg_off, msg_on = pl.pallas_call(
         step_one_kernel,
         out_shape=(
             shape(2, STATE, 2, 40, 128),
@@ -639,8 +641,11 @@
         ],
         compiler_params=params,
     )(own, sides, from_yminus, from_yplus)
-    from_low = lax.ppermute(msg_high, "gx", ring("gx", 1, True))
-    from_high = lax.ppermute(msg_low, "gx", ring("gx", -1, True))
+    x_count = lax.axis_size("gx")
+    off_chip = [(i, (i + (1 if i % 2 else -1)) % x_count) for i in range(x_count)]
+    on_chip = [(i, i + (-1 if i % 2 else 1)) for i in range(x_count)]
+    from_off = lax.ppermute(msg_off, "gx", off_chip)
+    from_on = lax.ppermute(msg_on, "gx", on_chip)
     return pl.pallas_call(
         step_two_kernel,
         out_shape=(shape(4, 2, 32, 128, d=bf16), shape(15, 2, 32, 128, d=bf16)),
@@ -656,7 +661,7 @@
             pltpu.SMEM((17,), jnp.int32),
         ],
         compiler_params=params,
-    )(slots, state, from_low, from_high, w_one, w_two, bias_mid, w_three, bias_out)
+    )(slots, state, from_off, from_on, w_one, w_two, bias_mid, w_three, bias_out)
 
 
 def solution(mesh):

time: 41.3 us -> 42.4 us (1.027)
  the two profiles are of different devices: /device:TPU:219 before, /device:TPU:24 now
where the time goes in v4:
time: 42.4 us; the launch traced here: 42.1 us
  starting transfers between devices  20.7 us (49%)
  waiting for transfers between devices  11.1 us (26%)
  Pallas kernels  9.39 us (22%)
  between operations  0.86 us (2%)
    ppermute x1, starting transfers between devices, local(): from_off = lax.ppermute(msg_off, 'gx', off_chip)  7.52 us
    ppermute x1, waiting for transfers between devices, local(): from_yplus = lax.ppermute(low_rows, 'gy', ring('gy', -1, True))  5.3 us
    pallas_call x1, Pallas kernels, local(): pl.pallas_call(step_two_kernel, out_shape=(shape(4, 2, 32, 128, d=bf16),...  5.27 us
    ppermute x1, starting transfers between devices, local(): from_yminus = lax.ppermute(high_rows, 'gy', ring('gy', 1, True))  4.7 us
    ppermute x1, waiting for transfers between devices, local(): from_plus = lax.ppermute(zpack, 'gz', ring('gz', -1, False))  4.2 us
    ppermute x1, starting transfers between devices, local(): from_minus = lax.ppermute(zpack, 'gz', ring('gz', 1, False))  3.4 us
    ppermute x1, starting transfers between devices, local(): from_on = lax.ppermute(msg_on, 'gx', on_chip)  1.92 us
    ppermute x1, starting transfers between devices, local(): from_yplus = lax.ppermute(low_rows, 'gy', ring('gy', -1, True))  1.92 us
  transfers between devices with their start and end apart: 6, of which 3 were waited for; matrix products, arithmetic and copies ran while one was open for 0% of the time, Pallas kernels for 2%

profile of v4, /device:TPU:24, one launch (start us, length us, event | category | flops | bytes accessed | tf_op | source)
XLA Modules:
  0.0 42.1 jit_solution(5581209693435202781)
XLA Ops:
  0.6 0.0 copy-start.2
  0.6 0.0 copy-start
  0.7 0.0 copy-start.5
  0.7 0.0 copy-start.6
  0.7 0.0 copy-start.3
  0.7 0.0 copy-start.8
  0.7 0.0 copy-start.4
  0.7 0.0 copy-start.1
  0.7 0.0 copy-start.7
  0.7 1.5 %shard_map.104 = (f32[2,32,128]{2,1,0:T(8,128)S(1)}, f32[104,128]{1,0:T(8,128)S(1)}, f32[104,128]{1,0:T(8,128)S(1)}) custom-call(f32[19,2,32,128]{3,2,1,0:T(8,128)} %pop.1, f32[6,2,32,128]{3,2,1,0:T(8,128)} %ori.1), custom_call_target="tpu_custom_call" | custom-call | flops 10000000000 | bytes 10000000 | tf_op jit(solution)/shard_map/pallas_call | solution.py:597
  2.3 3.4 %collective-permute-start = (f32[2,32,128]{2,1,0:T(8,128)S(1)}, f32[2,32,128]{2,1,0:T(8,128)S(1)}, u32[]{:S(2)}, u32[]{:S(2)}) collective-permute-start(f32[2,32,128]{2,1,0:T(8,128)S(1)} %get-tuple-element.18.after), channel_id=1, source_target_pairs={{0,1},{1,2},{2,3},{4,5},{5,6},{6,7},{8,9},{9,10},{10,11},{12,13},{... | collective-permute-start | bytes 98312 | tf_op jit(solution)/shard_map/ppermute | solution.py:617
  5.7 1.3 %collective-permute-start.1 = (f32[2,32,128]{2,1,0:T(8,128)S(1)}, f32[2,32,128]{2,1,0:T(8,128)S(1)}, u32[]{:S(2)}, u32[]{:S(2)}) collective-permute-start(f32[2,32,128]{2,1,0:T(8,128)S(1)} %get-tuple-element.18.after), channel_id=1, source_target_pairs={{1,0},{2,1},{3,2},{5,4},{6,5},{7,6},{9,8},{10,9},{11,10},{13,12},{... | collective-permute-start | bytes 98312 | tf_op jit(solution)/shard_map/ppermute | solution.py:618
  7.0 0.0 copy-done.2
  7.0 0.0 copy-done
  7.0 0.3 shard_map.105
  7.3 0.0 collective-permute-done.from_minus
  7.3 4.2 %collective-permute-done.1.from_plus = f32[2,32,128]{2,1,0:T(8,128)S(1)} collective-permute-done((f32[2,32,128]{2,1,0:T(8,128)S(1)}, f32[2,32,128]{2,1,0:T(8,128)S(1)}, u32[]{:S(2)}, u32[]{:S(2)}) %collective-permute-start.1) | collective-permute-done | bytes 32800 | tf_op jit(solution)/shard_map/ppermute | solution.py:618
  11.5 4.7 %collective-permute-start.2 = (f32[104,128]{1,0:T(8,128)S(1)}, f32[104,128]{1,0:T(8,128)S(1)}, u32[]{:S(2)}, u32[]{:S(2)}) collective-permute-start(f32[104,128]{1,0:T(8,128)S(1)} %get-tuple-element.24), channel_id=1, source_target_pairs={{0,4},{4,8},{8,12},{12,16},{16,20},{20,24},{24,28},{28,0},{1,5},{5... | collective-permute-start | bytes 159752 | tf_op jit(solution)/shard_map/ppermute | solution.py:626
  16.2 1.9 %collective-permute-start.3 = (f32[104,128]{1,0:T(8,128)S(1)}, f32[104,128]{1,0:T(8,128)S(1)}, u32[]{:S(2)}, u32[]{:S(2)}) collective-permute-start(f32[104,128]{1,0:T(8,128)S(1)} %get-tuple-element.25), channel_id=1, source_target_pairs={{0,28},{4,0},{8,4},{12,8},{16,12},{20,16},{24,20},{28,24},{1,29},{... | collective-permute-start | bytes 159752 | tf_op jit(solution)/shard_map/ppermute | solution.py:627
  18.1 0.0 collective-permute-done.2.from_yminus
  18.2 5.3 %collective-permute-done.3.from_yplus = f32[104,128]{1,0:T(8,128)S(1)} collective-permute-done((f32[104,128]{1,0:T(8,128)S(1)}, f32[104,128]{1,0:T(8,128)S(1)}, u32[]{:S(2)}, u32[]{:S(2)}) %collective-permute-start.3) | collective-permute-done | bytes 53280 | tf_op jit(solution)/shard_map/ppermute | solution.py:627
  23.5 1.7 %shard_map.107 = (f32[2,38,2,40,128]{4,3,2,1,0:T(8,128)S(1)}, bf16[1072,128]{1,0:T(8,128)(2,1)S(1)}, bf16[1072,128]{1,0:T(8,128)(2,1)S(1)}) custom-call(f32[28,2,32,128]{3,2,1,0:T(8,128)S(1)} %get-tuple-element.19.own, f32[2,32,128]{2,1,0:T(8,128)S(1)} %get-tuple-element.23.sides, f32[104,128]{1,0:T(8,128)S(1)} %collective-permute-done.2.from_yminus, ...), custom_call_target="tpu_custom_call" | custom-call | tf_op jit(solution)/shard_map/pallas_call | solution.py:628
  25.1 7.5 %collective-permute-start.4 = (bf16[1072,128]{1,0:T(8,128)(2,1)S(1)}, bf16[1072,128]{1,0:T(8,128)(2,1)S(1)}, u32[]{:S(2)}, u32[]{:S(2)}) collective-permute-start(bf16[1072,128]{1,0:T(8,128)(2,1)S(1)} %get-tuple-element.27), channel_id=1, source_target_pairs={{0,480},{32,64},{64,32},{96,128},{128,96},{160,192},{192,160},{224... | collective-permute-start | bytes 823304 | tf_op jit(solution)/shard_map/ppermute | solution.py:647
  32.7 1.9 %collective-permute-start.5 = (bf16[1072,128]{1,0:T(8,128)(2,1)S(1)}, bf16[1072,128]{1,0:T(8,128)(2,1)S(1)}, u32[]{:S(2)}, u32[]{:S(2)}) collective-permute-start(bf16[1072,128]{1,0:T(8,128)(2,1)S(1)} %get-tuple-element.28), channel_id=1, source_target_pairs={{0,32},{32,0},{64,96},{96,64},{128,160},{160,128},{192,224},{224,1... | collective-permute-start | bytes 823304 | tf_op jit(solution)/shard_map/ppermute | solution.py:648
  34.6 0.0 copy-done.5
  34.6 0.0 copy-done.6
  34.6 0.0 copy-done.3
  34.6 0.0 copy-done.8
  34.6 0.0 copy-done.4
  34.6 0.0 copy-done.1
  34.7 0.6 %shard_map.108 = (bf16[512,8]{1,0:T(8,128)(2,1)S(1)}, bf16[512,512]{1,0:T(8,128)(2,1)S(1)}, f32[512,128]{1,0:T(8,128)S(1)}, bf16[15,512]{1,0:T(8,128)(2,1)S(1)}, f32[16,128]{1,0:T(8,128)S(1)}) custom-call(bf16[6,512]{1,0:T(8,128)(2,1)S(1)} %copy-done.4, f32[1,512]{1,0:T(1,128)S(1)} %bitcast.8, bf16[512,512]{1,0:T(8,128)(2,1)S(1)} %copy-done.1, ...), custom_call_target="tpu_custom_call" | custom-call | tf_op jit(solution)/shard_map/pallas_call | solution.py:575
  35.3 1.6 %collective-permute-done.4.from_off = bf16[1072,128]{1,0:T(8,128)(2,1)S(1)} collective-permute-done((bf16[1072,128]{1,0:T(8,128)(2,1)S(1)}, bf16[1072,128]{1,0:T(8,128)(2,1)S(1)}, u32[]{:S(2)}, u32[]{:S(2)}) %collective-permute-start.4) | collective-permute-done | bytes 274464 | tf_op jit(solution)/shard_map/ppermute | solution.py:647
  36.8 0.0 collective-permute-done.5.from_on
  36.8 0.0 copy-done.7
  36.8 5.3 %shard_map.109 = (bf16[4,2,32,128]{3,2,1,0:T(8,128)(2,1)}, bf16[15,2,32,128]{3,2,1,0:T(8,128)(2,1)}) custom-call(s32[2,1,32]{2,1,0:T(1,128)S(1)} %bitcast.10, f32[2,38,2,40,128]{4,3,2,1,0:T(8,128)S(1)} %get-tuple-element.26.state, bf16[1072,128]{1,0:T(8,128)(2,1)S(1)} %collective-permute-done.4.from_off, ...), custom_call_target="tpu_custom_call" | custom-call | tf_op jit(solution)/shard_map/pallas_call | solution.py:649
  (1 shorter events, 0.0 us)
Async XLA Ops:
  0.6 6.4 %copy-start.2 = (f32[6,2,32,128]{3,2,1,0:T(8,128)S(1)}, f32[6,2,32,128]{3,2,1,0:T(8,128)}, u32[]{:S(2)}) copy-start(f32[6,2,32,128]{3,2,1,0:T(8,128)} %ori.1) | copy-start | bytes 589828
  0.6 6.4 %copy-start = (f32[19,2,32,128]{3,2,1,0:T(8,128)S(1)}, f32[19,2,32,128]{3,2,1,0:T(8,128)}, u32[]{:S(2)}) copy-start(f32[19,2,32,128]{3,2,1,0:T(8,128)} %pop.1) | copy-start | bytes 1867780
  0.7 33.9 %copy-start.5 = (f32[512]{0:T(512)S(1)}, f32[512]{0:T(512)}, u32[]{:S(2)}) copy-start(f32[512]{0:T(512)} %param.13) | copy-start | bytes 6148
  0.7 33.9 %copy-start.6 = (f32[512]{0:T(512)S(1)}, f32[512]{0:T(512)}, u32[]{:S(2)}) copy-start(f32[512]{0:T(512)} %param.15) | copy-start | bytes 6148
  0.7 33.9 %copy-start.3 = (bf16[512,15]{0,1:T(8,128)(2,1)S(1)}, bf16[512,15]{0,1:T(8,128)(2,1)}, u32[]{:S(2)}) copy-start(bf16[512,15]{0,1:T(8,128)(2,1)} %param.16) | copy-start | bytes 46084
  0.7 33.9 %copy-start.8 = (f32[15]{0:T(128)S(1)}, f32[15]{0:T(128)}, u32[]{:S(2)}) copy-start(f32[15]{0:T(128)} %param.17) | copy-start | bytes 184
  0.7 33.9 %copy-start.4 = (bf16[6,512]{1,0:T(8,128)(2,1)S(1)}, bf16[6,512]{1,0:T(8,128)(2,1)}, u32[]{:S(2)}) copy-start(bf16[6,512]{1,0:T(8,128)(2,1)} %w_in_hbm.1) | copy-start | bytes 18436
  0.7 33.9 %copy-start.1 = (bf16[512,512]{1,0:T(8,128)(2,1)S(1)}, bf16[512,512]{1,0:T(8,128)(2,1)}, u32[]{:S(2)}) copy-start(bf16[512,512]{1,0:T(8,128)(2,1)} %w_mid_hbm.1) | copy-start | bytes 1572868
  0.7 36.1 %copy-start.7 = (s32[2,32,1]{1,2,0:T(1,128)S(1)}, s32[2,32,1]{1,2,0:T(1,128)}, u32[]{:S(2)}) copy-start(s32[2,32,1]{1,2,0:T(1,128)} %param.11) | copy-start | bytes 772
  2.3 5.0 %collective-permute-start = (f32[2,32,128]{2,1,0:T(8,128)S(1)}, f32[2,32,128]{2,1,0:T(8,128)S(1)}, u32[]{:S(2)}, u32[]{:S(2)}) collective-permute-start(f32[2,32,128]{2,1,0:T(8,128)S(1)} %get-tuple-element.18.after), channel_id=1, source_target_pairs={{0,1},{1,2},{2,3},{4,5},{5,6},{6,7},{8,9},{9,10},{10,11},{12,13},{... | collective-permute-start | bytes 98312 | tf_op jit(solution)/shard_map/ppermute | solution.py:617
  5.7 5.8 %collective-permute-start.1 = (f32[2,32,128]{2,1,0:T(8,128)S(1)}, f32[2,32,128]{2,1,0:T(8,128)S(1)}, u32[]{:S(2)}, u32[]{:S(2)}) collective-permute-start(f32[2,32,128]{2,1,0:T(8,128)S(1)} %get-tuple-element.18.after), channel_id=1, source_target_pairs={{1,0},{2,1},{3,2},{5,4},{6,5},{7,6},{9,8},{10,9},{11,10},{13,12},{... | collective-permute-start | bytes 98312 | tf_op jit(solution)/shard_map/ppermute | solution.py:618
  11.5 6.6 %collective-permute-start.2 = (f32[104,128]{1,0:T(8,128)S(1)}, f32[104,128]{1,0:T(8,128)S(1)}, u32[]{:S(2)}, u32[]{:S(2)}) collective-permute-start(f32[104,128]{1,0:T(8,128)S(1)} %get-tuple-element.24), channel_id=1, source_target_pairs={{0,4},{4,8},{8,12},{12,16},{16,20},{20,24},{24,28},{28,0},{1,5},{5... | collective-permute-start | bytes 159752 | tf_op jit(solution)/shard_map/ppermute | solution.py:626
  16.2 7.2 %collective-permute-start.3 = (f32[104,128]{1,0:T(8,128)S(1)}, f32[104,128]{1,0:T(8,128)S(1)}, u32[]{:S(2)}, u32[]{:S(2)}) collective-permute-start(f32[104,128]{1,0:T(8,128)S(1)} %get-tuple-element.25), channel_id=1, source_target_pairs={{0,28},{4,0},{8,4},{12,8},{16,12},{20,16},{24,20},{28,24},{1,29},{... | collective-permute-start | bytes 159752 | tf_op jit(solution)/shard_map/ppermute | solution.py:627
  25.1 11.7 %collective-permute-start.4 = (bf16[1072,128]{1,0:T(8,128)(2,1)S(1)}, bf16[1072,128]{1,0:T(8,128)(2,1)S(1)}, u32[]{:S(2)}, u32[]{:S(2)}) collective-permute-start(bf16[1072,128]{1,0:T(8,128)(2,1)S(1)} %get-tuple-element.27), channel_id=1, source_target_pairs={{0,480},{32,64},{64,32},{96,128},{128,96},{160,192},{192,160},{224... | collective-permute-start | bytes 823304 | tf_op jit(solution)/shard_map/ppermute | solution.py:647
  32.7 4.2 %collective-permute-start.5 = (bf16[1072,128]{1,0:T(8,128)(2,1)S(1)}, bf16[1072,128]{1,0:T(8,128)(2,1)S(1)}, u32[]{:S(2)}, u32[]{:S(2)}) collective-permute-start(bf16[1072,128]{1,0:T(8,128)(2,1)S(1)} %get-tuple-element.28), channel_id=1, source_target_pairs={{0,32},{32,0},{64,96},{96,64},{128,160},{160,128},{192,224},{224,1... | collective-permute-start | bytes 823304 | tf_op jit(solution)/shard_map/ppermute | solution.py:648

commit v5 on v3

--- a/solution.py
+++ b/solution.py
@@ -42,8 +42,11 @@
 KNOWN = {0: [i for i in range(19) if VELOCITIES[i][0] != 1], 1: [i for i in range(19) if VELOCITIES[i][0] != -1]}
 MSG_WIDE = 23
 MSG_ROWS = 1072
-HALO_AT = 928
-SIDE_AT = 1024
+MID_ROWS = 480
+SIDE_MID = 464
+RIM_AT = 480
+HALO_AT = 944
+SIDE_RIM = 1040
 CORNER_AT = 1056
 MIB = 1024 * 1024
 LIMIT_PACK = 5375 * MIB // 100
@@ -157,6 +160,18 @@
                 z[j][k] = plus(z[j][k], times(full(j, m), mix[m][k]))
     scaled = SHAPE_FACTOR * twice
     return [plus(z[j][k], z[k][j]) - scaled * full(j, k) for j, k in PAIRS]
+
+
+def field_row(k, r):
+    return 16 * k + 8 * (r - 1) if r in (1, 2) else RIM_AT + 16 * k + 8 * (r // 3)
+
+
+def side_row(r):
+    return SIDE_MID + 8 * (r - 1) if r in (1, 2) else (CORNER_AT if r == 4 else SIDE_RIM + 8 * (r // 3))
+
+
+def state_row(r):
+    return {1: 0, 2: 8, 0: 0, 3: 8, 4: 16}[r]
 
 
 def put(ref, at, r, v):
@@ -284,97 +299,114 @@
         high_rows[pl.ds(100 + 2 * t, 2), :] = sides[t, 30:32, :]
 
 
-def step_one_kernel(own, sides, from_yminus, from_yplus, state, msg_low, msg_high, halo, fields, out):
+def collide_group(raw, fields, x, t, r):
+    numbers = list(range(19))
+    f = [raw(i) for i in numbers]
+    rho, mom = moments(f, numbers)
+    inv = 1.0 / rho
+    u = [m * inv for m in mom]
+    relaxed = relax(f, rho, u, numbers)
+    for i in numbers:
+        put(fields, (i, x, t), r, relaxed[i])
+    for j in range(3):
+        put(fields, (19 + j, x, t), r, u[j])
+    for k in range(6):
+        put(fields, (22 + k, x, t), r, raw(19 + k))
+
+
+def advance_group(fields, state, out, x, r, low, high):
+    lane, row = lanes_of(), rows_of()
+    place = lambda f, xs=x: (lambda t: (f, xs, t))
+    known = [{}, {}]
+    for i in KNOWN[x]:
+        xs = x - VELOCITIES[i][0]
+        pair = stream(fields, place(i, xs), i, r, low, high, lambda i=i: get(fields, (opposite(i), x, 0), r))
+        known[0][i], known[1][i] = pair
+    grad = [[[None] * 3 for _ in range(3)] for _ in range(2)]
+    sign = 0.5 if x == 0 else -0.5
+    for j in range(3):
+        by_y = central(fields, place(19 + j), r, 1, low, high, False)
+        by_z = central(fields, place(19 + j), r, 2, low, high, False)
+        for t in range(2):
+            grad[t][j][0] = sign * get(fields, (19 + j, 1 - x, t), r)
+            grad[t][j][1] = by_y[t]
+            grad[t][j][2] = by_z[t]
+    u = [[get(fields, (19 + j, x, t), r) for j in range(3)] for t in range(2)]
+    a = [[get(fields, (22 + k, x, t), r) for k in range(6)] for t in range(2)]
+    advect = [[], []]
+    for k in range(6):
+        by_y = central(fields, place(22 + k), r, 1, low, high, True)
+        by_z = central(fields, place(22 + k), r, 2, low, high, True)
+        for t in range(2):
+            by_x = sign * get(fields, (22 + k, 1 - x, t), r)
+            advect[t].append(u[t][0] * by_x + u[t][1] * by_y[t] + u[t][2] * by_z[t])
+    side_pack = jnp.zeros((8, 128), jnp.float32)
+    for t in range(2):
+        rate = jeffery(a[t], grad[t])
+        part = [a[t][k] + ORIENT_STEP * (rate[k] - advect[t][k]) for k in range(6)]
+        rho, mom = moments(known[t], KNOWN[x])
+        outward = [get(fields, (i, x, t), r) for i in TOWARD[x]]
+        keep = [known[t][i] for i in KNOWN[x]] + [rho] + mom + part + u[t] + a[t] + outward
+        for k in range(STATE):
+            state[x, k, t, pl.ds(state_row(r), 8), :] = keep[k]
+        wide = outward + u[t] + a[t] + [rho] + mom + [known[t][i] for i in TOWARD[x]]
+        if t == 1:
+            for k in range(MSG_WIDE):
+                at = 4 * k
+                side_pack = jnp.where((lane >= at) & (lane < at + 4), roll(wide[k], at + 2, 1), side_pack)
+        elif r < 4:
+            for k, v in enumerate(wide + part):
+                out[x, pl.ds(field_row(k, r), 8), :] = v
+        else:
+            inner = (row >= 2) & (row < 6)
+            for k in range(0, MSG_WIDE, 2):
+                v = wide[k]
+                if k + 1 < MSG_WIDE:
+                    v = jnp.where(inner, roll(wide[k + 1], 4, 0), v)
+                out[x, pl.ds(HALO_AT + 4 * k, 8), :] = v
+    out[x, pl.ds(side_row(r), 8), :] = side_pack
+
+
+def middle_kernel(own, sides, fields, state, message, out):
     low, high = walls()
-    lane, row = lanes_of(), rows_of()
+    for x in range(2):
+        for r in range(4):
+            rows = pl.ds(8 * r, 8)
+            for k in range(28):
+                put(fields, (k, x, 0), r, own[k, x, rows, :])
+
+            def raw(f):
+                s = 2 * f + x
+                return roll(sides[s // 32, rows, :], -(4 * (s % 32) + 2), 1)
+
+            collide_group(raw, fields, x, 1, r)
+    for x in range(2):
+        for r in (1, 2):
+            advance_group(fields, state, out, x, r, low, high)
+    message[...] = out[...].astype(jnp.bfloat16)
+
+
+def step_one_kernel(before, middle, from_yminus, from_yplus, fields, state, msg_low, msg_high, halo, out):
+    del before
+    low, high = walls()
     for s in range(52):
         halo[s, 0:2, :] = from_yplus[pl.ds(2 * s, 2), :]
         halo[s, 6:8, :] = from_yminus[pl.ds(2 * s, 2), :]
-
-    def raw(f, x, t, r):
-        s = 2 * f + x
-        if t == 0:
-            return halo[s]
-        packed = halo[50 + s // 32] if r == 4 else sides[s // 32, pl.ds(8 * r, 8), :]
-        return roll(packed, -(4 * (s % 32) + 2), 1)
-
-    numbers = list(range(19))
     for x in range(2):
         for t in range(2):
-            for r in range(5):
-                if t == 0 and r < 4:
-                    for k in range(28):
-                        put(fields, (k, x, t), r, own[k, x, pl.ds(8 * r, 8), :])
-                    continue
-                f = [raw(i, x, t, r) for i in numbers]
-                rho, mom = moments(f, numbers)
-                inv = 1.0 / rho
-                u = [m * inv for m in mom]
-                relaxed = relax(f, rho, u, numbers)
-                for i in numbers:
-                    put(fields, (i, x, t), r, relaxed[i])
-                for j in range(3):
-                    put(fields, (19 + j, x, t), r, u[j])
-                for k in range(6):
-                    put(fields, (22 + k, x, t), r, raw(19 + k, x, t, r))
-
+
+            def raw(f):
+                s = 2 * f + x
+                return halo[s] if t == 0 else roll(halo[50 + s // 32], -(4 * (s % 32) + 2), 1)
+
+            collide_group(raw, fields, x, t, 4)
     for x in range(2):
-        for r in range(5):
-            place = lambda f, xs=x: (lambda t: (f, xs, t))
-            known = [{}, {}]
-            for i in KNOWN[x]:
-                xs = x - VELOCITIES[i][0]
-                pair = stream(
-                    fields, place(i, xs), i, r, low, high, lambda i=i: get(fields, (opposite(i), x, 0), r)
-                )
-                known[0][i], known[1][i] = pair
-            grad = [[[None] * 3 for _ in range(3)] for _ in range(2)]
-            sign = 0.5 if x == 0 else -0.5
-            for j in range(3):
-                by_y = central(fields, place(19 + j), r, 1, low, high, False)
-                by_z = central(fields, place(19 + j), r, 2, low, high, False)
-                for t in range(2):
-                    grad[t][j][0] = sign * get(fields, (19 + j, 1 - x, t), r)
-                    grad[t][j][1] = by_y[t]
-                    grad[t][j][2] = by_z[t]
-            u = [[get(fields, (19 + j, x, t), r) for j in range(3)] for t in range(2)]
-            a = [[get(fields, (22 + k, x, t), r) for k in range(6)] for t in range(2)]
-            advect = [[], []]
-            for k in range(6):
-                by_y = central(fields, place(22 + k), r, 1, low, high, True)
-                by_z = central(fields, place(22 + k), r, 2, low, high, True)
-                for t in range(2):
-                    by_x = sign * get(fields, (22 + k, 1 - x, t), r)
-                    advect[t].append(u[t][0] * by_x + u[t][1] * by_y[t] + u[t][2] * by_z[t])
-            side_pack = jnp.zeros((8, 128), jnp.float32)
-            for t in range(2):
-                rate = jeffery(a[t], grad[t])
-                part = [a[t][k] + ORIENT_STEP * (rate[k] - advect[t][k]) for k in range(6)]
-                rho, mom = moments(known[t], KNOWN[x])
-                outward = [get(fields, (i, x, t), r) for i in TOWARD[x]]
-                keep = [known[t][i] for i in KNOWN[x]] + [rho] + mom + part + u[t] + a[t] + outward
-                for k in range(STATE):
-                    state[x, k, t, pl.ds(8 * r, 8), :] = keep[k]
-                wide = outward + u[t] + a[t] + [rho] + mom + [known[t][i] for i in TOWARD[x]]
-                if t == 1:
-                    for k in range(MSG_WIDE):
-                        at = 4 * k
-                        side_pack = jnp.where((lane >= at) & (lane < at + 4), roll(wide[k], at + 2, 1), side_pack)
-                elif r < 4:
-                    for k, v in enumerate(wide + part):
-                        out[x, pl.ds(32 * k + 8 * r, 8), :] = v
-                else:
-                    inner = (row >= 2) & (row < 6)
-                    for k in range(0, MSG_WIDE, 2):
-                        v = wide[k]
-                        if k + 1 < MSG_WIDE:
-                            v = jnp.where(inner, roll(wide[k + 1], 4, 0), v)
-                        out[x, pl.ds(HALO_AT + 4 * k, 8), :] = v
-            out[x, pl.ds(SIDE_AT + 8 * r if r < 4 else CORNER_AT, 8), :] = side_pack
-    for x in range(2):
+        for r in (0, 3, 4):
+            advance_group(fields, state, out, x, r, low, high)
         out[x, pl.ds(CORNER_AT + 8, 8), :] = jnp.zeros((8, 128), jnp.float32)
-    msg_low[...] = out[0].astype(jnp.bfloat16)
-    msg_high[...] = out[1].astype(jnp.bfloat16)
+    for x, msg in enumerate((msg_low, msg_high)):
+        msg[0:MID_ROWS, :] = middle[x]
+        msg[MID_ROWS:MSG_ROWS, :] = out[x, MID_ROWS:MSG_ROWS, :].astype(jnp.bfloat16)
 
 
 def weights_kernel(
@@ -407,7 +439,7 @@
 
 
 def step_two_kernel(
-    slots, state, from_low, from_high, w_one, w_mid, b_mid, w_out, b_out, flow, closure,
+    slots, state_mid, state_rim, from_low, from_high, w_one, w_mid, b_mid, w_out, b_out, flow, closure,
     got, fields, near, level, feats, spread, place,
 ):
     low, high = walls()
@@ -421,14 +453,17 @@
 
     def arrived(x, k, t, r):
         if t == 0 and r < 4:
-            return got[x, pl.ds(32 * k + 8 * r, 8), :]
+            return got[x, pl.ds(field_row(k, r), 8), :]
         if t == 0:
             v = got[x, pl.ds(HALO_AT + 8 * (k // 2), 8), :]
             return roll(v, 4, 0) if k % 2 else v
-        v = got[x, pl.ds(SIDE_AT + 8 * r if r < 4 else CORNER_AT, 8), :]
+        v = got[x, pl.ds(side_row(r), 8), :]
         return roll(v, -(4 * k + 2), 1)
 
-    kept = lambda x, k, t, r: state[x, k, t, pl.ds(8 * r, 8), :]
+    def kept(x, k, t, r):
+        part = state_mid if r in (1, 2) else state_rim
+        return part[x, k, t, pl.ds(state_row(r), 8), :]
+
     for x in range(2):
         for t in range(2):
             for r in range(5):
@@ -562,7 +597,7 @@
     shape = lambda *s, d=f32: jax.ShapeDtypeStruct(s, d)
     vmem = pl.BlockSpec(memory_space=pltpu.VMEM)
     smem = pl.BlockSpec(memory_space=pltpu.SMEM)
-    params = pltpu.CompilerParams(vmem_limit_bytes=48 * 1024 * 1024)
+    params = pltpu.CompilerParams(vmem_limit_bytes=24 * MIB)
 
     def ring(axis, step, wrap):
         n = lax.axis_size(axis)
@@ -621,30 +656,37 @@
         out_specs=(vmem,) * 3,
         compiler_params=params,
     )(from_minus, from_plus, low_raw, high_raw, token)
+    fields_shape = shape(28, 2, 2, 64, 128)
+    fields, state_mid, middle = pl.pallas_call(
+        middle_kernel,
+        out_shape=(fields_shape, shape(2, STATE, 2, 16, 128), shape(2, MID_ROWS, 128, d=bf16)),
+        in_specs=[vmem] * 2,
+        out_specs=(vmem,) * 3,
+        scratch_shapes=[pltpu.VMEM((2, MID_ROWS, 128), f32)],
+        compiler_params=params,
+    )(own, sides)
     from_yminus = lax.ppermute(high_rows, "gy", ring("gy", 1, True))
     from_yplus = lax.ppermute(low_rows, "gy", ring("gy", -1, True))
-    state, msg_low, msg_high = pl.pallas_call(
+    fields, state_rim, msg_low, msg_high = pl.pallas_call(
         step_one_kernel,
         out_shape=(
-            shape(2, STATE, 2, 40, 128),
+            fields_shape,
+            shape(2, STATE, 2, 24, 128),
             shape(MSG_ROWS, 128, d=bf16),
             shape(MSG_ROWS, 128, d=bf16),
         ),
         in_specs=[vmem] * 4,
-        out_specs=(vmem,) * 3,
-        scratch_shapes=[
-            pltpu.VMEM((52, 8, 128), f32),
-            pltpu.VMEM((28, 2, 2, 64, 128), f32),
-            pltpu.VMEM((2, MSG_ROWS, 128), f32),
-        ],
+        out_specs=(vmem,) * 4,
+        scratch_shapes=[pltpu.VMEM((52, 8, 128), f32), pltpu.VMEM((2, MSG_ROWS, 128), f32)],
+        input_output_aliases={0: 0},
         compiler_params=params,
-    )(own, sides, from_yminus, from_yplus)
+    )(fields, middle, from_yminus, from_yplus)
     from_low = lax.ppermute(msg_high, "gx", ring("gx", 1, True))
     from_high = lax.ppermute(msg_low, "gx", ring("gx", -1, True))
     return pl.pallas_call(
         step_two_kernel,
         out_shape=(shape(4, 2, 32, 128, d=bf16), shape(15, 2, 32, 128, d=bf16)),
-        in_specs=[smem] + [vmem] * 8,
+        in_specs=[smem] + [vmem] * 9,
         out_specs=(vmem,) * 2,
         scratch_shapes=[
             pltpu.VMEM((2, MSG_ROWS, 128), f32),
@@ -656,7 +698,7 @@
             pltpu.SMEM((17,), jnp.int32),
         ],
         compiler_params=params,
-    )(slots, state, from_low, from_high, w_one, w_two, bias_mid, w_three, bias_out)
+    )(slots, state_mid, state_rim, from_low, from_high, w_one, w_two, bias_mid, w_three, bias_out)
 
 
 def solution(mesh):

time: 41.3 us -> 40.8 us (0.988)
  the two profiles are of different devices: /device:TPU:219 before, /device:TPU:217 now
where the time goes in v5:
time: 40.8 us; the launch traced here: 40.6 us
  starting transfers between devices  17.6 us (43%)
  waiting for transfers between devices  12.8 us (31%)
  Pallas kernels  9.3 us (23%)
  between operations  0.83 us (2%)
    ppermute x1, starting transfers between devices, local(): from_low = lax.ppermute(msg_high, 'gx', ring('gx', 1, True))  6.73 us
    pallas_call x1, Pallas kernels, local(): pl.pallas_call(step_two_kernel, out_shape=(shape(4, 2, 32, 128, d=bf16),...  5.16 us
    ppermute x1, starting transfers between devices, local(): from_yminus = lax.ppermute(high_rows, 'gy', ring('gy', 1, True))  4.42 us
    ppermute x1, waiting for transfers between devices, local(): from_high = lax.ppermute(msg_low, 'gx', ring('gx', -1, True))  3.69 us
    ppermute x1, waiting for transfers between devices, local(): from_yplus = lax.ppermute(low_rows, 'gy', ring('gy', -1, True))  3.3 us
    ppermute x1, starting transfers between devices, local(): from_minus = lax.ppermute(zpack, 'gz', ring('gz', 1, False))  3.25 us
    ppermute x1, waiting for transfers between devices, local(): from_plus = lax.ppermute(zpack, 'gz', ring('gz', -1, False))  3.05 us
    ppermute x1, waiting for transfers between devices, local(): from_low = lax.ppermute(msg_high, 'gx', ring('gx', 1, True))  2.79 us
  transfers between devices with their start and end apart: 6, of which 4 were waited for; matrix products, arithmetic and copies ran while one was open for 0% of the time, Pallas kernels for 4%

profile of v5, /device:TPU:217, one launch (start us, length us, event | category | flops | bytes accessed | tf_op | source)
XLA Modules:
  0.0 40.6 jit_solution(11957057823593373624)
XLA Ops:
  0.6 0.0 copy-start
  0.6 0.0 copy-start.2
  0.6 1.5 %shard_map.104 = (f32[2,32,128]{2,1,0:T(8,128)S(1)}, f32[104,128]{1,0:T(8,128)S(1)}, f32[104,128]{1,0:T(8,128)S(1)}) custom-call(f32[19,2,32,128]{3,2,1,0:T(8,128)} %pop.1, f32[6,2,32,128]{3,2,1,0:T(8,128)} %ori.1), custom_call_target="tpu_custom_call" | custom-call | flops 10000000000 | bytes 10000000 | tf_op jit(solution)/shard_map/pallas_call | solution.py:630
  2.2 0.0 copy-start.1
  2.2 0.0 copy-start.3
  2.2 0.0 copy-start.4
  2.2 0.0 copy-start.5
  2.2 0.0 copy-start.6
  2.2 0.0 copy-start.8
  2.3 0.0 copy-start.7
  2.3 3.2 %collective-permute-start = (f32[2,32,128]{2,1,0:T(8,128)S(1)}, f32[2,32,128]{2,1,0:T(8,128)S(1)}, u32[]{:S(2)}, u32[]{:S(2)}) collective-permute-start(f32[2,32,128]{2,1,0:T(8,128)S(1)} %get-tuple-element.21.after), channel_id=1, source_target_pairs={{0,1},{1,2},{2,3},{4,5},{5,6},{6,7},{8,9},{9,10},{10,11},{12,13},{... | collective-permute-start | bytes 98312 | tf_op jit(solution)/shard_map/ppermute | solution.py:650
  5.5 1.3 %collective-permute-start.1 = (f32[2,32,128]{2,1,0:T(8,128)S(1)}, f32[2,32,128]{2,1,0:T(8,128)S(1)}, u32[]{:S(2)}, u32[]{:S(2)}) collective-permute-start(f32[2,32,128]{2,1,0:T(8,128)S(1)} %get-tuple-element.21.after), channel_id=1, source_target_pairs={{1,0},{2,1},{3,2},{5,4},{6,5},{7,6},{9,8},{10,9},{11,10},{13,12},{... | collective-permute-start | bytes 98312 | tf_op jit(solution)/shard_map/ppermute | solution.py:651
  6.8 0.0 copy-done
  6.8 0.0 copy-done.2
  6.8 0.3 shard_map.105
  7.1 0.0 collective-permute-done.from_minus
  7.1 3.1 %collective-permute-done.1.from_plus = f32[2,32,128]{2,1,0:T(8,128)S(1)} collective-permute-done((f32[2,32,128]{2,1,0:T(8,128)S(1)}, f32[2,32,128]{2,1,0:T(8,128)S(1)}, u32[]{:S(2)}, u32[]{:S(2)}) %collective-permute-start.1) | collective-permute-done | bytes 32800 | tf_op jit(solution)/shard_map/ppermute | solution.py:651
  10.2 4.4 %collective-permute-start.2 = (f32[104,128]{1,0:T(8,128)S(1)}, f32[104,128]{1,0:T(8,128)S(1)}, u32[]{:S(2)}, u32[]{:S(2)}) collective-permute-start(f32[104,128]{1,0:T(8,128)S(1)} %get-tuple-element.30), channel_id=1, source_target_pairs={{0,4},{4,8},{8,12},{12,16},{16,20},{20,24},{24,28},{28,0},{1,5},{5... | collective-permute-start | bytes 159752 | tf_op jit(solution)/shard_map/ppermute | solution.py:668
  14.6 1.9 %collective-permute-start.3 = (f32[104,128]{1,0:T(8,128)S(1)}, f32[104,128]{1,0:T(8,128)S(1)}, u32[]{:S(2)}, u32[]{:S(2)}) collective-permute-start(f32[104,128]{1,0:T(8,128)S(1)} %get-tuple-element.31), channel_id=1, source_target_pairs={{0,28},{4,0},{8,4},{12,8},{16,12},{20,16},{24,20},{28,24},{1,29},{... | collective-permute-start | bytes 159752 | tf_op jit(solution)/shard_map/ppermute | solution.py:669
  16.6 0.8 %shard_map.107 = (f32[28,2,2,64,128]{4,3,2,1,0:T(8,128)S(1)}, f32[2,38,2,16,128]{4,3,2,1,0:T(8,128)S(1)}, bf16[2,480,128]{2,1,0:T(8,128)(2,1)S(1)}) custom-call(f32[28,2,32,128]{3,2,1,0:T(8,128)S(1)} %get-tuple-element.22.own, f32[2,32,128]{2,1,0:T(8,128)S(1)} %get-tuple-element.26.sides), custom_call_target="tpu_custom_call" | custom-call | tf_op jit(solution)/shard_map/pallas_call | solution.py:660
  17.4 0.0 collective-permute-done.2.from_yminus
  17.4 3.3 %collective-permute-done.3.from_yplus = f32[104,128]{1,0:T(8,128)S(1)} collective-permute-done((f32[104,128]{1,0:T(8,128)S(1)}, f32[104,128]{1,0:T(8,128)S(1)}, u32[]{:S(2)}, u32[]{:S(2)}) %collective-permute-start.3) | collective-permute-done | bytes 53280 | tf_op jit(solution)/shard_map/ppermute | solution.py:669
  20.7 0.9 %shard_map.108 = (f32[28,2,2,64,128]{4,3,2,1,0:T(8,128)S(1)}, f32[2,38,2,24,128]{4,3,2,1,0:T(8,128)S(1)}, bf16[1072,128]{1,0:T(8,128)(2,1)S(1)}, bf16[1072,128]{1,0:T(8,128)(2,1)S(1)}) custom-call(f32[28,2,2,64,128]{4,3,2,1,0:T(8,128)S(1)} %get-tuple-element.28.before, ...), custom_call_target="tpu_custom_call", output_to_operand_aliasing={{0}: (0, {})} | custom-call | tf_op jit(solution)/shard_map/pallas_call | solution.py:670
  21.6 6.7 %collective-permute-start.4 = (bf16[1072,128]{1,0:T(8,128)(2,1)S(1)}, bf16[1072,128]{1,0:T(8,128)(2,1)S(1)}, u32[]{:S(2)}, u32[]{:S(2)}) collective-permute-start(bf16[1072,128]{1,0:T(8,128)(2,1)S(1)} %get-tuple-element.33), channel_id=1, source_target_pairs={{0,32},{32,64},{64,96},{96,128},{128,160},{160,192},{192,224},{224... | collective-permute-start | bytes 823304 | tf_op jit(solution)/shard_map/ppermute | solution.py:684
  28.3 0.0 collective-permute-start.5
  28.3 0.0 copy-done.1
  28.3 0.0 copy-done.3
  28.3 0.0 copy-done.4
  28.3 0.0 copy-done.5
  28.4 0.0 copy-done.6
  28.4 0.0 copy-done.8
  28.4 0.6 %shard_map.109 = (bf16[512,8]{1,0:T(8,128)(2,1)S(1)}, bf16[512,512]{1,0:T(8,128)(2,1)S(1)}, f32[512,128]{1,0:T(8,128)S(1)}, bf16[15,512]{1,0:T(8,128)(2,1)S(1)}, f32[16,128]{1,0:T(8,128)S(1)}) custom-call(bf16[6,512]{1,0:T(8,128)(2,1)S(1)} %copy-done.4, f32[1,512]{1,0:T(1,128)S(1)} %bitcast.8, bf16[512,512]{1,0:T(8,128)(2,1)S(1)} %copy-done.1, ...), custom_call_target="tpu_custom_call" | custom-call | tf_op jit(solution)/shard_map/pallas_call | solution.py:608
  29.0 2.8 %collective-permute-done.4.from_low = bf16[1072,128]{1,0:T(8,128)(2,1)S(1)} collective-permute-done((bf16[1072,128]{1,0:T(8,128)(2,1)S(1)}, bf16[1072,128]{1,0:T(8,128)(2,1)S(1)}, u32[]{:S(2)}, u32[]{:S(2)}) %collective-permute-start.4) | collective-permute-done | bytes 274464 | tf_op jit(solution)/shard_map/ppermute | solution.py:684
  31.8 3.7 %collective-permute-done.5.from_high = bf16[1072,128]{1,0:T(8,128)(2,1)S(1)} collective-permute-done((bf16[1072,128]{1,0:T(8,128)(2,1)S(1)}, bf16[1072,128]{1,0:T(8,128)(2,1)S(1)}, u32[]{:S(2)}, u32[]{:S(2)}) %collective-permute-start.5) | collective-permute-done | bytes 274464 | tf_op jit(solution)/shard_map/ppermute | solution.py:685
  35.5 0.0 copy-done.7
  35.5 5.2 %shard_map.110 = (bf16[4,2,32,128]{3,2,1,0:T(8,128)(2,1)}, bf16[15,2,32,128]{3,2,1,0:T(8,128)(2,1)}) custom-call(s32[2,1,32]{2,1,0:T(1,128)S(1)} %bitcast.10, f32[2,38,2,16,128]{4,3,2,1,0:T(8,128)S(1)} %get-tuple-element.27.state_mid, f32[2,38,2,24,128]{4,3,2,1,0:T(8,128)S(1)} %get-tuple-element.32.state_rim, ...), custom_call_target="tpu_custom_call" | custom-call | tf_op jit(solution)/shard_map/pallas_call | solution.py:686
  (1 shorter events, 0.0 us)
Async XLA Ops:
  0.6 6.2 %copy-start = (f32[19,2,32,128]{3,2,1,0:T(8,128)S(1)}, f32[19,2,32,128]{3,2,1,0:T(8,128)}, u32[]{:S(2)}) copy-start(f32[19,2,32,128]{3,2,1,0:T(8,128)} %pop.1) | copy-start | bytes 1867780
  0.6 6.2 %copy-start.2 = (f32[6,2,32,128]{3,2,1,0:T(8,128)S(1)}, f32[6,2,32,128]{3,2,1,0:T(8,128)}, u32[]{:S(2)}) copy-start(f32[6,2,32,128]{3,2,1,0:T(8,128)} %ori.1) | copy-start | bytes 589828
  2.2 26.1 %copy-start.1 = (bf16[512,512]{1,0:T(8,128)(2,1)S(1)}, bf16[512,512]{1,0:T(8,128)(2,1)}, u32[]{:S(2)}) copy-start(bf16[512,512]{1,0:T(8,128)(2,1)} %w_mid_hbm.1) | copy-start | bytes 1572868
  2.2 26.1 %copy-start.3 = (bf16[512,15]{0,1:T(8,128)(2,1)S(1)}, bf16[512,15]{0,1:T(8,128)(2,1)}, u32[]{:S(2)}) copy-start(bf16[512,15]{0,1:T(8,128)(2,1)} %param.16) | copy-start | bytes 46084
  2.2 26.1 %copy-start.4 = (bf16[6,512]{1,0:T(8,128)(2,1)S(1)}, bf16[6,512]{1,0:T(8,128)(2,1)}, u32[]{:S(2)}) copy-start(bf16[6,512]{1,0:T(8,128)(2,1)} %w_in_hbm.1) | copy-start | bytes 18436
  2.2 26.1 %copy-start.5 = (f32[512]{0:T(512)S(1)}, f32[512]{0:T(512)}, u32[]{:S(2)}) copy-start(f32[512]{0:T(512)} %param.13) | copy-start | bytes 6148
  2.2 26.1 %copy-start.6 = (f32[512]{0:T(512)S(1)}, f32[512]{0:T(512)}, u32[]{:S(2)}) copy-start(f32[512]{0:T(512)} %param.15) | copy-start | bytes 6148
  2.2 26.1 %copy-start.8 = (f32[15]{0:T(128)S(1)}, f32[15]{0:T(128)}, u32[]{:S(2)}) copy-start(f32[15]{0:T(128)} %param.17) | copy-start | bytes 184
  2.3 33.2 %copy-start.7 = (s32[2,32,1]{1,2,0:T(1,128)S(1)}, s32[2,32,1]{1,2,0:T(1,128)}, u32[]{:S(2)}) copy-start(s32[2,32,1]{1,2,0:T(1,128)} %param.11) | copy-start | bytes 772
  2.3 4.9 %collective-permute-start = (f32[2,32,128]{2,1,0:T(8,128)S(1)}, f32[2,32,128]{2,1,0:T(8,128)S(1)}, u32[]{:S(2)}, u32[]{:S(2)}) collective-permute-start(f32[2,32,128]{2,1,0:T(8,128)S(1)} %get-tuple-element.21.after), channel_id=1, source_target_pairs={{0,1},{1,2},{2,3},{4,5},{5,6},{6,7},{8,9},{9,10},{10,11},{12,13},{... | collective-permute-start | bytes 98312 | tf_op jit(solution)/shard_map/ppermute | solution.py:650
  5.5 4.7 %collective-permute-start.1 = (f32[2,32,128]{2,1,0:T(8,128)S(1)}, f32[2,32,128]{2,1,0:T(8,128)S(1)}, u32[]{:S(2)}, u32[]{:S(2)}) collective-permute-start(f32[2,32,128]{2,1,0:T(8,128)S(1)} %get-tuple-element.21.after), channel_id=1, source_target_pairs={{1,0},{2,1},{3,2},{5,4},{6,5},{7,6},{9,8},{10,9},{11,10},{13,12},{... | collective-permute-start | bytes 98312 | tf_op jit(solution)/shard_map/ppermute | solution.py:651
  10.2 7.2 %collective-permute-start.2 = (f32[104,128]{1,0:T(8,128)S(1)}, f32[104,128]{1,0:T(8,128)S(1)}, u32[]{:S(2)}, u32[]{:S(2)}) collective-permute-start(f32[104,128]{1,0:T(8,128)S(1)} %get-tuple-element.30), channel_id=1, source_target_pairs={{0,4},{4,8},{8,12},{12,16},{16,20},{20,24},{24,28},{28,0},{1,5},{5... | collective-permute-start | bytes 159752 | tf_op jit(solution)/shard_map/ppermute | solution.py:668
  14.6 6.1 %collective-permute-start.3 = (f32[104,128]{1,0:T(8,128)S(1)}, f32[104,128]{1,0:T(8,128)S(1)}, u32[]{:S(2)}, u32[]{:S(2)}) collective-permute-start(f32[104,128]{1,0:T(8,128)S(1)} %get-tuple-element.31), channel_id=1, source_target_pairs={{0,28},{4,0},{8,4},{12,8},{16,12},{20,16},{24,20},{28,24},{1,29},{... | collective-permute-start | bytes 159752 | tf_op jit(solution)/shard_map/ppermute | solution.py:669
  21.6 10.2 %collective-permute-start.4 = (bf16[1072,128]{1,0:T(8,128)(2,1)S(1)}, bf16[1072,128]{1,0:T(8,128)(2,1)S(1)}, u32[]{:S(2)}, u32[]{:S(2)}) collective-permute-start(bf16[1072,128]{1,0:T(8,128)(2,1)S(1)} %get-tuple-element.33), channel_id=1, source_target_pairs={{0,32},{32,64},{64,96},{96,128},{128,160},{160,192},{192,224},{224... | collective-permute-start | bytes 823304 | tf_op jit(solution)/shard_map/ppermute | solution.py:684
  28.3 7.1 %collective-permute-start.5 = (bf16[1072,128]{1,0:T(8,128)(2,1)S(1)}, bf16[1072,128]{1,0:T(8,128)(2,1)S(1)}, u32[]{:S(2)}, u32[]{:S(2)}) collective-permute-start(bf16[1072,128]{1,0:T(8,128)(2,1)S(1)} %get-tuple-element.34), channel_id=1, source_target_pairs={{0,480},{32,0},{64,32},{96,64},{128,96},{160,128},{192,160},{224,1... | collective-permute-start | bytes 823304 | tf_op jit(solution)/shard_map/ppermute | solution.py:685

commit v6 on v5

--- a/solution.py
+++ b/solution.py
@@ -248,25 +248,50 @@
     return copies
 
 
-def pack_z_kernel(pop_hbm, ori_hbm, zpack, low_rows, high_rows, pop, ori, sems):
-    for copy in fetch([(pop_hbm, pop), (ori_hbm, ori)], sems):
-        copy.wait()
+PIECES = [(0, 5), (5, 10), (10, 15), (15, 19)]
+
+
+def pack_z_kernel(pop_hbm, ori_hbm, zlow, zhigh, low_rows, high_rows, pop, ori, sems):
+    pairs = [(pop_hbm.at[pl.ds(a, b - a)], pop.at[pl.ds(a, b - a)]) for a, b in PIECES]
+    copies = fetch(pairs + [(ori_hbm, ori)], sems)
+    starts = [a for a, _ in PIECES] + [19]
     lane = lax.broadcasted_iota(jnp.int32, (32, 128), 1)
-    tiles = [jnp.zeros((32, 128), jnp.float32), jnp.zeros((32, 128), jnp.float32)]
+    low = jnp.zeros((32, 128), jnp.float32)
+    high = jnp.zeros((32, 128), jnp.float32)
     for f in range(25):
+        if f in starts:
+            copies[starts.index(f)].wait()
+        src = pop if f < 19 else ori
+        k = f if f < 19 else f - 19
         for x in range(2):
             s = 2 * f + x
-            src = pop if f < 19 else ori
-            k = f if f < 19 else f - 19
-            v = src[k, x]
-            at = 4 * (s % 32)
-            tiles[s // 32] = jnp.where((lane >= at) & (lane < at + 4), roll(v, at + 2, 1), tiles[s // 32])
+            at = 2 * s
+            v = roll(src[k, x], at + 2, 1)
+            high = jnp.where((lane >= at) & (lane < at + 2), v, high)
+            low = jnp.where((lane >= at + 2) & (lane < at + 4), v, low)
             low_rows[pl.ds(2 * s, 2), :] = src[k, x, 0:2, :]
             high_rows[pl.ds(2 * s, 2), :] = src[k, x, 30:32, :]
-    zpack[0] = tiles[0]
-    zpack[1] = tiles[1]
-    low_rows[100:104, :] = jnp.zeros((4, 128), jnp.float32)
-    high_rows[100:104, :] = jnp.zeros((4, 128), jnp.float32)
+    zlow[...] = low.astype(jnp.bfloat16)
+    zhigh[...] = high.astype(jnp.bfloat16)
+    low_rows[100:112, :] = jnp.zeros((12, 128), jnp.float32)
+    high_rows[100:112, :] = jnp.zeros((12, 128), jnp.float32)
+
+
+def unpack_z(from_minus, from_plus, s):
+    shift = -(2 * s + 2)
+    return jnp.where(lanes_of() < 64, roll(from_plus, shift, 1), roll(from_minus, shift, 1))
+
+
+def pack_y_kernel(from_minus, from_plus, low_in, high_in, token, sides, low_rows, high_rows, low, high):
+    del token
+    low[...] = low_in[...]
+    high[...] = high_in[...]
+    for t, part in enumerate((from_minus, from_plus)):
+        sides[t] = part[...].astype(jnp.float32)
+        low[pl.ds(100 + 2 * t, 2), :] = sides[t, 0:2, :]
+        high[pl.ds(100 + 2 * t, 2), :] = sides[t, 30:32, :]
+    low_rows[...] = low[...].astype(jnp.bfloat16)
+    high_rows[...] = high[...].astype(jnp.bfloat16)
 
 
 def own_kernel(pop, ori, after, own, token):
@@ -286,17 +311,6 @@
                 own[19 + j, x, rows, :] = u[j]
             for k in range(6):
                 own[22 + k, x, rows, :] = ori[k, x, rows, :]
-
-
-def pack_y_kernel(from_minus, from_plus, low_in, high_in, token, sides, low_rows, high_rows):
-    lane = lax.broadcasted_iota(jnp.int32, (32, 128), 1)
-    low_rows[...] = low_in[...]
-    high_rows[...] = high_in[...]
-    for t in range(2):
-        both = jnp.where(lane % 4 < 2, from_minus[t], from_plus[t])
-        sides[t] = both
-        low_rows[pl.ds(100 + 2 * t, 2), :] = sides[t, 0:2, :]
-        high_rows[pl.ds(100 + 2 * t, 2), :] = sides[t, 30:32, :]
 
 
 def collide_group(raw, fields, x, t, r):
@@ -376,8 +390,7 @@
                 put(fields, (k, x, 0), r, own[k, x, rows, :])
 
             def raw(f):
-                s = 2 * f + x
-                return roll(sides[s // 32, rows, :], -(4 * (s % 32) + 2), 1)
+                return unpack_z(sides[0, rows, :], sides[1, rows, :], 2 * f + x)
 
             collide_group(raw, fields, x, 1, r)
     for x in range(2):
@@ -386,18 +399,20 @@
     message[...] = out[...].astype(jnp.bfloat16)
 
 
-def step_one_kernel(before, middle, from_yminus, from_yplus, fields, state, msg_low, msg_high, halo, out):
+def step_one_kernel(before, middle, from_yminus, from_yplus, fields, state, msg_low, msg_high, halo, out, got):
     del before
     low, high = walls()
+    got[0] = from_yminus[...].astype(jnp.float32)
+    got[1] = from_yplus[...].astype(jnp.float32)
     for s in range(52):
-        halo[s, 0:2, :] = from_yplus[pl.ds(2 * s, 2), :]
-        halo[s, 6:8, :] = from_yminus[pl.ds(2 * s, 2), :]
+        halo[s, 0:2, :] = got[1, pl.ds(2 * s, 2), :]
+        halo[s, 6:8, :] = got[0, pl.ds(2 * s, 2), :]
     for x in range(2):
         for t in range(2):
 
             def raw(f):
                 s = 2 * f + x
-                return halo[s] if t == 0 else roll(halo[50 + s // 32], -(4 * (s % 32) + 2), 1)
+                return halo[s] if t == 0 else unpack_z(halo[50], halo[51], s)
 
             collide_group(raw, fields, x, t, 4)
     for x in range(2):
@@ -627,15 +642,15 @@
         ],
         compiler_params=pltpu.CompilerParams(vmem_limit_bytes=LIMIT_WEIGHTS),
     )(w_in, b_in.reshape(1, 512), w_mid, b_mid.reshape(1, 512), w_out.T, b_out.reshape(1, 15))
-    zpack, low_raw, high_raw = pl.pallas_call(
+    zlow, zhigh, low_raw, high_raw = pl.pallas_call(
         pack_z_kernel,
-        out_shape=(shape(2, 32, 128), shape(104, 128), shape(104, 128)),
+        out_shape=(shape(32, 128, d=bf16), shape(32, 128, d=bf16), shape(112, 128), shape(112, 128)),
         in_specs=[hbm] * 2,
-        out_specs=(vmem,) * 3,
+        out_specs=(vmem,) * 4,
         scratch_shapes=[
             pltpu.VMEM((19, 2, 32, 128), f32),
             pltpu.VMEM((6, 2, 32, 128), f32),
-            pltpu.SemaphoreType.DMA((2,)),
+            pltpu.SemaphoreType.DMA((5,)),
         ],
         compiler_params=pltpu.CompilerParams(vmem_limit_bytes=LIMIT_PACK),
         cost_estimate=COST_PACK,
@@ -646,14 +661,15 @@
         in_specs=[vmem] * 3,
         out_specs=(vmem,) * 2,
         compiler_params=params,
-    )(populations, orientation, zpack)
-    from_minus = lax.ppermute(zpack, "gz", ring("gz", 1, False))
-    from_plus = lax.ppermute(zpack, "gz", ring("gz", -1, False))
+    )(populations, orientation, low_raw)
+    from_minus = lax.ppermute(zhigh, "gz", ring("gz", 1, False))
+    from_plus = lax.ppermute(zlow, "gz", ring("gz", -1, False))
     sides, low_rows, high_rows = pl.pallas_call(
         pack_y_kernel,
-        out_shape=(shape(2, 32, 128), shape(104, 128), shape(104, 128)),
+        out_shape=(shape(2, 32, 128), shape(112, 128, d=bf16), shape(112, 128, d=bf16)),
         in_specs=[vmem] * 5,
         out_specs=(vmem,) * 3,
+        scratch_shapes=[pltpu.VMEM((112, 128), f32), pltpu.VMEM((112, 128), f32)],
         compiler_params=params,
     )(from_minus, from_plus, low_raw, high_raw, token)
     fields_shape = shape(28, 2, 2, 64, 128)
@@ -677,7 +693,11 @@
         ),
         in_specs=[vmem] * 4,
         out_specs=(vmem,) * 4,
-        scratch_shapes=[pltpu.VMEM((52, 8, 128), f32), pltpu.VMEM((2, MSG_ROWS, 128), f32)],
+        scratch_shapes=[
+            pltpu.VMEM((52, 8, 128), f32),
+            pltpu.VMEM((2, MSG_ROWS, 128), f32),
+            pltpu.VMEM((2, 112, 128), f32),
+        ],
         input_output_aliases={0: 0},
         compiler_params=params,
     )(fields, middle, from_yminus, from_yplus)

time: 40.8 us -> 40.4 us (level)
  the two profiles are of different devices: /device:TPU:217 before, /device:TPU:219 now
where the time goes in v6:
time: 40.4 us; the launch traced here: 40.2 us
  starting transfers between devices  18.5 us (46%)
  waiting for transfers between devices  11.3 us (28%)
  Pallas kernels  9.58 us (24%)
  between operations  0.84 us (2%)
    ppermute x1, starting transfers between devices, local(): from_low = lax.ppermute(msg_high, 'gx', ring('gx', 1, True))  6.73 us
    pallas_call x1, Pallas kernels, local(): pl.pallas_call(step_two_kernel, out_shape=(shape(4, 2, 32, 128, d=bf16),...  5.16 us
    ppermute x1, starting transfers between devices, local(): from_yminus = lax.ppermute(high_rows, 'gy', ring('gy', 1, True))  4.41 us
    ppermute x1, waiting for transfers between devices, local(): from_high = lax.ppermute(msg_low, 'gx', ring('gx', -1, True))  3.69 us
    ppermute x1, starting transfers between devices, local(): from_minus = lax.ppermute(zhigh, 'gz', ring('gz', 1, False))  3.25 us
    ppermute x1, waiting for transfers between devices, local(): from_yplus = lax.ppermute(low_rows, 'gy', ring('gy', -1, True))  2.86 us
    ppermute x1, waiting for transfers between devices, local(): from_low = lax.ppermute(msg_high, 'gx', ring('gx', 1, True))  2.79 us
    ppermute x1, starting transfers between devices, local(): from_plus = lax.ppermute(zlow, 'gz', ring('gz', -1, False))  2.16 us
  transfers between devices with their start and end apart: 6, of which 4 were waited for; matrix products, arithmetic and copies ran while one was open for 0% of the time, Pallas kernels for 5%

profile of v6, /device:TPU:219, one launch (start us, length us, event | category | flops | bytes accessed | tf_op | source)
XLA Modules:
  0.0 40.2 jit_solution(5279208721734760404)
XLA Ops:
  0.6 0.0 copy-start
  0.6 0.0 copy-start.2
  0.6 1.6 %shard_map.104 = (bf16[32,128]{1,0:T(8,128)(2,1)S(1)}, bf16[32,128]{1,0:T(8,128)(2,1)S(1)}, f32[112,128]{1,0:T(8,128)S(1)}, f32[112,128]{1,0:T(8,128)S(1)}) custom-call(f32[19,2,32,128]{3,2,1,0:T(8,128)} %pop.1, f32[6,2,32,128]{3,2,1,0:T(8,128)} %ori.1), custom_call_target="tpu_custom_call" | custom-call | flops 10000000000 | bytes 10000000 | tf_op jit(solution)/shard_map/pallas_call | solution.py:645
  2.3 0.0 copy-start.1
  2.3 0.0 copy-start.3
  2.3 0.0 copy-start.4
  2.3 0.0 copy-start.5
  2.3 0.0 copy-start.6
  2.3 0.0 copy-start.8
  2.3 0.0 copy-start.7
  2.3 3.3 %collective-permute-start = (bf16[32,128]{1,0:T(8,128)(2,1)S(1)}, bf16[32,128]{1,0:T(8,128)(2,1)S(1)}, u32[]{:S(2)}, u32[]{:S(2)}) collective-permute-start(bf16[32,128]{1,0:T(8,128)(2,1)S(1)} %get-tuple-element.24), channel_id=1, source_target_pairs={{0,1},{1,2},{2,3},{4,5},{5,6},{6,7},{8,9},{9,10},{10,11},{12,13},{... | collective-permute-start | bytes 24584 | tf_op jit(solution)/shard_map/ppermute | solution.py:665
  5.6 2.2 %collective-permute-start.1 = (bf16[32,128]{1,0:T(8,128)(2,1)S(1)}, bf16[32,128]{1,0:T(8,128)(2,1)S(1)}, u32[]{:S(2)}, u32[]{:S(2)}) collective-permute-start(bf16[32,128]{1,0:T(8,128)(2,1)S(1)} %get-tuple-element.25), channel_id=1, source_target_pairs={{1,0},{2,1},{3,2},{5,4},{6,5},{7,6},{9,8},{10,9},{11,10},{13,12},{... | collective-permute-start | bytes 24584 | tf_op jit(solution)/shard_map/ppermute | solution.py:666
  7.8 0.0 copy-done
  7.8 0.0 copy-done.2
  7.8 0.3 shard_map.105
  8.1 0.0 collective-permute-done.from_minus
  8.1 1.9 %collective-permute-done.1.from_plus = bf16[32,128]{1,0:T(8,128)(2,1)S(1)} collective-permute-done((bf16[32,128]{1,0:T(8,128)(2,1)S(1)}, bf16[32,128]{1,0:T(8,128)(2,1)S(1)}, u32[]{:S(2)}, u32[]{:S(2)}) %collective-permute-start.1) | collective-permute-done | bytes 8224 | tf_op jit(solution)/shard_map/ppermute | solution.py:666
  10.0 4.4 %collective-permute-start.2 = (bf16[112,128]{1,0:T(8,128)(2,1)S(1)}, bf16[112,128]{1,0:T(8,128)(2,1)S(1)}, u32[]{:S(2)}, u32[]{:S(2)}) collective-permute-start(bf16[112,128]{1,0:T(8,128)(2,1)S(1)} %get-tuple-element.32), channel_id=1, source_target_pairs={{0,4},{4,8},{8,12},{12,16},{16,20},{20,24},{24,28},{28,0},{1,5},{5... | collective-permute-start | bytes 86024 | tf_op jit(solution)/shard_map/ppermute | solution.py:684
  14.4 1.9 %collective-permute-start.3 = (bf16[112,128]{1,0:T(8,128)(2,1)S(1)}, bf16[112,128]{1,0:T(8,128)(2,1)S(1)}, u32[]{:S(2)}, u32[]{:S(2)}) collective-permute-start(bf16[112,128]{1,0:T(8,128)(2,1)S(1)} %get-tuple-element.33), channel_id=1, source_target_pairs={{0,28},{4,0},{8,4},{12,8},{16,12},{20,16},{24,20},{28,24},{1,29},{... | collective-permute-start | bytes 86024 | tf_op jit(solution)/shard_map/ppermute | solution.py:685
  16.4 1.0 %shard_map.107 = (f32[28,2,2,64,128]{4,3,2,1,0:T(8,128)S(1)}, f32[2,38,2,16,128]{4,3,2,1,0:T(8,128)S(1)}, bf16[2,480,128]{2,1,0:T(8,128)(2,1)S(1)}) custom-call(f32[28,2,32,128]{3,2,1,0:T(8,128)S(1)} %get-tuple-element.23.own, f32[2,32,128]{2,1,0:T(8,128)S(1)} %get-tuple-element.28.sides), custom_call_target="tpu_custom_call" | custom-call | tf_op jit(solution)/shard_map/pallas_call | solution.py:676
  17.4 0.0 collective-permute-done.2.from_yminus
  17.4 2.9 %collective-permute-done.3.from_yplus = bf16[112,128]{1,0:T(8,128)(2,1)S(1)} collective-permute-done((bf16[112,128]{1,0:T(8,128)(2,1)S(1)}, bf16[112,128]{1,0:T(8,128)(2,1)S(1)}, u32[]{:S(2)}, u32[]{:S(2)}) %collective-permute-start.3) | collective-permute-done | bytes 28704 | tf_op jit(solution)/shard_map/ppermute | solution.py:685
  20.3 0.9 %shard_map.108 = (f32[28,2,2,64,128]{4,3,2,1,0:T(8,128)S(1)}, f32[2,38,2,24,128]{4,3,2,1,0:T(8,128)S(1)}, bf16[1072,128]{1,0:T(8,128)(2,1)S(1)}, bf16[1072,128]{1,0:T(8,128)(2,1)S(1)}) custom-call(f32[28,2,2,64,128]{4,3,2,1,0:T(8,128)S(1)} %get-tuple-element.30.before, ...), custom_call_target="tpu_custom_call", output_to_operand_aliasing={{0}: (0, {})} | custom-call | tf_op jit(solution)/shard_map/pallas_call | solution.py:686
  21.2 6.7 %collective-permute-start.4 = (bf16[1072,128]{1,0:T(8,128)(2,1)S(1)}, bf16[1072,128]{1,0:T(8,128)(2,1)S(1)}, u32[]{:S(2)}, u32[]{:S(2)}) collective-permute-start(bf16[1072,128]{1,0:T(8,128)(2,1)S(1)} %get-tuple-element.35), channel_id=1, source_target_pairs={{0,32},{32,64},{64,96},{96,128},{128,160},{160,192},{192,224},{224... | collective-permute-start | bytes 823304 | tf_op jit(solution)/shard_map/ppermute | solution.py:704
  27.9 0.0 collective-permute-start.5
  27.9 0.0 copy-done.1
  27.9 0.0 copy-done.3
  27.9 0.0 copy-done.4
  27.9 0.0 copy-done.5
  27.9 0.0 copy-done.6
  28.0 0.0 copy-done.8
  28.0 0.6 %shard_map.109 = (bf16[512,8]{1,0:T(8,128)(2,1)S(1)}, bf16[512,512]{1,0:T(8,128)(2,1)S(1)}, f32[512,128]{1,0:T(8,128)S(1)}, bf16[15,512]{1,0:T(8,128)(2,1)S(1)}, f32[16,128]{1,0:T(8,128)S(1)}) custom-call(bf16[6,512]{1,0:T(8,128)(2,1)S(1)} %copy-done.4, f32[1,512]{1,0:T(1,128)S(1)} %bitcast.8, bf16[512,512]{1,0:T(8,128)(2,1)S(1)} %copy-done.1, ...), custom_call_target="tpu_custom_call" | custom-call | tf_op jit(solution)/shard_map/pallas_call | solution.py:623
  28.6 2.8 %collective-permute-done.4.from_low = bf16[1072,128]{1,0:T(8,128)(2,1)S(1)} collective-permute-done((bf16[1072,128]{1,0:T(8,128)(2,1)S(1)}, bf16[1072,128]{1,0:T(8,128)(2,1)S(1)}, u32[]{:S(2)}, u32[]{:S(2)}) %collective-permute-start.4) | collective-permute-done | bytes 274464 | tf_op jit(solution)/shard_map/ppermute | solution.py:704
  31.4 3.7 %collective-permute-done.5.from_high = bf16[1072,128]{1,0:T(8,128)(2,1)S(1)} collective-permute-done((bf16[1072,128]{1,0:T(8,128)(2,1)S(1)}, bf16[1072,128]{1,0:T(8,128)(2,1)S(1)}, u32[]{:S(2)}, u32[]{:S(2)}) %collective-permute-start.5) | collective-permute-done | bytes 274464 | tf_op jit(solution)/shard_map/ppermute | solution.py:705
  35.0 0.0 copy-done.7
  35.1 5.2 %shard_map.110 = (bf16[4,2,32,128]{3,2,1,0:T(8,128)(2,1)}, bf16[15,2,32,128]{3,2,1,0:T(8,128)(2,1)}) custom-call(s32[2,1,32]{2,1,0:T(1,128)S(1)} %bitcast.10, f32[2,38,2,16,128]{4,3,2,1,0:T(8,128)S(1)} %get-tuple-element.29.state_mid, f32[2,38,2,24,128]{4,3,2,1,0:T(8,128)S(1)} %get-tuple-element.34.state_rim, ...), custom_call_target="tpu_custom_call" | custom-call | tf_op jit(solution)/shard_map/pallas_call | solution.py:706
  (1 shorter events, 0.0 us)
Async XLA Ops:
  0.6 7.1 %copy-start = (f32[19,2,32,128]{3,2,1,0:T(8,128)S(1)}, f32[19,2,32,128]{3,2,1,0:T(8,128)}, u32[]{:S(2)}) copy-start(f32[19,2,32,128]{3,2,1,0:T(8,128)} %pop.1) | copy-start | bytes 1867780
  0.6 7.1 %copy-start.2 = (f32[6,2,32,128]{3,2,1,0:T(8,128)S(1)}, f32[6,2,32,128]{3,2,1,0:T(8,128)}, u32[]{:S(2)}) copy-start(f32[6,2,32,128]{3,2,1,0:T(8,128)} %ori.1) | copy-start | bytes 589828
  2.3 25.7 %copy-start.1 = (bf16[512,512]{1,0:T(8,128)(2,1)S(1)}, bf16[512,512]{1,0:T(8,128)(2,1)}, u32[]{:S(2)}) copy-start(bf16[512,512]{1,0:T(8,128)(2,1)} %w_mid_hbm.1) | copy-start | bytes 1572868
  2.3 25.7 %copy-start.3 = (bf16[512,15]{0,1:T(8,128)(2,1)S(1)}, bf16[512,15]{0,1:T(8,128)(2,1)}, u32[]{:S(2)}) copy-start(bf16[512,15]{0,1:T(8,128)(2,1)} %param.16) | copy-start | bytes 46084
  2.3 25.6 %copy-start.4 = (bf16[6,512]{1,0:T(8,128)(2,1)S(1)}, bf16[6,512]{1,0:T(8,128)(2,1)}, u32[]{:S(2)}) copy-start(bf16[6,512]{1,0:T(8,128)(2,1)} %w_in_hbm.1) | copy-start | bytes 18436
  2.3 25.6 %copy-start.5 = (f32[512]{0:T(512)S(1)}, f32[512]{0:T(512)}, u32[]{:S(2)}) copy-start(f32[512]{0:T(512)} %param.13) | copy-start | bytes 6148
  2.3 25.6 %copy-start.6 = (f32[512]{0:T(512)S(1)}, f32[512]{0:T(512)}, u32[]{:S(2)}) copy-start(f32[512]{0:T(512)} %param.15) | copy-start | bytes 6148
  2.3 25.6 %copy-start.8 = (f32[15]{0:T(128)S(1)}, f32[15]{0:T(128)}, u32[]{:S(2)}) copy-start(f32[15]{0:T(128)} %param.17) | copy-start | bytes 184
  2.3 32.7 %copy-start.7 = (s32[2,32,1]{1,2,0:T(1,128)S(1)}, s32[2,32,1]{1,2,0:T(1,128)}, u32[]{:S(2)}) copy-start(s32[2,32,1]{1,2,0:T(1,128)} %param.11) | copy-start | bytes 772
  2.3 5.7 %collective-permute-start = (bf16[32,128]{1,0:T(8,128)(2,1)S(1)}, bf16[32,128]{1,0:T(8,128)(2,1)S(1)}, u32[]{:S(2)}, u32[]{:S(2)}) collective-permute-start(bf16[32,128]{1,0:T(8,128)(2,1)S(1)} %get-tuple-element.24), channel_id=1, source_target_pairs={{0,1},{1,2},{2,3},{4,5},{5,6},{6,7},{8,9},{9,10},{10,11},{12,13},{... | collective-permute-start | bytes 24584 | tf_op jit(solution)/shard_map/ppermute | solution.py:665
  5.6 4.4 %collective-permute-start.1 = (bf16[32,128]{1,0:T(8,128)(2,1)S(1)}, bf16[32,128]{1,0:T(8,128)(2,1)S(1)}, u32[]{:S(2)}, u32[]{:S(2)}) collective-permute-start(bf16[32,128]{1,0:T(8,128)(2,1)S(1)} %get-tuple-element.25), channel_id=1, source_target_pairs={{1,0},{2,1},{3,2},{5,4},{6,5},{7,6},{9,8},{10,9},{11,10},{13,12},{... | collective-permute-start | bytes 24584 | tf_op jit(solution)/shard_map/ppermute | solution.py:666
  10.0 7.4 %collective-permute-start.2 = (bf16[112,128]{1,0:T(8,128)(2,1)S(1)}, bf16[112,128]{1,0:T(8,128)(2,1)S(1)}, u32[]{:S(2)}, u32[]{:S(2)}) collective-permute-start(bf16[112,128]{1,0:T(8,128)(2,1)S(1)} %get-tuple-element.32), channel_id=1, source_target_pairs={{0,4},{4,8},{8,12},{12,16},{16,20},{20,24},{24,28},{28,0},{1,5},{5... | collective-permute-start | bytes 86024 | tf_op jit(solution)/shard_map/ppermute | solution.py:684
  14.4 5.8 %collective-permute-start.3 = (bf16[112,128]{1,0:T(8,128)(2,1)S(1)}, bf16[112,128]{1,0:T(8,128)(2,1)S(1)}, u32[]{:S(2)}, u32[]{:S(2)}) collective-permute-start(bf16[112,128]{1,0:T(8,128)(2,1)S(1)} %get-tuple-element.33), channel_id=1, source_target_pairs={{0,28},{4,0},{8,4},{12,8},{16,12},{20,16},{24,20},{28,24},{1,29},{... | collective-permute-start | bytes 86024 | tf_op jit(solution)/shard_map/ppermute | solution.py:685
  21.2 10.2 %collective-permute-start.4 = (bf16[1072,128]{1,0:T(8,128)(2,1)S(1)}, bf16[1072,128]{1,0:T(8,128)(2,1)S(1)}, u32[]{:S(2)}, u32[]{:S(2)}) collective-permute-start(bf16[1072,128]{1,0:T(8,128)(2,1)S(1)} %get-tuple-element.35), channel_id=1, source_target_pairs={{0,32},{32,64},{64,96},{96,128},{128,160},{160,192},{192,224},{224... | collective-permute-start | bytes 823304 | tf_op jit(solution)/shard_map/ppermute | solution.py:704
  27.9 7.1 %collective-permute-start.5 = (bf16[1072,128]{1,0:T(8,128)(2,1)S(1)}, bf16[1072,128]{1,0:T(8,128)(2,1)S(1)}, u32[]{:S(2)}, u32[]{:S(2)}) collective-permute-start(bf16[1072,128]{1,0:T(8,128)(2,1)S(1)} %get-tuple-element.36), channel_id=1, source_target_pairs={{0,480},{32,0},{64,32},{96,64},{128,96},{160,128},{192,160},{224,1... | collective-permute-start | bytes 823304 | tf_op jit(solution)/shard_map/ppermute | solution.py:705

commit v7 on v6

--- a/solution.py
+++ b/solution.py
@@ -399,7 +399,7 @@
     message[...] = out[...].astype(jnp.bfloat16)
 
 
-def step_one_kernel(before, middle, from_yminus, from_yplus, fields, state, msg_low, msg_high, halo, out, got):
+def step_one_kernel(before, middle, from_yminus, from_yplus, fields, state, msg_off, msg_on, halo, out, got):
     del before
     low, high = walls()
     got[0] = from_yminus[...].astype(jnp.float32)
@@ -419,7 +419,8 @@
         for r in (0, 3, 4):
             advance_group(fields, state, out, x, r, low, high)
         out[x, pl.ds(CORNER_AT + 8, 8), :] = jnp.zeros((8, 128), jnp.float32)
-    for x, msg in enumerate((msg_low, msg_high)):
+    odd = lax.axis_index("gx") % 2
+    for x, msg in ((odd, msg_off), (1 - odd, msg_on)):
         msg[0:MID_ROWS, :] = middle[x]
         msg[MID_ROWS:MSG_ROWS, :] = out[x, MID_ROWS:MSG_ROWS, :].astype(jnp.bfloat16)
 
@@ -454,12 +455,13 @@
 
 
 def step_two_kernel(
-    slots, state_mid, state_rim, from_low, from_high, w_one, w_mid, b_mid, w_out, b_out, flow, closure,
+    slots, state_mid, state_rim, from_off, from_on, w_one, w_mid, b_mid, w_out, b_out, flow, closure,
     got, fields, near, level, feats, spread, place,
 ):
     low, high = walls()
-    got[0] = from_low[...].astype(jnp.float32)
-    got[1] = from_high[...].astype(jnp.float32)
+    odd = lax.axis_index("gx") % 2
+    got[odd] = from_off[...].astype(jnp.float32)
+    got[1 - odd] = from_on[...].astype(jnp.float32)
     for s in range(17):
         place[s] = 64
     for b in range(64):
@@ -683,7 +685,7 @@
     )(own, sides)
     from_yminus = lax.ppermute(high_rows, "gy", ring("gy", 1, True))
     from_yplus = lax.ppermute(low_rows, "gy", ring("gy", -1, True))
-    fields, state_rim, msg_low, msg_high = pl.pallas_call(
+    fields, state_rim, msg_off, msg_on = pl.pallas_call(
         step_one_kernel,
         out_shape=(
             fields_shape,
@@ -701,8 +703,11 @@
         input_output_aliases={0: 0},
         compiler_params=params,
     )(fields, middle, from_yminus, from_yplus)
-    from_low = lax.ppermute(msg_high, "gx", ring("gx", 1, True))
-    from_high = lax.ppermute(msg_low, "gx", ring("gx", -1, True))
+    x_count = lax.axis_size("gx")
+    off_chip = [(i, (i + (1 if i % 2 else -1)) % x_count) for i in range(x_count)]
+    on_chip = [(i, i + (-1 if i % 2 else 1)) for i in range(x_count)]
+    from_on = lax.ppermute(msg_on, "gx", on_chip)
+    from_off = lax.ppermute(msg_off, "gx", off_chip)
     return pl.pallas_call(
         step_two_kernel,
         out_shape=(shape(4, 2, 32, 128, d=bf16), shape(15, 2, 32, 128, d=bf16)),
@@ -718,7 +723,7 @@
             pltpu.SMEM((17,), jnp.int32),
         ],
         compiler_params=params,
-    )(slots, state_mid, state_rim, from_low, from_high, w_one, w_two, bias_mid, w_three, bias_out)
+    )(slots, state_mid, state_rim, from_off, from_on, w_one, w_two, bias_mid, w_three, bias_out)
 
 
 def solution(mesh):

time: 40.4 us -> 41.4 us (1.025)
  the two profiles are of different devices: /device:TPU:219 before, /device:TPU:24 now
where the time goes in v7:
time: 41.4 us; the launch traced here: 41.1 us
  starting transfers between devices  20.9 us (50%)
  Pallas kernels  9.79 us (24%)
  waiting for transfers between devices  9.54 us (23%)
  between operations  0.86 us (2%)
    ppermute x1, starting transfers between devices, local(): from_off = lax.ppermute(msg_off, 'gx', off_chip)  7.54 us
    pallas_call x1, Pallas kernels, local(): pl.pallas_call(step_two_kernel, out_shape=(shape(4, 2, 32, 128, d=bf16),...  5.3 us
    ppermute x1, starting transfers between devices, local(): from_yminus = lax.ppermute(high_rows, 'gy', ring('gy', 1, True))  4.69 us
    ppermute x1, waiting for transfers between devices, local(): from_yplus = lax.ppermute(low_rows, 'gy', ring('gy', -1, True))  4.01 us
    ppermute x1, waiting for transfers between devices, local(): from_plus = lax.ppermute(zlow, 'gz', ring('gz', -1, False))  3.94 us
    ppermute x1, starting transfers between devices, local(): from_minus = lax.ppermute(zhigh, 'gz', ring('gz', 1, False))  3.53 us
    ppermute x1, starting transfers between devices, local(): from_on = lax.ppermute(msg_on, 'gx', on_chip)  1.92 us
    ppermute x1, starting transfers between devices, local(): from_yplus = lax.ppermute(low_rows, 'gy', ring('gy', -1, True))  1.92 us
  transfers between devices with their start and end apart: 6, of which 3 were waited for; matrix products, arithmetic and copies ran while one was open for 0% of the time, Pallas kernels for 5%

profile of v7, /device:TPU:24, one launch (start us, length us, event | category | flops | bytes accessed | tf_op | source)
XLA Modules:
  0.0 41.1 jit_solution(11501777770050049450)
XLA Ops:
  0.6 0.0 copy-start
  0.6 0.0 copy-start.2
  0.6 1.6 %shard_map.104 = (bf16[32,128]{1,0:T(8,128)(2,1)S(1)}, bf16[32,128]{1,0:T(8,128)(2,1)S(1)}, f32[112,128]{1,0:T(8,128)S(1)}, f32[112,128]{1,0:T(8,128)S(1)}) custom-call(f32[19,2,32,128]{3,2,1,0:T(8,128)} %pop.1, f32[6,2,32,128]{3,2,1,0:T(8,128)} %ori.1), custom_call_target="tpu_custom_call" | custom-call | flops 10000000000 | bytes 10000000 | tf_op jit(solution)/shard_map/pallas_call | solution.py:647
  2.3 0.0 copy-start.1
  2.3 0.0 copy-start.3
  2.3 0.0 copy-start.4
  2.3 0.0 copy-start.5
  2.3 0.0 copy-start.6
  2.3 0.0 copy-start.8
  2.3 0.0 copy-start.7
  2.3 3.5 %collective-permute-start = (bf16[32,128]{1,0:T(8,128)(2,1)S(1)}, bf16[32,128]{1,0:T(8,128)(2,1)S(1)}, u32[]{:S(2)}, u32[]{:S(2)}) collective-permute-start(bf16[32,128]{1,0:T(8,128)(2,1)S(1)} %get-tuple-element.24), channel_id=1, source_target_pairs={{0,1},{1,2},{2,3},{4,5},{5,6},{6,7},{8,9},{9,10},{10,11},{12,13},{... | collective-permute-start | bytes 24584 | tf_op jit(solution)/shard_map/ppermute | solution.py:667
  5.9 1.3 %collective-permute-start.1 = (bf16[32,128]{1,0:T(8,128)(2,1)S(1)}, bf16[32,128]{1,0:T(8,128)(2,1)S(1)}, u32[]{:S(2)}, u32[]{:S(2)}) collective-permute-start(bf16[32,128]{1,0:T(8,128)(2,1)S(1)} %get-tuple-element.25), channel_id=1, source_target_pairs={{1,0},{2,1},{3,2},{5,4},{6,5},{7,6},{9,8},{10,9},{11,10},{13,12},{... | collective-permute-start | bytes 24584 | tf_op jit(solution)/shard_map/ppermute | solution.py:668
  7.2 0.0 copy-done
  7.2 0.0 copy-done.2
  7.2 0.3 shard_map.105
  7.5 0.0 collective-permute-done.from_minus
  7.5 3.9 %collective-permute-done.1.from_plus = bf16[32,128]{1,0:T(8,128)(2,1)S(1)} collective-permute-done((bf16[32,128]{1,0:T(8,128)(2,1)S(1)}, bf16[32,128]{1,0:T(8,128)(2,1)S(1)}, u32[]{:S(2)}, u32[]{:S(2)}) %collective-permute-start.1) | collective-permute-done | bytes 8224 | tf_op jit(solution)/shard_map/ppermute | solution.py:668
  11.4 4.7 %collective-permute-start.2 = (bf16[112,128]{1,0:T(8,128)(2,1)S(1)}, bf16[112,128]{1,0:T(8,128)(2,1)S(1)}, u32[]{:S(2)}, u32[]{:S(2)}) collective-permute-start(bf16[112,128]{1,0:T(8,128)(2,1)S(1)} %get-tuple-element.32), channel_id=1, source_target_pairs={{0,4},{4,8},{8,12},{12,16},{16,20},{20,24},{24,28},{28,0},{1,5},{5... | collective-permute-start | bytes 86024 | tf_op jit(solution)/shard_map/ppermute | solution.py:686
  16.1 1.9 %collective-permute-start.3 = (bf16[112,128]{1,0:T(8,128)(2,1)S(1)}, bf16[112,128]{1,0:T(8,128)(2,1)S(1)}, u32[]{:S(2)}, u32[]{:S(2)}) collective-permute-start(bf16[112,128]{1,0:T(8,128)(2,1)S(1)} %get-tuple-element.33), channel_id=1, source_target_pairs={{0,28},{4,0},{8,4},{12,8},{16,12},{20,16},{24,20},{28,24},{1,29},{... | collective-permute-start | bytes 86024 | tf_op jit(solution)/shard_map/ppermute | solution.py:687
  18.1 1.0 %shard_map.107 = (f32[28,2,2,64,128]{4,3,2,1,0:T(8,128)S(1)}, f32[2,38,2,16,128]{4,3,2,1,0:T(8,128)S(1)}, bf16[2,480,128]{2,1,0:T(8,128)(2,1)S(1)}) custom-call(f32[28,2,32,128]{3,2,1,0:T(8,128)S(1)} %get-tuple-element.23.own, f32[2,32,128]{2,1,0:T(8,128)S(1)} %get-tuple-element.28.sides), custom_call_target="tpu_custom_call" | custom-call | tf_op jit(solution)/shard_map/pallas_call | solution.py:678
  19.1 0.0 collective-permute-done.2.from_yminus
  19.1 4.0 %collective-permute-done.3.from_yplus = bf16[112,128]{1,0:T(8,128)(2,1)S(1)} collective-permute-done((bf16[112,128]{1,0:T(8,128)(2,1)S(1)}, bf16[112,128]{1,0:T(8,128)(2,1)S(1)}, u32[]{:S(2)}, u32[]{:S(2)}) %collective-permute-start.3) | collective-permute-done | bytes 28704 | tf_op jit(solution)/shard_map/ppermute | solution.py:687
  23.1 1.0 %shard_map.108 = (f32[28,2,2,64,128]{4,3,2,1,0:T(8,128)S(1)}, f32[2,38,2,24,128]{4,3,2,1,0:T(8,128)S(1)}, bf16[1072,128]{1,0:T(8,128)(2,1)S(1)}, bf16[1072,128]{1,0:T(8,128)(2,1)S(1)}) custom-call(f32[28,2,2,64,128]{4,3,2,1,0:T(8,128)S(1)} %get-tuple-element.30.before, ...), custom_call_target="tpu_custom_call", output_to_operand_aliasing={{0}: (0, {})} | custom-call | tf_op jit(solution)/shard_map/pallas_call | solution.py:688
  24.1 7.5 %collective-permute-start.4 = (bf16[1072,128]{1,0:T(8,128)(2,1)S(1)}, bf16[1072,128]{1,0:T(8,128)(2,1)S(1)}, u32[]{:S(2)}, u32[]{:S(2)}) collective-permute-start(bf16[1072,128]{1,0:T(8,128)(2,1)S(1)} %get-tuple-element.35), channel_id=1, source_target_pairs={{0,480},{32,64},{64,32},{96,128},{128,96},{160,192},{192,160},{224... | collective-permute-start | bytes 823304 | tf_op jit(solution)/shard_map/ppermute | solution.py:710
  31.6 1.9 %collective-permute-start.5 = (bf16[1072,128]{1,0:T(8,128)(2,1)S(1)}, bf16[1072,128]{1,0:T(8,128)(2,1)S(1)}, u32[]{:S(2)}, u32[]{:S(2)}) collective-permute-start(bf16[1072,128]{1,0:T(8,128)(2,1)S(1)} %get-tuple-element.36), channel_id=1, source_target_pairs={{0,32},{32,0},{64,96},{96,64},{128,160},{160,128},{192,224},{224,1... | collective-permute-start | bytes 823304 | tf_op jit(solution)/shard_map/ppermute | solution.py:709
  33.6 0.0 copy-done.1
  33.6 0.0 copy-done.3
  33.6 0.0 copy-done.4
  33.6 0.0 copy-done.5
  33.6 0.0 copy-done.6
  33.6 0.0 copy-done.8
  33.6 0.6 %shard_map.109 = (bf16[512,8]{1,0:T(8,128)(2,1)S(1)}, bf16[512,512]{1,0:T(8,128)(2,1)S(1)}, f32[512,128]{1,0:T(8,128)S(1)}, bf16[15,512]{1,0:T(8,128)(2,1)S(1)}, f32[16,128]{1,0:T(8,128)S(1)}) custom-call(bf16[6,512]{1,0:T(8,128)(2,1)S(1)} %copy-done.4, f32[1,512]{1,0:T(1,128)S(1)} %bitcast.8, bf16[512,512]{1,0:T(8,128)(2,1)S(1)} %copy-done.1, ...), custom_call_target="tpu_custom_call" | custom-call | tf_op jit(solution)/shard_map/pallas_call | solution.py:625
  34.2 1.6 %collective-permute-done.4.from_off = bf16[1072,128]{1,0:T(8,128)(2,1)S(1)} collective-permute-done((bf16[1072,128]{1,0:T(8,128)(2,1)S(1)}, bf16[1072,128]{1,0:T(8,128)(2,1)S(1)}, u32[]{:S(2)}, u32[]{:S(2)}) %collective-permute-start.4) | collective-permute-done | bytes 274464 | tf_op jit(solution)/shard_map/ppermute | solution.py:710
  35.8 0.0 collective-permute-done.5.from_on
  35.8 0.0 copy-done.7
  35.8 5.3 %shard_map.110 = (bf16[4,2,32,128]{3,2,1,0:T(8,128)(2,1)}, bf16[15,2,32,128]{3,2,1,0:T(8,128)(2,1)}) custom-call(s32[2,1,32]{2,1,0:T(1,128)S(1)} %bitcast.10, f32[2,38,2,16,128]{4,3,2,1,0:T(8,128)S(1)} %get-tuple-element.29.state_mid, f32[2,38,2,24,128]{4,3,2,1,0:T(8,128)S(1)} %get-tuple-element.34.state_rim, ...), custom_call_target="tpu_custom_call" | custom-call | tf_op jit(solution)/shard_map/pallas_call | solution.py:711
  (1 shorter events, 0.0 us)
Async XLA Ops:
  0.6 6.5 %copy-start = (f32[19,2,32,128]{3,2,1,0:T(8,128)S(1)}, f32[19,2,32,128]{3,2,1,0:T(8,128)}, u32[]{:S(2)}) copy-start(f32[19,2,32,128]{3,2,1,0:T(8,128)} %pop.1) | copy-start | bytes 1867780
  0.6 6.5 %copy-start.2 = (f32[6,2,32,128]{3,2,1,0:T(8,128)S(1)}, f32[6,2,32,128]{3,2,1,0:T(8,128)}, u32[]{:S(2)}) copy-start(f32[6,2,32,128]{3,2,1,0:T(8,128)} %ori.1) | copy-start | bytes 589828
  2.3 31.3 %copy-start.1 = (bf16[512,512]{1,0:T(8,128)(2,1)S(1)}, bf16[512,512]{1,0:T(8,128)(2,1)}, u32[]{:S(2)}) copy-start(bf16[512,512]{1,0:T(8,128)(2,1)} %w_mid_hbm.1) | copy-start | bytes 1572868
  2.3 31.3 %copy-start.3 = (bf16[512,15]{0,1:T(8,128)(2,1)S(1)}, bf16[512,15]{0,1:T(8,128)(2,1)}, u32[]{:S(2)}) copy-start(bf16[512,15]{0,1:T(8,128)(2,1)} %param.16) | copy-start | bytes 46084
  2.3 31.3 %copy-start.4 = (bf16[6,512]{1,0:T(8,128)(2,1)S(1)}, bf16[6,512]{1,0:T(8,128)(2,1)}, u32[]{:S(2)}) copy-start(bf16[6,512]{1,0:T(8,128)(2,1)} %w_in_hbm.1) | copy-start | bytes 18436
  2.3 31.3 %copy-start.5 = (f32[512]{0:T(512)S(1)}, f32[512]{0:T(512)}, u32[]{:S(2)}) copy-start(f32[512]{0:T(512)} %param.13) | copy-start | bytes 6148
  2.3 31.3 %copy-start.6 = (f32[512]{0:T(512)S(1)}, f32[512]{0:T(512)}, u32[]{:S(2)}) copy-start(f32[512]{0:T(512)} %param.15) | copy-start | bytes 6148
  2.3 31.3 %copy-start.8 = (f32[15]{0:T(128)S(1)}, f32[15]{0:T(128)}, u32[]{:S(2)}) copy-start(f32[15]{0:T(128)} %param.17) | copy-start | bytes 184
  2.3 33.5 %copy-start.7 = (s32[2,32,1]{1,2,0:T(1,128)S(1)}, s32[2,32,1]{1,2,0:T(1,128)}, u32[]{:S(2)}) copy-start(s32[2,32,1]{1,2,0:T(1,128)} %param.11) | copy-start | bytes 772
  2.3 5.1 %collective-permute-start = (bf16[32,128]{1,0:T(8,128)(2,1)S(1)}, bf16[32,128]{1,0:T(8,128)(2,1)S(1)}, u32[]{:S(2)}, u32[]{:S(2)}) collective-permute-start(bf16[32,128]{1,0:T(8,128)(2,1)S(1)} %get-tuple-element.24), channel_id=1, source_target_pairs={{0,1},{1,2},{2,3},{4,5},{5,6},{6,7},{8,9},{9,10},{10,11},{12,13},{... | collective-permute-start | bytes 24584 | tf_op jit(solution)/shard_map/ppermute | solution.py:667
  5.9 5.5 %collective-permute-start.1 = (bf16[32,128]{1,0:T(8,128)(2,1)S(1)}, bf16[32,128]{1,0:T(8,128)(2,1)S(1)}, u32[]{:S(2)}, u32[]{:S(2)}) collective-permute-start(bf16[32,128]{1,0:T(8,128)(2,1)S(1)} %get-tuple-element.25), channel_id=1, source_target_pairs={{1,0},{2,1},{3,2},{5,4},{6,5},{7,6},{9,8},{10,9},{11,10},{13,12},{... | collective-permute-start | bytes 24584 | tf_op jit(solution)/shard_map/ppermute | solution.py:668
  11.4 7.7 %collective-permute-start.2 = (bf16[112,128]{1,0:T(8,128)(2,1)S(1)}, bf16[112,128]{1,0:T(8,128)(2,1)S(1)}, u32[]{:S(2)}, u32[]{:S(2)}) collective-permute-start(bf16[112,128]{1,0:T(8,128)(2,1)S(1)} %get-tuple-element.32), channel_id=1, source_target_pairs={{0,4},{4,8},{8,12},{12,16},{16,20},{20,24},{24,28},{28,0},{1,5},{5... | collective-permute-start | bytes 86024 | tf_op jit(solution)/shard_map/ppermute | solution.py:686
  16.1 7.0 %collective-permute-start.3 = (bf16[112,128]{1,0:T(8,128)(2,1)S(1)}, bf16[112,128]{1,0:T(8,128)(2,1)S(1)}, u32[]{:S(2)}, u32[]{:S(2)}) collective-permute-start(bf16[112,128]{1,0:T(8,128)(2,1)S(1)} %get-tuple-element.33), channel_id=1, source_target_pairs={{0,28},{4,0},{8,4},{12,8},{16,12},{20,16},{24,20},{28,24},{1,29},{... | collective-permute-start | bytes 86024 | tf_op jit(solution)/shard_map/ppermute | solution.py:687
  24.1 11.7 %collective-permute-start.4 = (bf16[1072,128]{1,0:T(8,128)(2,1)S(1)}, bf16[1072,128]{1,0:T(8,128)(2,1)S(1)}, u32[]{:S(2)}, u32[]{:S(2)}) collective-permute-start(bf16[1072,128]{1,0:T(8,128)(2,1)S(1)} %get-tuple-element.35), channel_id=1, source_target_pairs={{0,480},{32,64},{64,32},{96,128},{128,96},{160,192},{192,160},{224... | collective-permute-start | bytes 823304 | tf_op jit(solution)/shard_map/ppermute | solution.py:710
  31.6 4.2 %collective-permute-start.5 = (bf16[1072,128]{1,0:T(8,128)(2,1)S(1)}, bf16[1072,128]{1,0:T(8,128)(2,1)S(1)}, u32[]{:S(2)}, u32[]{:S(2)}) collective-permute-start(bf16[1072,128]{1,0:T(8,128)(2,1)S(1)} %get-tuple-element.36), channel_id=1, source_target_pairs={{0,32},{32,0},{64,96},{96,64},{128,160},{160,128},{192,224},{224,1... | collective-permute-start | bytes 823304 | tf_op jit(solution)/shard_map/ppermute | solution.py:709

commit v8 on v7

--- a/solution.py
+++ b/solution.py
@@ -455,7 +455,7 @@
 
 
 def step_two_kernel(
-    slots, state_mid, state_rim, from_off, from_on, w_one, w_mid, b_mid, w_out, b_out, flow, closure,
+    slots, state_mid, state_rim, from_on, from_off, w_one, w_mid, b_mid, w_out, b_out, flow, closure,
     got, fields, near, level, feats, spread, place,
 ):
     low, high = walls()
@@ -723,7 +723,7 @@
             pltpu.SMEM((17,), jnp.int32),
         ],
         compiler_params=params,
-    )(slots, state_mid, state_rim, from_off, from_on, w_one, w_two, bias_mid, w_three, bias_out)
+    )(slots, state_mid, state_rim, from_on, from_off, w_one, w_two, bias_mid, w_three, bias_out)
 
 
 def solution(mesh):

time: 41.4 us -> 46.8 us (1.13)
  starting transfers between devices: 20.9 us -> 24.4 us
  waiting for transfers between devices: 9.54 us -> 11.5 us
    ppermute x1, starting transfers between devices: 7.54 us -> 11.1 us  [local(): from_off = lax.ppermute(msg_off, 'gx', off_chip)]
    ppermute x1, waiting for transfers between devices: 1.57 us -> 3.49 us  [local(): from_off = lax.ppermute(msg_off, 'gx', off_chip)]
  transfers between devices with their start and end apart: 6 -> 6, of which waited for: 3 -> 3; matrix products, arithmetic and copies ran while one was open for 0% -> 0% of each run, Pallas kernels for 5% -> 4%
where the time goes in v8:
time: 46.8 us; the launch traced here: 46.6 us
  starting transfers between devices  24.4 us (52%)
  waiting for transfers between devices  11.5 us (25%)
  Pallas kernels  9.79 us (21%)
  between operations  0.87 us (2%)
    ppermute x1, starting transfers between devices, local(): from_off = lax.ppermute(msg_off, 'gx', off_chip)  11.1 us
    pallas_call x1, Pallas kernels, local(): pl.pallas_call(step_two_kernel, out_shape=(shape(4, 2, 32, 128, d=bf16),...  5.3 us
    ppermute x1, starting transfers between devices, local(): from_yminus = lax.ppermute(high_rows, 'gy', ring('gy', 1, True))  4.69 us
    ppermute x1, waiting for transfers between devices, local(): from_yplus = lax.ppermute(low_rows, 'gy', ring('gy', -1, True))  4.01 us
    ppermute x1, waiting for transfers between devices, local(): from_plus = lax.ppermute(zlow, 'gz', ring('gz', -1, False))  3.94 us
    ppermute x1, starting transfers between devices, local(): from_minus = lax.ppermute(zhigh, 'gz', ring('gz', 1, False))  3.53 us
    ppermute x1, waiting for transfers between devices, local(): from_off = lax.ppermute(msg_off, 'gx', off_chip)  3.49 us
    ppermute x1, starting transfers between devices, local(): from_on = lax.ppermute(msg_on, 'gx', on_chip)  1.92 us
  transfers between devices with their start and end apart: 6, of which 3 were waited for; matrix products, arithmetic and copies ran while one was open for 0% of the time, Pallas kernels for 4%

profile of v8, /device:TPU:24, one launch (start us, length us, event | category | flops | bytes accessed | tf_op | source)
XLA Modules:
  0.0 46.6 jit_solution(12592950638250146303)
XLA Ops:
  0.6 0.0 copy-start
  0.6 0.0 copy-start.2
  0.6 1.6 %shard_map.104 = (bf16[32,128]{1,0:T(8,128)(2,1)S(1)}, bf16[32,128]{1,0:T(8,128)(2,1)S(1)}, f32[112,128]{1,0:T(8,128)S(1)}, f32[112,128]{1,0:T(8,128)S(1)}) custom-call(f32[19,2,32,128]{3,2,1,0:T(8,128)} %pop.1, f32[6,2,32,128]{3,2,1,0:T(8,128)} %ori.1), custom_call_target="tpu_custom_call" | custom-call | flops 10000000000 | bytes 10000000 | tf_op jit(solution)/shard_map/pallas_call | solution.py:647
  2.3 0.0 copy-start.1
  2.3 0.0 copy-start.3
  2.3 0.0 copy-start.4
  2.3 0.0 copy-start.5
  2.3 0.0 copy-start.6
  2.3 0.0 copy-start.8
  2.3 0.0 copy-start.7
  2.3 3.5 %collective-permute-start = (bf16[32,128]{1,0:T(8,128)(2,1)S(1)}, bf16[32,128]{1,0:T(8,128)(2,1)S(1)}, u32[]{:S(2)}, u32[]{:S(2)}) collective-permute-start(bf16[32,128]{1,0:T(8,128)(2,1)S(1)} %get-tuple-element.24), channel_id=1, source_target_pairs={{0,1},{1,2},{2,3},{4,5},{5,6},{6,7},{8,9},{9,10},{10,11},{12,13},{... | collective-permute-start | bytes 24584 | tf_op jit(solution)/shard_map/ppermute | solution.py:667
  5.9 1.3 %collective-permute-start.1 = (bf16[32,128]{1,0:T(8,128)(2,1)S(1)}, bf16[32,128]{1,0:T(8,128)(2,1)S(1)}, u32[]{:S(2)}, u32[]{:S(2)}) collective-permute-start(bf16[32,128]{1,0:T(8,128)(2,1)S(1)} %get-tuple-element.25), channel_id=1, source_target_pairs={{1,0},{2,1},{3,2},{5,4},{6,5},{7,6},{9,8},{10,9},{11,10},{13,12},{... | collective-permute-start | bytes 24584 | tf_op jit(solution)/shard_map/ppermute | solution.py:668
  7.2 0.0 copy-done
  7.2 0.0 copy-done.2
  7.2 0.3 shard_map.105
  7.5 0.0 collective-permute-done.from_minus
  7.5 3.9 %collective-permute-done.1.from_plus = bf16[32,128]{1,0:T(8,128)(2,1)S(1)} collective-permute-done((bf16[32,128]{1,0:T(8,128)(2,1)S(1)}, bf16[32,128]{1,0:T(8,128)(2,1)S(1)}, u32[]{:S(2)}, u32[]{:S(2)}) %collective-permute-start.1) | collective-permute-done | bytes 8224 | tf_op jit(solution)/shard_map/ppermute | solution.py:668
  11.4 4.7 %collective-permute-start.2 = (bf16[112,128]{1,0:T(8,128)(2,1)S(1)}, bf16[112,128]{1,0:T(8,128)(2,1)S(1)}, u32[]{:S(2)}, u32[]{:S(2)}) collective-permute-start(bf16[112,128]{1,0:T(8,128)(2,1)S(1)} %get-tuple-element.32), channel_id=1, source_target_pairs={{0,4},{4,8},{8,12},{12,16},{16,20},{20,24},{24,28},{28,0},{1,5},{5... | collective-permute-start | bytes 86024 | tf_op jit(solution)/shard_map/ppermute | solution.py:686
  16.1 1.9 %collective-permute-start.3 = (bf16[112,128]{1,0:T(8,128)(2,1)S(1)}, bf16[112,128]{1,0:T(8,128)(2,1)S(1)}, u32[]{:S(2)}, u32[]{:S(2)}) collective-permute-start(bf16[112,128]{1,0:T(8,128)(2,1)S(1)} %get-tuple-element.33), channel_id=1, source_target_pairs={{0,28},{4,0},{8,4},{12,8},{16,12},{20,16},{24,20},{28,24},{1,29},{... | collective-permute-start | bytes 86024 | tf_op jit(solution)/shard_map/ppermute | solution.py:687
  18.1 1.0 %shard_map.107 = (f32[28,2,2,64,128]{4,3,2,1,0:T(8,128)S(1)}, f32[2,38,2,16,128]{4,3,2,1,0:T(8,128)S(1)}, bf16[2,480,128]{2,1,0:T(8,128)(2,1)S(1)}) custom-call(f32[28,2,32,128]{3,2,1,0:T(8,128)S(1)} %get-tuple-element.23.own, f32[2,32,128]{2,1,0:T(8,128)S(1)} %get-tuple-element.28.sides), custom_call_target="tpu_custom_call" | custom-call | tf_op jit(solution)/shard_map/pallas_call | solution.py:678
  19.1 0.0 collective-permute-done.2.from_yminus
  19.1 4.0 %collective-permute-done.3.from_yplus = bf16[112,128]{1,0:T(8,128)(2,1)S(1)} collective-permute-done((bf16[112,128]{1,0:T(8,128)(2,1)S(1)}, bf16[112,128]{1,0:T(8,128)(2,1)S(1)}, u32[]{:S(2)}, u32[]{:S(2)}) %collective-permute-start.3) | collective-permute-done | bytes 28704 | tf_op jit(solution)/shard_map/ppermute | solution.py:687
  23.1 1.0 %shard_map.108 = (f32[28,2,2,64,128]{4,3,2,1,0:T(8,128)S(1)}, f32[2,38,2,24,128]{4,3,2,1,0:T(8,128)S(1)}, bf16[1072,128]{1,0:T(8,128)(2,1)S(1)}, bf16[1072,128]{1,0:T(8,128)(2,1)S(1)}) custom-call(f32[28,2,2,64,128]{4,3,2,1,0:T(8,128)S(1)} %get-tuple-element.30.before, ...), custom_call_target="tpu_custom_call", output_to_operand_aliasing={{0}: (0, {})} | custom-call | tf_op jit(solution)/shard_map/pallas_call | solution.py:688
  24.1 1.9 %collective-permute-start.4 = (bf16[1072,128]{1,0:T(8,128)(2,1)S(1)}, bf16[1072,128]{1,0:T(8,128)(2,1)S(1)}, u32[]{:S(2)}, u32[]{:S(2)}) collective-permute-start(bf16[1072,128]{1,0:T(8,128)(2,1)S(1)} %get-tuple-element.35), channel_id=1, source_target_pairs={{0,32},{32,0},{64,96},{96,64},{128,160},{160,128},{192,224},{224,1... | collective-permute-start | bytes 823304 | tf_op jit(solution)/shard_map/ppermute | solution.py:709
  26.0 11.1 %collective-permute-start.5 = (bf16[1072,128]{1,0:T(8,128)(2,1)S(1)}, bf16[1072,128]{1,0:T(8,128)(2,1)S(1)}, u32[]{:S(2)}, u32[]{:S(2)}) collective-permute-start(bf16[1072,128]{1,0:T(8,128)(2,1)S(1)} %get-tuple-element.36), channel_id=1, source_target_pairs={{0,480},{32,64},{64,32},{96,128},{128,96},{160,192},{192,160},{224... | collective-permute-start | bytes 823304 | tf_op jit(solution)/shard_map/ppermute | solution.py:710
  37.1 0.0 copy-done.1
  37.1 0.0 copy-done.3
  37.1 0.0 copy-done.4
  37.1 0.0 copy-done.5
  37.1 0.0 copy-done.6
  37.1 0.0 copy-done.8
  37.1 0.6 %shard_map.109 = (bf16[512,8]{1,0:T(8,128)(2,1)S(1)}, bf16[512,512]{1,0:T(8,128)(2,1)S(1)}, f32[512,128]{1,0:T(8,128)S(1)}, bf16[15,512]{1,0:T(8,128)(2,1)S(1)}, f32[16,128]{1,0:T(8,128)S(1)}) custom-call(bf16[6,512]{1,0:T(8,128)(2,1)S(1)} %copy-done.4, f32[1,512]{1,0:T(1,128)S(1)} %bitcast.8, bf16[512,512]{1,0:T(8,128)(2,1)S(1)} %copy-done.1, ...), custom_call_target="tpu_custom_call" | custom-call | tf_op jit(solution)/shard_map/pallas_call | solution.py:625
  37.8 0.0 collective-permute-done.4.from_on
  37.8 3.5 %collective-permute-done.5.from_off = bf16[1072,128]{1,0:T(8,128)(2,1)S(1)} collective-permute-done((bf16[1072,128]{1,0:T(8,128)(2,1)S(1)}, bf16[1072,128]{1,0:T(8,128)(2,1)S(1)}, u32[]{:S(2)}, u32[]{:S(2)}) %collective-permute-start.5) | collective-permute-done | bytes 274464 | tf_op jit(solution)/shard_map/ppermute | solution.py:710
  41.3 0.0 copy-done.7
  41.3 5.3 %shard_map.110 = (bf16[4,2,32,128]{3,2,1,0:T(8,128)(2,1)}, bf16[15,2,32,128]{3,2,1,0:T(8,128)(2,1)}) custom-call(s32[2,1,32]{2,1,0:T(1,128)S(1)} %bitcast.10, f32[2,38,2,16,128]{4,3,2,1,0:T(8,128)S(1)} %get-tuple-element.29.state_mid, f32[2,38,2,24,128]{4,3,2,1,0:T(8,128)S(1)} %get-tuple-element.34.state_rim, ...), custom_call_target="tpu_custom_call" | custom-call | tf_op jit(solution)/shard_map/pallas_call | solution.py:711
  (1 shorter events, 0.0 us)
Async XLA Ops:
  0.6 6.5 %copy-start = (f32[19,2,32,128]{3,2,1,0:T(8,128)S(1)}, f32[19,2,32,128]{3,2,1,0:T(8,128)}, u32[]{:S(2)}) copy-start(f32[19,2,32,128]{3,2,1,0:T(8,128)} %pop.1) | copy-start | bytes 1867780
  0.6 6.5 %copy-start.2 = (f32[6,2,32,128]{3,2,1,0:T(8,128)S(1)}, f32[6,2,32,128]{3,2,1,0:T(8,128)}, u32[]{:S(2)}) copy-start(f32[6,2,32,128]{3,2,1,0:T(8,128)} %ori.1) | copy-start | bytes 589828
  2.3 34.8 %copy-start.1 = (bf16[512,512]{1,0:T(8,128)(2,1)S(1)}, bf16[512,512]{1,0:T(8,128)(2,1)}, u32[]{:S(2)}) copy-start(bf16[512,512]{1,0:T(8,128)(2,1)} %w_mid_hbm.1) | copy-start | bytes 1572868
  2.3 34.8 %copy-start.3 = (bf16[512,15]{0,1:T(8,128)(2,1)S(1)}, bf16[512,15]{0,1:T(8,128)(2,1)}, u32[]{:S(2)}) copy-start(bf16[512,15]{0,1:T(8,128)(2,1)} %param.16) | copy-start | bytes 46084
  2.3 34.8 %copy-start.4 = (bf16[6,512]{1,0:T(8,128)(2,1)S(1)}, bf16[6,512]{1,0:T(8,128)(2,1)}, u32[]{:S(2)}) copy-start(bf16[6,512]{1,0:T(8,128)(2,1)} %w_in_hbm.1) | copy-start | bytes 18436
  2.3 34.8 %copy-start.5 = (f32[512]{0:T(512)S(1)}, f32[512]{0:T(512)}, u32[]{:S(2)}) copy-start(f32[512]{0:T(512)} %param.13) | copy-start | bytes 6148
  2.3 34.8 %copy-start.6 = (f32[512]{0:T(512)S(1)}, f32[512]{0:T(512)}, u32[]{:S(2)}) copy-start(f32[512]{0:T(512)} %param.15) | copy-start | bytes 6148
  2.3 34.8 %copy-start.8 = (f32[15]{0:T(128)S(1)}, f32[15]{0:T(128)}, u32[]{:S(2)}) copy-start(f32[15]{0:T(128)} %param.17) | copy-start | bytes 184
  2.3 38.9 %copy-start.7 = (s32[2,32,1]{1,2,0:T(1,128)S(1)}, s32[2,32,1]{1,2,0:T(1,128)}, u32[]{:S(2)}) copy-start(s32[2,32,1]{1,2,0:T(1,128)} %param.11) | copy-start | bytes 772
  2.3 5.1 %collective-permute-start = (bf16[32,128]{1,0:T(8,128)(2,1)S(1)}, bf16[32,128]{1,0:T(8,128)(2,1)S(1)}, u32[]{:S(2)}, u32[]{:S(2)}) collective-permute-start(bf16[32,128]{1,0:T(8,128)(2,1)S(1)} %get-tuple-element.24), channel_id=1, source_target_pairs={{0,1},{1,2},{2,3},{4,5},{5,6},{6,7},{8,9},{9,10},{10,11},{12,13},{... | collective-permute-start | bytes 24584 | tf_op jit(solution)/shard_map/ppermute | solution.py:667
  5.9 5.5 %collective-permute-start.1 = (bf16[32,128]{1,0:T(8,128)(2,1)S(1)}, bf16[32,128]{1,0:T(8,128)(2,1)S(1)}, u32[]{:S(2)}, u32[]{:S(2)}) collective-permute-start(bf16[32,128]{1,0:T(8,128)(2,1)S(1)} %get-tuple-element.25), channel_id=1, source_target_pairs={{1,0},{2,1},{3,2},{5,4},{6,5},{7,6},{9,8},{10,9},{11,10},{13,12},{... | collective-permute-start | bytes 24584 | tf_op jit(solution)/shard_map/ppermute | solution.py:668
  11.4 7.7 %collective-permute-start.2 = (bf16[112,128]{1,0:T(8,128)(2,1)S(1)}, bf16[112,128]{1,0:T(8,128)(2,1)S(1)}, u32[]{:S(2)}, u32[]{:S(2)}) collective-permute-start(bf16[112,128]{1,0:T(8,128)(2,1)S(1)} %get-tuple-element.32), channel_id=1, source_target_pairs={{0,4},{4,8},{8,12},{12,16},{16,20},{20,24},{24,28},{28,0},{1,5},{5... | collective-permute-start | bytes 86024 | tf_op jit(solution)/shard_map/ppermute | solution.py:686
  16.1 7.0 %collective-permute-start.3 = (bf16[112,128]{1,0:T(8,128)(2,1)S(1)}, bf16[112,128]{1,0:T(8,128)(2,1)S(1)}, u32[]{:S(2)}, u32[]{:S(2)}) collective-permute-start(bf16[112,128]{1,0:T(8,128)(2,1)S(1)} %get-tuple-element.33), channel_id=1, source_target_pairs={{0,28},{4,0},{8,4},{12,8},{16,12},{20,16},{24,20},{28,24},{1,29},{... | collective-permute-start | bytes 86024 | tf_op jit(solution)/shard_map/ppermute | solution.py:687
  24.1 13.7 %collective-permute-start.4 = (bf16[1072,128]{1,0:T(8,128)(2,1)S(1)}, bf16[1072,128]{1,0:T(8,128)(2,1)S(1)}, u32[]{:S(2)}, u32[]{:S(2)}) collective-permute-start(bf16[1072,128]{1,0:T(8,128)(2,1)S(1)} %get-tuple-element.35), channel_id=1, source_target_pairs={{0,32},{32,0},{64,96},{96,64},{128,160},{160,128},{192,224},{224,1... | collective-permute-start | bytes 823304 | tf_op jit(solution)/shard_map/ppermute | solution.py:709
  26.0 15.2 %collective-permute-start.5 = (bf16[1072,128]{1,0:T(8,128)(2,1)S(1)}, bf16[1072,128]{1,0:T(8,128)(2,1)S(1)}, u32[]{:S(2)}, u32[]{:S(2)}) collective-permute-start(bf16[1072,128]{1,0:T(8,128)(2,1)S(1)} %get-tuple-element.36), channel_id=1, source_target_pairs={{0,480},{32,64},{64,32},{96,128},{128,96},{160,192},{192,160},{224... | collective-permute-start | bytes 823304 | tf_op jit(solution)/shard_map/ppermute | solution.py:710

commit v9 on v6

--- a/solution.py
+++ b/solution.py
@@ -251,7 +251,7 @@
 PIECES = [(0, 5), (5, 10), (10, 15), (15, 19)]
 
 
-def pack_z_kernel(pop_hbm, ori_hbm, zlow, zhigh, low_rows, high_rows, pop, ori, sems):
+def pack_z_kernel(pop_hbm, ori_hbm, zlow, zhigh, pop, ori, sems):
     pairs = [(pop_hbm.at[pl.ds(a, b - a)], pop.at[pl.ds(a, b - a)]) for a, b in PIECES]
     copies = fetch(pairs + [(ori_hbm, ori)], sems)
     starts = [a for a, _ in PIECES] + [19]
@@ -269,12 +269,8 @@
             v = roll(src[k, x], at + 2, 1)
             high = jnp.where((lane >= at) & (lane < at + 2), v, high)
             low = jnp.where((lane >= at + 2) & (lane < at + 4), v, low)
-            low_rows[pl.ds(2 * s, 2), :] = src[k, x, 0:2, :]
-            high_rows[pl.ds(2 * s, 2), :] = src[k, x, 30:32, :]
     zlow[...] = low.astype(jnp.bfloat16)
     zhigh[...] = high.astype(jnp.bfloat16)
-    low_rows[100:112, :] = jnp.zeros((12, 128), jnp.float32)
-    high_rows[100:112, :] = jnp.zeros((12, 128), jnp.float32)
 
 
 def unpack_z(from_minus, from_plus, s):
@@ -282,8 +278,7 @@
     return jnp.where(lanes_of() < 64, roll(from_plus, shift, 1), roll(from_minus, shift, 1))
 
 
-def pack_y_kernel(from_minus, from_plus, low_in, high_in, token, sides, low_rows, high_rows, low, high):
-    del token
+def pack_y_kernel(from_minus, from_plus, low_in, high_in, sides, low_rows, high_rows, low, high):
     low[...] = low_in[...]
     high[...] = high_in[...]
     for t, part in enumerate((from_minus, from_plus)):
@@ -294,8 +289,17 @@
     high_rows[...] = high[...].astype(jnp.bfloat16)
 
 
-def own_kernel(pop, ori, after, own, token):
-    token[...] = jnp.zeros(token.shape, jnp.float32)
+def own_kernel(pop, ori, after, own, low_rows, high_rows):
+    del after
+    for f in range(25):
+        src = pop if f < 19 else ori
+        k = f if f < 19 else f - 19
+        for x in range(2):
+            rows = pl.ds(2 * (2 * f + x), 2)
+            low_rows[rows, :] = src[k, x, 0:2, :]
+            high_rows[rows, :] = src[k, x, 30:32, :]
+    low_rows[100:112, :] = jnp.zeros((12, 128), jnp.float32)
+    high_rows[100:112, :] = jnp.zeros((12, 128), jnp.float32)
     numbers = list(range(19))
     for x in range(2):
         for r in range(4):
@@ -454,17 +458,14 @@
 
 
 def step_two_kernel(
-    slots, state_mid, state_rim, from_low, from_high, w_one, w_mid, b_mid, w_out, b_out, flow, closure,
-    got, fields, near, level, feats, spread, place,
+    slots_hbm, state_mid, state_rim, from_low, from_high, w_one, w_mid, b_mid, w_out, b_out, flow, closure,
+    got, fields, near, level, feats, spread, place, slots, sem,
 ):
     low, high = walls()
     got[0] = from_low[...].astype(jnp.float32)
     got[1] = from_high[...].astype(jnp.float32)
-    for s in range(17):
-        place[s] = 64
-    for b in range(64):
-        s = slots[b // 32, 0, b % 32]
-        place[jnp.where(s >= 0, s, 16)] = b
+    slots_copy = pltpu.make_async_copy(slots_hbm, slots, sem)
+    slots_copy.start()
 
     def arrived(x, k, t, r):
         if t == 0 and r < 4:
@@ -545,6 +546,12 @@
                         a1 = arrived(x, 23 + k, t, r) + ORIENT_STEP * (rate[k] - drift * a0[k])
                         level[x, 3 + k, pl.ds(8 * r, 8), :] = a1
 
+    slots_copy.wait()
+    for s in range(17):
+        place[s] = 64
+    for b in range(64):
+        s = slots[b // 32, 0, b % 32]
+        place[jnp.where(s >= 0, s, 16)] = b
     feats[...] = jnp.ones(feats.shape, jnp.float32)
     for x in range(2):
         for r in range(4):
@@ -611,7 +618,6 @@
     f32, bf16 = jnp.float32, jnp.bfloat16
     shape = lambda *s, d=f32: jax.ShapeDtypeStruct(s, d)
     vmem = pl.BlockSpec(memory_space=pltpu.VMEM)
-    smem = pl.BlockSpec(memory_space=pltpu.SMEM)
     params = pltpu.CompilerParams(vmem_limit_bytes=24 * MIB)
 
     def ring(axis, step, wrap):
@@ -642,11 +648,11 @@
         ],
         compiler_params=pltpu.CompilerParams(vmem_limit_bytes=LIMIT_WEIGHTS),
     )(w_in, b_in.reshape(1, 512), w_mid, b_mid.reshape(1, 512), w_out.T, b_out.reshape(1, 15))
-    zlow, zhigh, low_raw, high_raw = pl.pallas_call(
+    zlow, zhigh = pl.pallas_call(
         pack_z_kernel,
-        out_shape=(shape(32, 128, d=bf16), shape(32, 128, d=bf16), shape(112, 128), shape(112, 128)),
+        out_shape=(shape(32, 128, d=bf16), shape(32, 128, d=bf16)),
         in_specs=[hbm] * 2,
-        out_specs=(vmem,) * 4,
+        out_specs=(vmem,) * 2,
         scratch_shapes=[
             pltpu.VMEM((19, 2, 32, 128), f32),
             pltpu.VMEM((6, 2, 32, 128), f32),
@@ -655,23 +661,23 @@
         compiler_params=pltpu.CompilerParams(vmem_limit_bytes=LIMIT_PACK),
         cost_estimate=COST_PACK,
     )(populations, orientation)
-    own, token = pl.pallas_call(
+    own, low_raw, high_raw = pl.pallas_call(
         own_kernel,
-        out_shape=(shape(28, 2, 32, 128), shape(8, 128)),
+        out_shape=(shape(28, 2, 32, 128), shape(112, 128), shape(112, 128)),
         in_specs=[vmem] * 3,
-        out_specs=(vmem,) * 2,
+        out_specs=(vmem,) * 3,
         compiler_params=params,
-    )(populations, orientation, low_raw)
+    )(populations, orientation, zlow)
     from_minus = lax.ppermute(zhigh, "gz", ring("gz", 1, False))
     from_plus = lax.ppermute(zlow, "gz", ring("gz", -1, False))
     sides, low_rows, high_rows = pl.pallas_call(
         pack_y_kernel,
         out_shape=(shape(2, 32, 128), shape(112, 128, d=bf16), shape(112, 128, d=bf16)),
-        in_specs=[vmem] * 5,
+        in_specs=[vmem] * 4,
         out_specs=(vmem,) * 3,
         scratch_shapes=[pltpu.VMEM((112, 128), f32), pltpu.VMEM((112, 128), f32)],
         compiler_params=params,
-    )(from_minus, from_plus, low_raw, high_raw, token)
+    )(from_minus, from_plus, low_raw, high_raw)
     fields_shape = shape(28, 2, 2, 64, 128)
     fields, state_mid, middle = pl.pallas_call(
         middle_kernel,
@@ -706,7 +712,7 @@
     return pl.pallas_call(
         step_two_kernel,
         out_shape=(shape(4, 2, 32, 128, d=bf16), shape(15, 2, 32, 128, d=bf16)),
-        in_specs=[smem] + [vmem] * 9,
+        in_specs=[hbm] + [vmem] * 9,
         out_specs=(vmem,) * 2,
         scratch_shapes=[
             pltpu.VMEM((2, MSG_ROWS, 128), f32),
@@ -716,6 +722,8 @@
             pltpu.VMEM((65 * 8, 128), f32),
             pltpu.VMEM((65 * 16, 128), f32),
             pltpu.SMEM((17,), jnp.int32),
+            pltpu.SMEM((2, 1, 32), jnp.int32),
+            pltpu.SemaphoreType.DMA,
         ],
         compiler_params=params,
     )(slots, state_mid, state_rim, from_low, from_high, w_one, w_two, bias_mid, w_three, bias_out)

time: 40.4 us -> 39.9 us (0.988)
  Pallas kernels: 9.58 us -> 9.09 us
    pallas_call x1, Pallas kernels: 5.16 us -> 4.66 us  [local(): pl.pallas_call(step_two_kernel, out_shape=(shape(4, 2, 32, 128, d=bf16),...]
where the time goes in v9:
time: 39.9 us; the launch traced here: 39.7 us
  starting transfers between devices  18.5 us (46%)
  waiting for transfers between devices  11.2 us (28%)
  Pallas kernels  9.09 us (23%)
  between operations  0.84 us (2%)
    ppermute x1, starting transfers between devices, local(): from_low = lax.ppermute(msg_high, 'gx', ring('gx', 1, True))  6.73 us
    pallas_call x1, Pallas kernels, local(): pl.pallas_call(step_two_kernel, out_shape=(shape(4, 2, 32, 128, d=bf16),...  4.66 us
    ppermute x1, starting transfers between devices, local(): from_yminus = lax.ppermute(high_rows, 'gy', ring('gy', 1, True))  4.41 us
    ppermute x1, waiting for transfers between devices, local(): from_high = lax.ppermute(msg_low, 'gx', ring('gx', -1, True))  3.69 us
    ppermute x1, starting transfers between devices, local(): from_minus = lax.ppermute(zhigh, 'gz', ring('gz', 1, False))  3.25 us
    ppermute x1, waiting for transfers between devices, local(): from_yplus = lax.ppermute(low_rows, 'gy', ring('gy', -1, True))  2.86 us
    ppermute x1, waiting for transfers between devices, local(): from_low = lax.ppermute(msg_high, 'gx', ring('gx', 1, True))  2.79 us
    ppermute x1, starting transfers between devices, local(): from_plus = lax.ppermute(zlow, 'gz', ring('gz', -1, False))  2.16 us
  transfers between devices with their start and end apart: 6, of which 4 were waited for; matrix products, arithmetic and copies ran while one was open for 0% of the time, Pallas kernels for 5%

profile of v9, /device:TPU:219, one launch (start us, length us, event | category | flops | bytes accessed | tf_op | source)
XLA Modules:
  0.0 39.7 jit_solution(18085004694704958845)
XLA Ops:
  0.6 0.0 copy-start
  0.6 0.0 copy-start.2
  0.6 1.6 %shard_map.104 = (bf16[32,128]{1,0:T(8,128)(2,1)S(1)}, bf16[32,128]{1,0:T(8,128)(2,1)S(1)}) custom-call(f32[19,2,32,128]{3,2,1,0:T(8,128)} %pop.1, f32[6,2,32,128]{3,2,1,0:T(8,128)} %ori.1), custom_call_target="tpu_custom_call" | custom-call | flops 10000000000 | bytes 10000000 | tf_op jit(solution)/shard_map/pallas_call | solution.py:651
  2.2 0.0 copy-start.1
  2.2 0.0 copy-start.3
  2.2 0.0 copy-start.4
  2.3 0.0 copy-start.5
  2.3 0.0 copy-start.6
  2.3 0.0 copy-start.8
  2.3 0.0 copy-start.7
  2.3 3.3 %collective-permute-start = (bf16[32,128]{1,0:T(8,128)(2,1)S(1)}, bf16[32,128]{1,0:T(8,128)(2,1)S(1)}, u32[]{:S(2)}, u32[]{:S(2)}) collective-permute-start(bf16[32,128]{1,0:T(8,128)(2,1)S(1)} %get-tuple-element.23), channel_id=1, source_target_pairs={{0,1},{1,2},{2,3},{4,5},{5,6},{6,7},{8,9},{9,10},{10,11},{12,13},{... | collective-permute-start | bytes 24584 | tf_op jit(solution)/shard_map/ppermute | solution.py:671
  5.6 2.2 %collective-permute-start.1 = (bf16[32,128]{1,0:T(8,128)(2,1)S(1)}, bf16[32,128]{1,0:T(8,128)(2,1)S(1)}, u32[]{:S(2)}, u32[]{:S(2)}) collective-permute-start(bf16[32,128]{1,0:T(8,128)(2,1)S(1)} %get-tuple-element.21.after), channel_id=1, source_target_pairs={{1,0},{2,1},{3,2},{5,4},{6,5},{7,6},{9,8},{10,9},{11,10},{13,12},{... | collective-permute-start | bytes 24584 | tf_op jit(solution)/shard_map/ppermute | solution.py:672
  7.7 0.0 copy-done
  7.7 0.0 copy-done.2
  7.7 0.3 shard_map.105
  8.1 0.0 collective-permute-done.from_minus
  8.1 1.9 %collective-permute-done.1.from_plus = bf16[32,128]{1,0:T(8,128)(2,1)S(1)} collective-permute-done((bf16[32,128]{1,0:T(8,128)(2,1)S(1)}, bf16[32,128]{1,0:T(8,128)(2,1)S(1)}, u32[]{:S(2)}, u32[]{:S(2)}) %collective-permute-start.1) | collective-permute-done | bytes 8224 | tf_op jit(solution)/shard_map/ppermute | solution.py:672
  10.0 4.4 %collective-permute-start.2 = (bf16[112,128]{1,0:T(8,128)(2,1)S(1)}, bf16[112,128]{1,0:T(8,128)(2,1)S(1)}, u32[]{:S(2)}, u32[]{:S(2)}) collective-permute-start(bf16[112,128]{1,0:T(8,128)(2,1)S(1)} %get-tuple-element.30), channel_id=1, source_target_pairs={{0,4},{4,8},{8,12},{12,16},{16,20},{20,24},{24,28},{28,0},{1,5},{5... | collective-permute-start | bytes 86024 | tf_op jit(solution)/shard_map/ppermute | solution.py:690
  14.4 1.9 %collective-permute-start.3 = (bf16[112,128]{1,0:T(8,128)(2,1)S(1)}, bf16[112,128]{1,0:T(8,128)(2,1)S(1)}, u32[]{:S(2)}, u32[]{:S(2)}) collective-permute-start(bf16[112,128]{1,0:T(8,128)(2,1)S(1)} %get-tuple-element.31), channel_id=1, source_target_pairs={{0,28},{4,0},{8,4},{12,8},{16,12},{20,16},{24,20},{28,24},{1,29},{... | collective-permute-start | bytes 86024 | tf_op jit(solution)/shard_map/ppermute | solution.py:691
  16.3 1.0 %shard_map.107 = (f32[28,2,2,64,128]{4,3,2,1,0:T(8,128)S(1)}, f32[2,38,2,16,128]{4,3,2,1,0:T(8,128)S(1)}, bf16[2,480,128]{2,1,0:T(8,128)(2,1)S(1)}) custom-call(f32[28,2,32,128]{3,2,1,0:T(8,128)S(1)} %get-tuple-element.22.own, f32[2,32,128]{2,1,0:T(8,128)S(1)} %get-tuple-element.26.sides), custom_call_target="tpu_custom_call" | custom-call | tf_op jit(solution)/shard_map/pallas_call | solution.py:682
  17.4 0.0 collective-permute-done.2.from_yminus
  17.4 2.9 %collective-permute-done.3.from_yplus = bf16[112,128]{1,0:T(8,128)(2,1)S(1)} collective-permute-done((bf16[112,128]{1,0:T(8,128)(2,1)S(1)}, bf16[112,128]{1,0:T(8,128)(2,1)S(1)}, u32[]{:S(2)}, u32[]{:S(2)}) %collective-permute-start.3) | collective-permute-done | bytes 28704 | tf_op jit(solution)/shard_map/ppermute | solution.py:691
  20.2 0.9 %shard_map.108 = (f32[28,2,2,64,128]{4,3,2,1,0:T(8,128)S(1)}, f32[2,38,2,24,128]{4,3,2,1,0:T(8,128)S(1)}, bf16[1072,128]{1,0:T(8,128)(2,1)S(1)}, bf16[1072,128]{1,0:T(8,128)(2,1)S(1)}) custom-call(f32[28,2,2,64,128]{4,3,2,1,0:T(8,128)S(1)} %get-tuple-element.28.before, ...), custom_call_target="tpu_custom_call", output_to_operand_aliasing={{0}: (0, {})} | custom-call | tf_op jit(solution)/shard_map/pallas_call | solution.py:692
  21.1 6.7 %collective-permute-start.4 = (bf16[1072,128]{1,0:T(8,128)(2,1)S(1)}, bf16[1072,128]{1,0:T(8,128)(2,1)S(1)}, u32[]{:S(2)}, u32[]{:S(2)}) collective-permute-start(bf16[1072,128]{1,0:T(8,128)(2,1)S(1)} %get-tuple-element.33), channel_id=1, source_target_pairs={{0,32},{32,64},{64,96},{96,128},{128,160},{160,192},{192,224},{224... | collective-permute-start | bytes 823304 | tf_op jit(solution)/shard_map/ppermute | solution.py:710
  27.9 0.0 collective-permute-start.5
  27.9 0.0 copy-done.1
  27.9 0.0 copy-done.3
  27.9 0.0 copy-done.4
  27.9 0.0 copy-done.5
  27.9 0.0 copy-done.6
  27.9 0.0 copy-done.8
  27.9 0.6 %shard_map.109 = (bf16[512,8]{1,0:T(8,128)(2,1)S(1)}, bf16[512,512]{1,0:T(8,128)(2,1)S(1)}, f32[512,128]{1,0:T(8,128)S(1)}, bf16[15,512]{1,0:T(8,128)(2,1)S(1)}, f32[16,128]{1,0:T(8,128)S(1)}) custom-call(bf16[6,512]{1,0:T(8,128)(2,1)S(1)} %copy-done.4, f32[1,512]{1,0:T(1,128)S(1)} %bitcast.8, bf16[512,512]{1,0:T(8,128)(2,1)S(1)} %copy-done.1, ...), custom_call_target="tpu_custom_call" | custom-call | tf_op jit(solution)/shard_map/pallas_call | solution.py:629
  28.5 2.8 %collective-permute-done.4.from_low = bf16[1072,128]{1,0:T(8,128)(2,1)S(1)} collective-permute-done((bf16[1072,128]{1,0:T(8,128)(2,1)S(1)}, bf16[1072,128]{1,0:T(8,128)(2,1)S(1)}, u32[]{:S(2)}, u32[]{:S(2)}) %collective-permute-start.4) | collective-permute-done | bytes 274464 | tf_op jit(solution)/shard_map/ppermute | solution.py:710
  31.3 3.7 %collective-permute-done.5.from_high = bf16[1072,128]{1,0:T(8,128)(2,1)S(1)} collective-permute-done((bf16[1072,128]{1,0:T(8,128)(2,1)S(1)}, bf16[1072,128]{1,0:T(8,128)(2,1)S(1)}, u32[]{:S(2)}, u32[]{:S(2)}) %collective-permute-start.5) | collective-permute-done | bytes 274464 | tf_op jit(solution)/shard_map/ppermute | solution.py:711
  35.0 0.0 copy-done.7
  35.0 4.7 %shard_map.110 = (bf16[4,2,32,128]{3,2,1,0:T(8,128)(2,1)}, bf16[15,2,32,128]{3,2,1,0:T(8,128)(2,1)}) custom-call(s32[2,1,32]{2,1,0:T(1,128)S(1)} %bitcast.10, f32[2,38,2,16,128]{4,3,2,1,0:T(8,128)S(1)} %get-tuple-element.27.state_mid, f32[2,38,2,24,128]{4,3,2,1,0:T(8,128)S(1)} %get-tuple-element.32.state_rim, ...), custom_call_target="tpu_custom_call" | custom-call | tf_op jit(solution)/shard_map/pallas_call | solution.py:712
  (1 shorter events, 0.0 us)
Async XLA Ops:
  0.6 7.1 %copy-start = (f32[19,2,32,128]{3,2,1,0:T(8,128)S(1)}, f32[19,2,32,128]{3,2,1,0:T(8,128)}, u32[]{:S(2)}) copy-start(f32[19,2,32,128]{3,2,1,0:T(8,128)} %pop.1) | copy-start | bytes 1867780
  0.6 7.1 %copy-start.2 = (f32[6,2,32,128]{3,2,1,0:T(8,128)S(1)}, f32[6,2,32,128]{3,2,1,0:T(8,128)}, u32[]{:S(2)}) copy-start(f32[6,2,32,128]{3,2,1,0:T(8,128)} %ori.1) | copy-start | bytes 589828
  2.2 25.7 %copy-start.1 = (bf16[512,512]{1,0:T(8,128)(2,1)S(1)}, bf16[512,512]{1,0:T(8,128)(2,1)}, u32[]{:S(2)}) copy-start(bf16[512,512]{1,0:T(8,128)(2,1)} %w_mid_hbm.1) | copy-start | bytes 1572868
  2.2 25.7 %copy-start.3 = (bf16[512,15]{0,1:T(8,128)(2,1)S(1)}, bf16[512,15]{0,1:T(8,128)(2,1)}, u32[]{:S(2)}) copy-start(bf16[512,15]{0,1:T(8,128)(2,1)} %param.16) | copy-start | bytes 46084
  2.2 25.6 %copy-start.4 = (bf16[6,512]{1,0:T(8,128)(2,1)S(1)}, bf16[6,512]{1,0:T(8,128)(2,1)}, u32[]{:S(2)}) copy-start(bf16[6,512]{1,0:T(8,128)(2,1)} %w_in_hbm.1) | copy-start | bytes 18436
  2.3 25.6 %copy-start.5 = (f32[512]{0:T(512)S(1)}, f32[512]{0:T(512)}, u32[]{:S(2)}) copy-start(f32[512]{0:T(512)} %param.13) | copy-start | bytes 6148
  2.3 25.6 %copy-start.6 = (f32[512]{0:T(512)S(1)}, f32[512]{0:T(512)}, u32[]{:S(2)}) copy-start(f32[512]{0:T(512)} %param.15) | copy-start | bytes 6148
  2.3 25.6 %copy-start.8 = (f32[15]{0:T(128)S(1)}, f32[15]{0:T(128)}, u32[]{:S(2)}) copy-start(f32[15]{0:T(128)} %param.17) | copy-start | bytes 184
  2.3 32.7 %copy-start.7 = (s32[2,32,1]{1,2,0:T(1,128)S(1)}, s32[2,32,1]{1,2,0:T(1,128)}, u32[]{:S(2)}) copy-start(s32[2,32,1]{1,2,0:T(1,128)} %param.11) | copy-start | bytes 772
  2.3 5.8 %collective-permute-start = (bf16[32,128]{1,0:T(8,128)(2,1)S(1)}, bf16[32,128]{1,0:T(8,128)(2,1)S(1)}, u32[]{:S(2)}, u32[]{:S(2)}) collective-permute-start(bf16[32,128]{1,0:T(8,128)(2,1)S(1)} %get-tuple-element.23), channel_id=1, source_target_pairs={{0,1},{1,2},{2,3},{4,5},{5,6},{6,7},{8,9},{9,10},{10,11},{12,13},{... | collective-permute-start | bytes 24584 | tf_op jit(solution)/shard_map/ppermute | solution.py:671
  5.6 4.4 %collective-permute-start.1 = (bf16[32,128]{1,0:T(8,128)(2,1)S(1)}, bf16[32,128]{1,0:T(8,128)(2,1)S(1)}, u32[]{:S(2)}, u32[]{:S(2)}) collective-permute-start(bf16[32,128]{1,0:T(8,128)(2,1)S(1)} %get-tuple-element.21.after), channel_id=1, source_target_pairs={{1,0},{2,1},{3,2},{5,4},{6,5},{7,6},{9,8},{10,9},{11,10},{13,12},{... | collective-permute-start | bytes 24584 | tf_op jit(solution)/shard_map/ppermute | solution.py:672
  10.0 7.4 %collective-permute-start.2 = (bf16[112,128]{1,0:T(8,128)(2,1)S(1)}, bf16[112,128]{1,0:T(8,128)(2,1)S(1)}, u32[]{:S(2)}, u32[]{:S(2)}) collective-permute-start(bf16[112,128]{1,0:T(8,128)(2,1)S(1)} %get-tuple-element.30), channel_id=1, source_target_pairs={{0,4},{4,8},{8,12},{12,16},{16,20},{20,24},{24,28},{28,0},{1,5},{5... | collective-permute-start | bytes 86024 | tf_op jit(solution)/shard_map/ppermute | solution.py:690
  14.4 5.8 %collective-permute-start.3 = (bf16[112,128]{1,0:T(8,128)(2,1)S(1)}, bf16[112,128]{1,0:T(8,128)(2,1)S(1)}, u32[]{:S(2)}, u32[]{:S(2)}) collective-permute-start(bf16[112,128]{1,0:T(8,128)(2,1)S(1)} %get-tuple-element.31), channel_id=1, source_target_pairs={{0,28},{4,0},{8,4},{12,8},{16,12},{20,16},{24,20},{28,24},{1,29},{... | collective-permute-start | bytes 86024 | tf_op jit(solution)/shard_map/ppermute | solution.py:691
  21.1 10.2 %collective-permute-start.4 = (bf16[1072,128]{1,0:T(8,128)(2,1)S(1)}, bf16[1072,128]{1,0:T(8,128)(2,1)S(1)}, u32[]{:S(2)}, u32[]{:S(2)}) collective-permute-start(bf16[1072,128]{1,0:T(8,128)(2,1)S(1)} %get-tuple-element.33), channel_id=1, source_target_pairs={{0,32},{32,64},{64,96},{96,128},{128,160},{160,192},{192,224},{224... | collective-permute-start | bytes 823304 | tf_op jit(solution)/shard_map/ppermute | solution.py:710
  27.9 7.1 %collective-permute-start.5 = (bf16[1072,128]{1,0:T(8,128)(2,1)S(1)}, bf16[1072,128]{1,0:T(8,128)(2,1)S(1)}, u32[]{:S(2)}, u32[]{:S(2)}) collective-permute-start(bf16[1072,128]{1,0:T(8,128)(2,1)S(1)} %get-tuple-element.34), channel_id=1, source_target_pairs={{0,480},{32,0},{64,32},{96,64},{128,96},{160,128},{192,160},{224,1... | collective-permute-start | bytes 823304 | tf_op jit(solution)/shard_map/ppermute | solution.py:711

commit v10 on v9

--- a/solution.py
+++ b/solution.py
@@ -458,7 +458,7 @@
 
 
 def step_two_kernel(
-    slots_hbm, state_mid, state_rim, from_low, from_high, w_one, w_mid, b_mid, w_out, b_out, flow, closure,
+    slots_hbm, state_mid, state_rim, from_high, from_low, w_one, w_mid, b_mid, w_out, b_out, flow, closure,
     got, fields, near, level, feats, spread, place, slots, sem,
 ):
     low, high = walls()
@@ -726,7 +726,7 @@
             pltpu.SemaphoreType.DMA,
         ],
         compiler_params=params,
-    )(slots, state_mid, state_rim, from_low, from_high, w_one, w_two, bias_mid, w_three, bias_out)
+    )(slots, state_mid, state_rim, from_high, from_low, w_one, w_two, bias_mid, w_three, bias_out)
 
 
 def solution(mesh):

time: 39.9 us -> 42.2 us (1.058)
  the two profiles are of different devices: /device:TPU:219 before, /device:TPU:24 now
where the time goes in v10:
time: 42.2 us; the launch traced here: 42 us
  starting transfers between devices  17.1 us (41%)
  waiting for transfers between devices  15 us (36%)
  Pallas kernels  9.09 us (22%)
  between operations  0.84 us (2%)
    ppermute x1, starting transfers between devices, local(): from_high = lax.ppermute(msg_low, 'gx', ring('gx', -1, True))  5.63 us
    ppermute x1, starting transfers between devices, local(): from_yminus = lax.ppermute(high_rows, 'gy', ring('gy', 1, True))  4.69 us
    pallas_call x1, Pallas kernels, local(): pl.pallas_call(step_two_kernel, out_shape=(shape(4, 2, 32, 128, d=bf16),...  4.66 us
    ppermute x1, waiting for transfers between devices, local(): from_yplus = lax.ppermute(low_rows, 'gy', ring('gy', -1, True))  4.01 us
    ppermute x1, waiting for transfers between devices, local(): from_plus = lax.ppermute(zlow, 'gz', ring('gz', -1, False))  3.9 us
    ppermute x1, waiting for transfers between devices, local(): from_low = lax.ppermute(msg_high, 'gx', ring('gx', 1, True))  3.7 us
    ppermute x1, starting transfers between devices, local(): from_minus = lax.ppermute(zhigh, 'gz', ring('gz', 1, False))  3.53 us
    ppermute x1, waiting for transfers between devices, local(): from_high = lax.ppermute(msg_low, 'gx', ring('gx', -1, True))  3.36 us
  transfers between devices with their start and end apart: 6, of which 4 were waited for; matrix products, arithmetic and copies ran while one was open for 0% of the time, Pallas kernels for 5%

profile of v10, /device:TPU:24, one launch (start us, length us, event | category | flops | bytes accessed | tf_op | source)
XLA Modules:
  0.0 42.0 jit_solution(3770218612152163307)
XLA Ops:
  0.6 0.0 copy-start
  0.6 0.0 copy-start.2
  0.6 1.6 %shard_map.104 = (bf16[32,128]{1,0:T(8,128)(2,1)S(1)}, bf16[32,128]{1,0:T(8,128)(2,1)S(1)}) custom-call(f32[19,2,32,128]{3,2,1,0:T(8,128)} %pop.1, f32[6,2,32,128]{3,2,1,0:T(8,128)} %ori.1), custom_call_target="tpu_custom_call" | custom-call | flops 10000000000 | bytes 10000000 | tf_op jit(solution)/shard_map/pallas_call | solution.py:651
  2.2 0.0 copy-start.1
  2.2 0.0 copy-start.3
  2.2 0.0 copy-start.4
  2.3 0.0 copy-start.5
  2.3 0.0 copy-start.6
  2.3 0.0 copy-start.8
  2.3 0.0 copy-start.7
  2.3 3.5 %collective-permute-start = (bf16[32,128]{1,0:T(8,128)(2,1)S(1)}, bf16[32,128]{1,0:T(8,128)(2,1)S(1)}, u32[]{:S(2)}, u32[]{:S(2)}) collective-permute-start(bf16[32,128]{1,0:T(8,128)(2,1)S(1)} %get-tuple-element.23), channel_id=1, source_target_pairs={{0,1},{1,2},{2,3},{4,5},{5,6},{6,7},{8,9},{9,10},{10,11},{12,13},{... | collective-permute-start | bytes 24584 | tf_op jit(solution)/shard_map/ppermute | solution.py:671
  5.8 1.3 %collective-permute-start.1 = (bf16[32,128]{1,0:T(8,128)(2,1)S(1)}, bf16[32,128]{1,0:T(8,128)(2,1)S(1)}, u32[]{:S(2)}, u32[]{:S(2)}) collective-permute-start(bf16[32,128]{1,0:T(8,128)(2,1)S(1)} %get-tuple-element.21.after), channel_id=1, source_target_pairs={{1,0},{2,1},{3,2},{5,4},{6,5},{7,6},{9,8},{10,9},{11,10},{13,12},{... | collective-permute-start | bytes 24584 | tf_op jit(solution)/shard_map/ppermute | solution.py:672
  7.1 0.0 copy-done
  7.1 0.0 copy-done.2
  7.2 0.3 shard_map.105
  7.5 0.0 collective-permute-done.from_minus
  7.5 3.9 %collective-permute-done.1.from_plus = bf16[32,128]{1,0:T(8,128)(2,1)S(1)} collective-permute-done((bf16[32,128]{1,0:T(8,128)(2,1)S(1)}, bf16[32,128]{1,0:T(8,128)(2,1)S(1)}, u32[]{:S(2)}, u32[]{:S(2)}) %collective-permute-start.1) | collective-permute-done | bytes 8224 | tf_op jit(solution)/shard_map/ppermute | solution.py:672
  11.4 4.7 %collective-permute-start.2 = (bf16[112,128]{1,0:T(8,128)(2,1)S(1)}, bf16[112,128]{1,0:T(8,128)(2,1)S(1)}, u32[]{:S(2)}, u32[]{:S(2)}) collective-permute-start(bf16[112,128]{1,0:T(8,128)(2,1)S(1)} %get-tuple-element.30), channel_id=1, source_target_pairs={{0,4},{4,8},{8,12},{12,16},{16,20},{20,24},{24,28},{28,0},{1,5},{5... | collective-permute-start | bytes 86024 | tf_op jit(solution)/shard_map/ppermute | solution.py:690
  16.1 1.9 %collective-permute-start.3 = (bf16[112,128]{1,0:T(8,128)(2,1)S(1)}, bf16[112,128]{1,0:T(8,128)(2,1)S(1)}, u32[]{:S(2)}, u32[]{:S(2)}) collective-permute-start(bf16[112,128]{1,0:T(8,128)(2,1)S(1)} %get-tuple-element.31), channel_id=1, source_target_pairs={{0,28},{4,0},{8,4},{12,8},{16,12},{20,16},{24,20},{28,24},{1,29},{... | collective-permute-start | bytes 86024 | tf_op jit(solution)/shard_map/ppermute | solution.py:691
  18.0 1.0 %shard_map.107 = (f32[28,2,2,64,128]{4,3,2,1,0:T(8,128)S(1)}, f32[2,38,2,16,128]{4,3,2,1,0:T(8,128)S(1)}, bf16[2,480,128]{2,1,0:T(8,128)(2,1)S(1)}) custom-call(f32[28,2,32,128]{3,2,1,0:T(8,128)S(1)} %get-tuple-element.22.own, f32[2,32,128]{2,1,0:T(8,128)S(1)} %get-tuple-element.26.sides), custom_call_target="tpu_custom_call" | custom-call | tf_op jit(solution)/shard_map/pallas_call | solution.py:682
  19.1 0.0 collective-permute-done.2.from_yminus
  19.1 4.0 %collective-permute-done.3.from_yplus = bf16[112,128]{1,0:T(8,128)(2,1)S(1)} collective-permute-done((bf16[112,128]{1,0:T(8,128)(2,1)S(1)}, bf16[112,128]{1,0:T(8,128)(2,1)S(1)}, u32[]{:S(2)}, u32[]{:S(2)}) %collective-permute-start.3) | collective-permute-done | bytes 28704 | tf_op jit(solution)/shard_map/ppermute | solution.py:691
  23.1 0.9 %shard_map.108 = (f32[28,2,2,64,128]{4,3,2,1,0:T(8,128)S(1)}, f32[2,38,2,24,128]{4,3,2,1,0:T(8,128)S(1)}, bf16[1072,128]{1,0:T(8,128)(2,1)S(1)}, bf16[1072,128]{1,0:T(8,128)(2,1)S(1)}) custom-call(f32[28,2,2,64,128]{4,3,2,1,0:T(8,128)S(1)} %get-tuple-element.28.before, ...), custom_call_target="tpu_custom_call", output_to_operand_aliasing={{0}: (0, {})} | custom-call | tf_op jit(solution)/shard_map/pallas_call | solution.py:692
  24.0 5.6 %collective-permute-start.4 = (bf16[1072,128]{1,0:T(8,128)(2,1)S(1)}, bf16[1072,128]{1,0:T(8,128)(2,1)S(1)}, u32[]{:S(2)}, u32[]{:S(2)}) collective-permute-start(bf16[1072,128]{1,0:T(8,128)(2,1)S(1)} %get-tuple-element.33), channel_id=1, source_target_pairs={{0,480},{32,0},{64,32},{96,64},{128,96},{160,128},{192,160},{224,1... | collective-permute-start | bytes 823304 | tf_op jit(solution)/shard_map/ppermute | solution.py:711
  29.6 0.0 collective-permute-start.5
  29.6 0.0 copy-done.1
  29.6 0.0 copy-done.3
  29.6 0.0 copy-done.4
  29.6 0.0 copy-done.5
  29.7 0.0 copy-done.6
  29.7 0.0 copy-done.8
  29.7 0.6 %shard_map.109 = (bf16[512,8]{1,0:T(8,128)(2,1)S(1)}, bf16[512,512]{1,0:T(8,128)(2,1)S(1)}, f32[512,128]{1,0:T(8,128)S(1)}, bf16[15,512]{1,0:T(8,128)(2,1)S(1)}, f32[16,128]{1,0:T(8,128)S(1)}) custom-call(bf16[6,512]{1,0:T(8,128)(2,1)S(1)} %copy-done.4, f32[1,512]{1,0:T(1,128)S(1)} %bitcast.8, bf16[512,512]{1,0:T(8,128)(2,1)S(1)} %copy-done.1, ...), custom_call_target="tpu_custom_call" | custom-call | tf_op jit(solution)/shard_map/pallas_call | solution.py:629
  30.3 3.4 %collective-permute-done.4.from_high = bf16[1072,128]{1,0:T(8,128)(2,1)S(1)} collective-permute-done((bf16[1072,128]{1,0:T(8,128)(2,1)S(1)}, bf16[1072,128]{1,0:T(8,128)(2,1)S(1)}, u32[]{:S(2)}, u32[]{:S(2)}) %collective-permute-start.4) | collective-permute-done | bytes 274464 | tf_op jit(solution)/shard_map/ppermute | solution.py:711
  33.6 3.7 %collective-permute-done.5.from_low = bf16[1072,128]{1,0:T(8,128)(2,1)S(1)} collective-permute-done((bf16[1072,128]{1,0:T(8,128)(2,1)S(1)}, bf16[1072,128]{1,0:T(8,128)(2,1)S(1)}, u32[]{:S(2)}, u32[]{:S(2)}) %collective-permute-start.5) | collective-permute-done | bytes 274464 | tf_op jit(solution)/shard_map/ppermute | solution.py:710
  37.3 0.0 copy-done.7
  37.4 4.7 %shard_map.110 = (bf16[4,2,32,128]{3,2,1,0:T(8,128)(2,1)}, bf16[15,2,32,128]{3,2,1,0:T(8,128)(2,1)}) custom-call(s32[2,1,32]{2,1,0:T(1,128)S(1)} %bitcast.10, f32[2,38,2,16,128]{4,3,2,1,0:T(8,128)S(1)} %get-tuple-element.27.state_mid, f32[2,38,2,24,128]{4,3,2,1,0:T(8,128)S(1)} %get-tuple-element.32.state_rim, ...), custom_call_target="tpu_custom_call" | custom-call | tf_op jit(solution)/shard_map/pallas_call | solution.py:712
  (1 shorter events, 0.0 us)
Async XLA Ops:
  0.6 6.5 %copy-start = (f32[19,2,32,128]{3,2,1,0:T(8,128)S(1)}, f32[19,2,32,128]{3,2,1,0:T(8,128)}, u32[]{:S(2)}) copy-start(f32[19,2,32,128]{3,2,1,0:T(8,128)} %pop.1) | copy-start | bytes 1867780
  0.6 6.5 %copy-start.2 = (f32[6,2,32,128]{3,2,1,0:T(8,128)S(1)}, f32[6,2,32,128]{3,2,1,0:T(8,128)}, u32[]{:S(2)}) copy-start(f32[6,2,32,128]{3,2,1,0:T(8,128)} %ori.1) | copy-start | bytes 589828
  2.2 27.4 %copy-start.1 = (bf16[512,512]{1,0:T(8,128)(2,1)S(1)}, bf16[512,512]{1,0:T(8,128)(2,1)}, u32[]{:S(2)}) copy-start(bf16[512,512]{1,0:T(8,128)(2,1)} %w_mid_hbm.1) | copy-start | bytes 1572868
  2.2 27.4 %copy-start.3 = (bf16[512,15]{0,1:T(8,128)(2,1)S(1)}, bf16[512,15]{0,1:T(8,128)(2,1)}, u32[]{:S(2)}) copy-start(bf16[512,15]{0,1:T(8,128)(2,1)} %param.16) | copy-start | bytes 46084
  2.2 27.4 %copy-start.4 = (bf16[6,512]{1,0:T(8,128)(2,1)S(1)}, bf16[6,512]{1,0:T(8,128)(2,1)}, u32[]{:S(2)}) copy-start(bf16[6,512]{1,0:T(8,128)(2,1)} %w_in_hbm.1) | copy-start | bytes 18436
  2.3 27.4 %copy-start.5 = (f32[512]{0:T(512)S(1)}, f32[512]{0:T(512)}, u32[]{:S(2)}) copy-start(f32[512]{0:T(512)} %param.13) | copy-start | bytes 6148
  2.3 27.4 %copy-start.6 = (f32[512]{0:T(512)S(1)}, f32[512]{0:T(512)}, u32[]{:S(2)}) copy-start(f32[512]{0:T(512)} %param.15) | copy-start | bytes 6148
  2.3 27.4 %copy-start.8 = (f32[15]{0:T(128)S(1)}, f32[15]{0:T(128)}, u32[]{:S(2)}) copy-start(f32[15]{0:T(128)} %param.17) | copy-start | bytes 184
  2.3 35.1 %copy-start.7 = (s32[2,32,1]{1,2,0:T(1,128)S(1)}, s32[2,32,1]{1,2,0:T(1,128)}, u32[]{:S(2)}) copy-start(s32[2,32,1]{1,2,0:T(1,128)} %param.11) | copy-start | bytes 772
  2.3 5.2 %collective-permute-start = (bf16[32,128]{1,0:T(8,128)(2,1)S(1)}, bf16[32,128]{1,0:T(8,128)(2,1)S(1)}, u32[]{:S(2)}, u32[]{:S(2)}) collective-permute-start(bf16[32,128]{1,0:T(8,128)(2,1)S(1)} %get-tuple-element.23), channel_id=1, source_target_pairs={{0,1},{1,2},{2,3},{4,5},{5,6},{6,7},{8,9},{9,10},{10,11},{12,13},{... | collective-permute-start | bytes 24584 | tf_op jit(solution)/shard_map/ppermute | solution.py:671
  5.8 5.5 %collective-permute-start.1 = (bf16[32,128]{1,0:T(8,128)(2,1)S(1)}, bf16[32,128]{1,0:T(8,128)(2,1)S(1)}, u32[]{:S(2)}, u32[]{:S(2)}) collective-permute-start(bf16[32,128]{1,0:T(8,128)(2,1)S(1)} %get-tuple-element.21.after), channel_id=1, source_target_pairs={{1,0},{2,1},{3,2},{5,4},{6,5},{7,6},{9,8},{10,9},{11,10},{13,12},{... | collective-permute-start | bytes 24584 | tf_op jit(solution)/shard_map/ppermute | solution.py:672
  11.4 7.7 %collective-permute-start.2 = (bf16[112,128]{1,0:T(8,128)(2,1)S(1)}, bf16[112,128]{1,0:T(8,128)(2,1)S(1)}, u32[]{:S(2)}, u32[]{:S(2)}) collective-permute-start(bf16[112,128]{1,0:T(8,128)(2,1)S(1)} %get-tuple-element.30), channel_id=1, source_target_pairs={{0,4},{4,8},{8,12},{12,16},{16,20},{20,24},{24,28},{28,0},{1,5},{5... | collective-permute-start | bytes 86024 | tf_op jit(solution)/shard_map/ppermute | solution.py:690
  16.1 7.0 %collective-permute-start.3 = (bf16[112,128]{1,0:T(8,128)(2,1)S(1)}, bf16[112,128]{1,0:T(8,128)(2,1)S(1)}, u32[]{:S(2)}, u32[]{:S(2)}) collective-permute-start(bf16[112,128]{1,0:T(8,128)(2,1)S(1)} %get-tuple-element.31), channel_id=1, source_target_pairs={{0,28},{4,0},{8,4},{12,8},{16,12},{20,16},{24,20},{28,24},{1,29},{... | collective-permute-start | bytes 86024 | tf_op jit(solution)/shard_map/ppermute | solution.py:691
  24.0 9.7 %collective-permute-start.4 = (bf16[1072,128]{1,0:T(8,128)(2,1)S(1)}, bf16[1072,128]{1,0:T(8,128)(2,1)S(1)}, u32[]{:S(2)}, u32[]{:S(2)}) collective-permute-start(bf16[1072,128]{1,0:T(8,128)(2,1)S(1)} %get-tuple-element.33), channel_id=1, source_target_pairs={{0,480},{32,0},{64,32},{96,64},{128,96},{160,128},{192,160},{224,1... | collective-permute-start | bytes 823304 | tf_op jit(solution)/shard_map/ppermute | solution.py:711
  29.6 7.7 %collective-permute-start.5 = (bf16[1072,128]{1,0:T(8,128)(2,1)S(1)}, bf16[1072,128]{1,0:T(8,128)(2,1)S(1)}, u32[]{:S(2)}, u32[]{:S(2)}) collective-permute-start(bf16[1072,128]{1,0:T(8,128)(2,1)S(1)} %get-tuple-element.34), channel_id=1, source_target_pairs={{0,32},{32,64},{64,96},{96,128},{128,160},{160,192},{192,224},{224... | collective-permute-start | bytes 823304 | tf_op jit(solution)/shard_map/ppermute | solution.py:710
